TPU v7x, 256 devices: a whole 4x4x8 slice. The times are simulated.
256 devices in a mesh: ctx: 128 (over x, z, y_hi, core), ch: 2 (over y_lo).
Axes of the slice: x: 4, y: 4 (y_hi: 2, y_lo: 2; y = y_hi * 2 + y_lo), z: 8, core: 2. Of those that a mesh axis runs over, the one named last changes fastest.
Arguments:
- queries: bfloat16 [32768, 4096], P('ctx', 'ch'), may hold values from -6 to 6
- keys: bfloat16 [32768, 4096], P('ctx', 'ch'), may hold values from -6 to 6
- values: bfloat16 [32768, 4096], P('ctx', 'ch'), may hold values from -6 to 6
- grad_out: bfloat16 [32768, 4096], P('ctx', 'ch'), may hold values from -0.0009765625 to 0.0009765625
Outputs:
- filter_grad: float32 [4, 1024], P('ch')
All inputs are finite; a program needn't handle non-finite values.
Results may differ from a plain program's by a relative error of at most 0.004.
Values may be sent and summed in bfloat16 or wider, within the bound.
No kernel may reach another device: no remote copies, remote signals or barrier semaphores. Data moves between devices by JAX's collectives and lax.ppermute only.
A program may use at most 64 MiB of HBM per device.

v0:
```python
import jax
import jax.numpy as jnp
from jax import lax
from jax.sharding import PartitionSpec as P

GROUP_CH = 1024
HOPS = 4


def from_behind(shard, axis, by):
    peers = lax.axis_size(axis)
    pairs = [(i, i + by) for i in range(peers) if 0 <= i + by < peers]
    return lax.ppermute(shard, axis, pairs)


def lag_sums(product):
    count = product.shape[0]
    tok_rows = product.shape[1]
    padded = jnp.pad(product, ((0, 0), (0, 0), (0, tok_rows)))
    flat = padded.reshape(count, tok_rows * 2 * tok_rows)[:, : tok_rows * (2 * tok_rows - 1)]
    return jnp.sum(flat.reshape(count, tok_rows, 2 * tok_rows - 1), axis=1)


def on_device(queries, keys, values, grad_out):
    mixed = (keys.astype(jnp.float32) * values.astype(jnp.float32)).astype(jnp.bfloat16)
    weighted = (queries.astype(jnp.float32) * grad_out.astype(jnp.float32)).astype(jnp.bfloat16)
    tok_rows = mixed.shape[0]
    groups_here = mixed.shape[1] // GROUP_CH
    blocks = [mixed]
    for offset in range(HOPS):
        blocks.append(from_behind(blocks[-1], "ctx", 1))
    target_rows = weighted.reshape(tok_rows, groups_here, GROUP_CH)
    totals = jnp.zeros((groups_here, (HOPS + 2) * tok_rows), jnp.float32)
    for distance in range(HOPS + 1):
        flipped = blocks[distance][::-1].reshape(tok_rows, groups_here, GROUP_CH)
        product = jnp.einsum(
            "tgc,sgc->gts", target_rows, flipped, preferred_element_type=jnp.float32
        )
        summed = lag_sums(product)
        begin = distance * tok_rows + 1
        totals = totals.at[:, begin : begin + 2 * tok_rows - 1].add(summed)
    partial_value = totals[:, tok_rows : tok_rows + HOPS * tok_rows]
    return lax.psum(partial_value, "ctx")


def solution(mesh):
    in_specs = (P("ctx", "ch"), P("ctx", "ch"), P("ctx", "ch"), P("ctx", "ch"))
    out_specs = P("ch", None)
    return jax.shard_map(
        on_device, mesh=mesh, in_specs=in_specs, out_specs=out_specs, check_vma=False
    )
```

profile of v0, /device:TPU:1, one launch (start us, length us, event | category | flops | bytes accessed | tf_op | source)
XLA Modules:
  0.0 446.7 jit_solution(9498662420436601433)
XLA Ops:
  0.0 1.9 multiply_convert_fusion
  2.0 6.3 %collective-permute-start = (bf16[256,2048]{1,0:T(8,128)(2,1)S(1)}, bf16[256,2048]{1,0:T(8,128)(2,1)}, u32[]{:S(2)}, u32[]{:S(2)}) collective-permute-start(bf16[256,2048]{1,0:T(8,128)(2,1)S(1)} %multiply_convert_fusion), channel_id=1, source_target_pairs={{0,2},{2,4},{4,6},{6,8},{8,10},{10,12},{12,14},{14,16},{16,18},{18... | collective-permute-start | bytes 3145736 | tf_op jit(solution)/shard_map/ppermute | solution.py:13
  8.3 11.7 %collective-permute-done = bf16[256,2048]{1,0:T(8,128)(2,1)} collective-permute-done((bf16[256,2048]{1,0:T(8,128)(2,1)S(1)}, bf16[256,2048]{1,0:T(8,128)(2,1)}, u32[]{:S(2)}, u32[]{:S(2)}) %collective-permute-start) | collective-permute-done | bytes 1048608 | tf_op jit(solution)/shard_map/ppermute | solution.py:13
  20.0 6.0 %collective-permute-start.1 = (bf16[256,2048]{1,0:T(8,128)(2,1)}, bf16[256,2048]{1,0:T(8,128)(2,1)}, u32[]{:S(2)}, u32[]{:S(2)}) collective-permute-start(bf16[256,2048]{1,0:T(8,128)(2,1)} %collective-permute-done), channel_id=1, source_target_pairs={{0,2},{2,4},{4,6},{6,8},{8,10},{10,12},{12,14},{14,16},{16,18},{18... | collective-permute-start | bytes 3145736 | tf_op jit(solution)/shard_map/ppermute | solution.py:13
  26.0 10.3 %rev.15 = bf16[256,2048]{1,0:T(8,128)(2,1)} reverse(bf16[256,2048]{1,0:T(8,128)(2,1)S(1)} %multiply_convert_fusion), dimensions={0} | reverse | bytes 2097152 | tf_op jit(solution)/shard_map/rev | solution.py:35
  36.3 0.4 multiply_convert_fusion.1
  36.7 1.3 collective-permute-done.1
  38.1 5.9 %collective-permute-start.2 = (bf16[256,2048]{1,0:T(8,128)(2,1)}, bf16[256,2048]{1,0:T(8,128)(2,1)}, u32[]{:S(2)}, u32[]{:S(2)}) collective-permute-start(bf16[256,2048]{1,0:T(8,128)(2,1)} %collective-permute-done.1), channel_id=1, source_target_pairs={{0,2},{2,4},{4,6},{6,8},{8,10},{10,12},{12,14},{14,16},{16,18},{18... | collective-permute-start | bytes 3145736 | tf_op jit(solution)/shard_map/ppermute | solution.py:13
  44.0 0.5 fusion.12
  44.5 0.1 pad_bitcast_fusion.4
  44.6 0.8 copy.31
  45.5 1.2 reshape.169
  46.7 0.1 reduce_sum.45
  46.8 0.6 compare_reduce_fusion.3
  47.4 0.6 broadcast_select_fusion
  48.2 0.6 compare_reduce_fusion.2
  48.8 0.6 compare_reduce_fusion.1
  49.5 0.7 compare_reduce_fusion
  50.1 12.7 %rev.16 = bf16[256,2048]{1,0:T(8,128)(2,1)S(1)} reverse(bf16[256,2048]{1,0:T(8,128)(2,1)} %collective-permute-done), dimensions={0} | reverse | bytes 2097152 | tf_op jit(solution)/shard_map/rev | solution.py:35
  62.9 0.5 fusion.9
  63.3 0.1 pad_bitcast_fusion.3
  63.5 0.8 copy.32
  64.4 1.2 reshape.172
  65.6 0.1 reduce_sum.46
  65.7 0.7 add_select_fusion.2
  66.3 0.4 scatter-add.19
  66.7 12.6 %rev.17 = bf16[256,2048]{1,0:T(8,128)(2,1)S(1)} reverse(bf16[256,2048]{1,0:T(8,128)(2,1)} %collective-permute-done.1), dimensions={0} | reverse | bytes 2097152 | tf_op jit(solution)/shard_map/rev | solution.py:35
  79.4 2.1 collective-permute-start.3
  81.5 0.5 fusion.6
  82.0 0.1 pad_bitcast_fusion.2
  82.1 0.8 copy.33
  83.0 1.2 reshape.175
  84.3 0.7 add_select_fusion.1
  85.0 0.3 scatter-add.20
  85.3 12.6 %rev.18 = bf16[256,2048]{1,0:T(8,128)(2,1)S(1)} reverse(bf16[256,2048]{1,0:T(8,128)(2,1)} %collective-permute-done.2), dimensions={0} | reverse | bytes 2097152 | tf_op jit(solution)/shard_map/rev | solution.py:35
  98.0 0.5 fusion.3
  98.4 0.1 pad_bitcast_fusion.1
  98.6 0.8 copy.34
  99.5 1.2 reshape.178
  100.8 0.7 add_select_fusion
  101.5 0.3 scatter-add.21
  101.8 12.6 %rev.19 = bf16[256,2048]{1,0:T(8,128)(2,1)S(1)} reverse(bf16[256,2048]{1,0:T(8,128)(2,1)} %collective-permute-done.3), dimensions={0} | reverse | bytes 2097152 | tf_op jit(solution)/shard_map/rev | solution.py:35
  114.4 0.5 fusion
  114.9 0.1 pad_bitcast_fusion
  115.0 0.8 copy.35
  115.9 1.2 reshape.181
  117.3 0.3 scatter-add.24
  117.6 329.0 %psum.7 = f32[2,1024]{1,0:T(2,128)} all-reduce(f32[2,1024]{1,0:T(2,128)S(1)} %slice.128), channel_id=1, replica_groups=mesh['ctx'=128,'ch'=2] {'ctx'}, use_global_device_ids=true, to_apply=%region_9.10 | all-reduce | flops 2048 | bytes 16384 | tf_op jit(solution)/shard_map/psum | solution.py:43
  (23 shorter events, 0.8 us)
Async XLA Ops:
  1.9 34.4 %copy-start = (bf16[256,2048]{1,0:T(8,128)(2,1)S(1)}, bf16[256,2048]{1,0:T(8,128)(2,1)}, u32[]{:S(2)}) copy-start(bf16[256,2048]{1,0:T(8,128)(2,1)} %param.17) | copy-start | bytes 3145732
  1.9 34.4 %copy-start.1 = (bf16[256,2048]{1,0:T(8,128)(2,1)S(1)}, bf16[256,2048]{1,0:T(8,128)(2,1)}, u32[]{:S(2)}) copy-start(bf16[256,2048]{1,0:T(8,128)(2,1)} %param.14) | copy-start | bytes 3145732
  2.0 18.1 %collective-permute-start = (bf16[256,2048]{1,0:T(8,128)(2,1)S(1)}, bf16[256,2048]{1,0:T(8,128)(2,1)}, u32[]{:S(2)}, u32[]{:S(2)}) collective-permute-start(bf16[256,2048]{1,0:T(8,128)(2,1)S(1)} %multiply_convert_fusion), channel_id=1, source_target_pairs={{0,2},{2,4},{4,6},{6,8},{8,10},{10,12},{12,14},{14,16},{16,18},{18... | collective-permute-start | bytes 3145736 | tf_op jit(solution)/shard_map/ppermute | solution.py:13
  20.0 18.0 %collective-permute-start.1 = (bf16[256,2048]{1,0:T(8,128)(2,1)}, bf16[256,2048]{1,0:T(8,128)(2,1)}, u32[]{:S(2)}, u32[]{:S(2)}) collective-permute-start(bf16[256,2048]{1,0:T(8,128)(2,1)} %collective-permute-done), channel_id=1, source_target_pairs={{0,2},{2,4},{4,6},{6,8},{8,10},{10,12},{12,14},{14,16},{16,18},{18... | collective-permute-start | bytes 3145736 | tf_op jit(solution)/shard_map/ppermute | solution.py:13
  36.3 7.6 %copy-start.4 = (bf16[256,2048]{1,0:T(8,128)(2,1)S(1)}, bf16[256,2048]{1,0:T(8,128)(2,1)}, u32[]{:S(2)}) copy-start(bf16[256,2048]{1,0:T(8,128)(2,1)} %rev.15) | copy-start | bytes 3145732
  36.7 7.2 %copy-start.2 = (bf16[256,2048]{1,0:T(8,128)(2,1)}, bf16[256,2048]{1,0:T(8,128)(2,1)S(1)}, u32[]{:S(2)}) copy-start(bf16[256,2048]{1,0:T(8,128)(2,1)S(1)} %multiply_convert_fusion.1) | copy-start | bytes 3145732
  38.1 41.3 %collective-permute-start.2 = (bf16[256,2048]{1,0:T(8,128)(2,1)}, bf16[256,2048]{1,0:T(8,128)(2,1)}, u32[]{:S(2)}, u32[]{:S(2)}) collective-permute-start(bf16[256,2048]{1,0:T(8,128)(2,1)} %collective-permute-done.1), channel_id=1, source_target_pairs={{0,2},{2,4},{4,6},{6,8},{8,10},{10,12},{12,14},{14,16},{16,18},{18... | collective-permute-start | bytes 3145736 | tf_op jit(solution)/shard_map/ppermute | solution.py:13
  50.1 12.7 %copy-start.3 = (bf16[256,2048]{1,0:T(8,128)(2,1)S(1)}, bf16[256,2048]{1,0:T(8,128)(2,1)}, u32[]{:S(2)}) copy-start(bf16[256,2048]{1,0:T(8,128)(2,1)} %copy-done.2) | copy-start | bytes 3145732
  79.4 22.4 %collective-permute-start.3 = (bf16[256,2048]{1,0:T(8,128)(2,1)}, bf16[256,2048]{1,0:T(8,128)(2,1)}, u32[]{:S(2)}, u32[]{:S(2)}) collective-permute-start(bf16[256,2048]{1,0:T(8,128)(2,1)} %collective-permute-done.2), channel_id=1, source_target_pairs={{0,2},{2,4},{4,6},{6,8},{8,10},{10,12},{12,14},{14,16},{16,18},{18... | collective-permute-start | bytes 3145736 | tf_op jit(solution)/shard_map/ppermute | solution.py:13
where the time goes:
time: 451 us; the launch traced here: 447 us
  blocking collectives  329 us (73%)
  local copies, waits for them, and re-layouts  73.4 us (16%)
  starting transfers between devices  20.3 us (5%)
  waiting for transfers between devices  13.1 us (3%)
  other arithmetic  8.06 us (2%)
    psum x1, blocking collectives, on_device(): return lax.psum(partial_value, 'ctx')  329 us
    rev x5, local copies, waits for them, and re-layouts, on_device(): flipped = blocks[distance][::-1].reshape(tok_rows, groups_here, GROUP_CH)  60.8 us
    ppermute x4, starting transfers between devices, from_behind(): return lax.ppermute(shard, axis, pairs)  20.3 us
    ppermute x4, waiting for transfers between devices, from_behind(): return lax.ppermute(shard, axis, pairs)  13.1 us
  transfers between devices with their start and end apart: 4, of which 2 were waited for; matrix products, arithmetic and copies ran while one was open for 15% of the time, Pallas kernels for 0%

commit v1 on v0

v1 whole, which is shorter than its diff:
```python
import jax
import jax.numpy as jnp
from jax import lax
from jax.experimental import pallas as pl
from jax.experimental.pallas import tpu as pltpu
from jax.sharding import PartitionSpec as P

BLK = 256
CH = 512
HALF = 256
LAGS = 1024
MIB = 1024 * 1024
NT = (((1,), (1,)), ((), ()))


def products(q, k, v, g):
    weighted = (q.astype(jnp.float32) * g.astype(jnp.float32)).astype(jnp.bfloat16)
    mixed = (k.astype(jnp.float32) * v.astype(jnp.float32)).astype(jnp.bfloat16)
    return weighted, mixed


def deal_kernel(me, q, k, v, g, near1, near2, far1, far2, flip, own):
    step = pl.program_id(0)
    weighted, mixed = products(q[...], k[...], v[...], g[...])

    def split(first, second):
        first[0] = mixed[:, :HALF]
        first[1] = weighted[:, HALF:]
        second[0] = mixed[:, HALF:]
        second[1] = weighted[:, :HALF]

    def whole(out):
        out[0] = weighted
        out[1] = mixed

    pl.when(step == 0)(lambda: split(near1, near2))
    pl.when(step == 1)(lambda: split(far1, far2))
    pl.when(step == 2)(lambda: whole(flip))
    pl.when(step == 3)(lambda: whole(own))


def deal(me, queries, keys, values, grad_out):
    def block(step, me):
        other_y = 1 - step // 2
        other_core = step % 2 - (step // 2) * (2 * (step % 2) - 1)
        return 0, (me[1] ^ other_core) * 2 + (me[0] ^ other_y)

    piece = pl.BlockSpec((BLK, CH), block)
    half = pl.BlockSpec((2, BLK, HALF), lambda step, me: (0, 0, 0))
    full = pl.BlockSpec((2, BLK, CH), lambda step, me: (0, 0, 0))
    half_t = jax.ShapeDtypeStruct((2, BLK, HALF), jnp.bfloat16)
    full_t = jax.ShapeDtypeStruct((2, BLK, CH), jnp.bfloat16)
    return pl.pallas_call(
        deal_kernel,
        grid_spec=pltpu.PrefetchScalarGridSpec(
            num_scalar_prefetch=1,
            grid=(4,),
            in_specs=[piece] * 4,
            out_specs=[half] * 4 + [full] * 2,
        ),
        out_shape=[half_t] * 4 + [full_t] * 2,
        compiler_params=pltpu.CompilerParams(vmem_limit_bytes=24 * MIB),
        name="deal",
    )(me, queries, keys, values, grad_out)


def lag_sums(table):
    wide = 5 * BLK
    rows = BLK
    while rows > 1:
        half = rows // 2
        low, high = table[:half], table[half:rows]
        if half % 128 == 0:
            wide = wide - half
            table = low[:, :wide] + high[:, half : half + wide]
        else:
            table = low + pltpu.roll(high, wide - half, 1)
        rows = half
    return table


def correlate_kernel(
    me, own, flip, near1, near2, far1, far2, mix_e, mix_l, wei_e, wei_l, out,
    mix_a, wei_a, mix_b, wei_b, table, sems,
):
    here = 2 * me[0]
    there = 2 - here
    spots = (here + me[1], here + 1 - me[1], there + me[1], there + 1 - me[1])
    copies = []

    def bring(src, dst, spot):
        at = pl.ds(pl.multiple_of(spot * BLK, BLK), HALF)
        copy = pltpu.make_async_copy(src, dst.at[:, at], sems.at[len(copies)])
        copy.start()
        copies.append(copy)

    for ref, spot in ((own, spots[0]), (flip, spots[1])):
        bring(ref.at[0, :, pl.ds(0, HALF)], wei_a, spot)
        bring(ref.at[0, :, pl.ds(HALF, HALF)], wei_b, spot)
        bring(ref.at[1, :, pl.ds(0, HALF)], mix_a, 4 + spot)
        bring(ref.at[1, :, pl.ds(HALF, HALF)], mix_b, spot)
    for first, second, spot in ((near1, near2, spots[2]), (far1, far2, spots[3])):
        bring(first.at[0], mix_a, 4 + spot)
        bring(first.at[1], wei_b, spot)
        bring(second.at[0], mix_b, spot)
        bring(second.at[1], wei_a, spot)
    for part, (mix, wei) in enumerate(((mix_e, wei_e), (mix_l, wei_l))):
        for i in range(2):
            bring(mix.at[i], mix_a, spots[2 * part + i])
            bring(wei.at[i], wei_b, 4 + spots[2 * part + i])
    for copy in copies:
        copy.wait()
    for d in range(5):
        one = lax.dot_general(
            mix_a[:, pl.ds((4 - d) * BLK, 4 * BLK)], wei_a[...], NT,
            preferred_element_type=jnp.float32,
        )
        two = lax.dot_general(
            mix_b[...], wei_b[:, pl.ds(d * BLK, 4 * BLK)], NT,
            preferred_element_type=jnp.float32,
        )
        table[:, pl.ds(d * BLK, BLK)] = one + two
    sums = lag_sums(table[...])
    for i in range(8):
        out[i : i + 1, :] = sums[:, i * 128 : (i + 1) * 128]


def correlate(me, *arrays):
    anywhere = pl.BlockSpec(memory_space=pl.ANY)
    return pl.pallas_call(
        correlate_kernel,
        in_specs=[pl.BlockSpec(memory_space=pltpu.SMEM)] + [anywhere] * len(arrays),
        out_specs=pl.BlockSpec(memory_space=pltpu.VMEM),
        out_shape=jax.ShapeDtypeStruct((8, 128), jnp.float32),
        scratch_shapes=[
            pltpu.VMEM((BLK, 8 * BLK), jnp.bfloat16),
            pltpu.VMEM((BLK, 4 * BLK), jnp.bfloat16),
            pltpu.VMEM((BLK, 4 * BLK), jnp.bfloat16),
            pltpu.VMEM((BLK, 8 * BLK), jnp.bfloat16),
            pltpu.VMEM((BLK, 5 * BLK), jnp.float32),
            pltpu.SemaphoreType.DMA((24,)),
        ],
        compiler_params=pltpu.CompilerParams(vmem_limit_bytes=24 * MIB),
        name="correlate",
    )(me, *arrays)


def swap(value, quads, far, flip):
    pairs = [
        ((q * 2 + y) * 2 + c, (q * 2 + (y ^ far)) * 2 + (c ^ flip))
        for q in range(quads) for y in range(2) for c in range(2)
    ]
    return lax.ppermute(value, "ctx", pairs)


def shift(value, quads, by):
    pairs = [
        (q * 4 + e, (q + by) * 4 + e)
        for q in range(quads) for e in range(4) if 0 <= q + by < quads
    ]
    return lax.ppermute(value, "ctx", pairs)


def on_device(queries, keys, values, grad_out):
    quads = lax.axis_size("ctx") // 4
    place = lax.axis_index("ctx")
    me = jnp.stack([(place // 2) % 2, place % 2]).astype(jnp.int32)
    near1, near2, far1, far2, flip, own = deal(me, queries, keys, values, grad_out)
    flip = swap(flip, quads, 0, 1)
    near1 = swap(near1, quads, 1, 0)
    far1 = swap(far1, quads, 1, 1)
    near2 = swap(near2, quads, 1, 0)
    far2 = swap(far2, quads, 1, 1)
    mix_e = shift(jnp.stack([own[1, :, :HALF], flip[1, :, :HALF]]), quads, 1)
    wei_e = shift(jnp.stack([own[0, :, HALF:], flip[0, :, HALF:]]), quads, -1)
    mix_l = shift(jnp.stack([near1[0], far1[0]]), quads, 1)
    wei_l = shift(jnp.stack([near1[1], far1[1]]), quads, -1)
    part = correlate(
        me, own, flip, near1, near2, far1, far2, mix_e, mix_l, wei_e, wei_l
    )
    part = part + swap(part, quads, 1, 0)
    groups = [[q * 4 + e for q in range(quads)] for e in range(4)]
    spread = jnp.broadcast_to(part[None], (quads, 8, 128))
    gathered = lax.all_to_all(spread, "ctx", 0, 0, axis_index_groups=groups)
    mine = jnp.sum(gathered, axis=0).reshape(1, LAGS)
    other = swap(mine, quads, 0, 1)
    first = place % 2 == 0
    return jnp.concatenate(
        [jnp.where(first, mine, other), jnp.where(first, other, mine)], axis=0
    )


def solution(mesh):
    spec = P("ctx", "ch")
    return jax.shard_map(
        on_device, mesh=mesh, in_specs=(spec,) * 4, out_specs=P("ch", None), check_vma=False
    )
```

time: 451 us -> 83.1 us (0.18)
  blocking collectives: 329 us -> 20.8 us
  local copies, waits for them, and re-layouts: 73.4 us -> 4.98 us
  waiting for transfers between devices: 13.1 us -> 25.9 us
  other arithmetic: 8.06 us -> 0.84 us
  Pallas kernels: 0 us -> 5.39 us
    psum x1 -> x0, blocking collectives: 329 us -> none  [on_device(): return lax.psum(partial_value, 'ctx')]
    rev x5 -> x0, local copies, waits for them, and re-layouts: 60.8 us -> none  [on_device(): flipped = blocks[distance][::-1].reshape(tok_rows, groups_here, GROUP_CH)]
    all_to_all x0 -> x1, blocking collectives: none -> 20.8 us  [on_device(): gathered = lax.all_to_all(spread, 'ctx', 0, 0, axis_index_groups=groups)]
    ppermute x4 -> x11, waiting for transfers between devices: 13.1 us -> 25.9 us  [the longest x7 17.3 us: swap(): return lax.ppermute(value, 'ctx', pairs)]
    reshape x5 -> x0, local copies, waits for them, and re-layouts: 6.16 us -> none  [lag_sums(): return jnp.sum(flat.reshape(count, tok_rows, 2 * tok_rows - 1), axis=1)]
    pallas_call x0 -> x2, Pallas kernels: none -> 5.39 us  [the longest x1 3.29 us: correlate(): pl.pallas_call(correlate_kernel, in_specs=[pl.BlockSpec(memory_space=pltp...]
    another operation x8 -> x5, other arithmetic: 5.26 us -> 0.18 us  [the longest x1 0.07 us: on_device(): me = jnp.stack([place // 2 % 2, place % 2]).astype(jnp.int32)]
    ppermute x4 -> x11, starting transfers between devices: 20.3 us -> 24.7 us  [the longest x7 16 us: swap(): return lax.ppermute(value, 'ctx', pairs)]
  transfers between devices with their start and end apart: 4 -> 11, of which waited for: 2 -> 6; matrix products, arithmetic and copies ran while one was open for 15% -> 0% of each run, Pallas kernels for 0% -> 0%
where the time goes in v1:
time: 83.1 us; the launch traced here: 82.7 us
  waiting for transfers between devices  25.9 us (31%)
  starting transfers between devices  24.7 us (30%)
  blocking collectives  20.8 us (25%)
  Pallas kernels  5.39 us (6%)
  local copies, waits for them, and re-layouts  4.98 us (6%)
  other arithmetic  0.84 us (1%)
    all_to_all x1, blocking collectives, on_device(): gathered = lax.all_to_all(spread, 'ctx', 0, 0, axis_index_groups=groups)  20.8 us
    ppermute x7, waiting for transfers between devices, swap(): return lax.ppermute(value, 'ctx', pairs)  17.3 us
    ppermute x7, starting transfers between devices, swap(): return lax.ppermute(value, 'ctx', pairs)  16 us
    ppermute x4, starting transfers between devices, shift(): return lax.ppermute(value, 'ctx', pairs)  8.64 us
    ppermute x4, waiting for transfers between devices, shift(): return lax.ppermute(value, 'ctx', pairs)  8.61 us
    unnamed x8, local copies, waits for them, and re-layouts  4.9 us
    pallas_call x1, Pallas kernels, correlate(): pl.pallas_call(correlate_kernel, in_specs=[pl.BlockSpec(memory_space=pltp...  3.29 us
    pallas_call x1, Pallas kernels, deal(): pl.pallas_call(deal_kernel, grid_spec=pltpu.PrefetchScalarGridSpec(num_sc...  2.1 us
  transfers between devices with their start and end apart: 11, of which 6 were waited for; matrix products, arithmetic and copies ran while one was open for 0% of the time, Pallas kernels for 0%

profile of v1, /device:TPU:1, one launch (start us, length us, event | category | flops | bytes accessed | tf_op | source)
XLA Modules:
  0.0 82.7 jit_solution(13816846808155919939)
XLA Ops:
  0.0 0.1 pad_add_fusion.me
  0.1 0.0 copy-start
  0.1 1.2 %copy-done = bf16[256,2048]{1,0:T(8,128)(2,1)S(1)} copy-done((bf16[256,2048]{1,0:T(8,128)(2,1)S(1)}, bf16[256,2048]{1,0:T(8,128)(2,1)}, u32[]{:S(2)}) %copy-start) | copy-done | bytes 1048600
  1.3 0.0 copy-start.1
  1.3 1.2 %copy-done.1 = bf16[256,2048]{1,0:T(8,128)(2,1)S(1)} copy-done((bf16[256,2048]{1,0:T(8,128)(2,1)S(1)}, bf16[256,2048]{1,0:T(8,128)(2,1)}, u32[]{:S(2)}) %copy-start.1) | copy-done | bytes 1048600
  2.5 0.0 copy-start.2
  2.5 1.2 %copy-done.2 = bf16[256,2048]{1,0:T(8,128)(2,1)S(1)} copy-done((bf16[256,2048]{1,0:T(8,128)(2,1)S(1)}, bf16[256,2048]{1,0:T(8,128)(2,1)}, u32[]{:S(2)}) %copy-start.2) | copy-done | bytes 1048600
  3.8 0.0 copy-start.3
  3.8 1.2 %copy-done.3 = bf16[256,2048]{1,0:T(8,128)(2,1)S(1)} copy-done((bf16[256,2048]{1,0:T(8,128)(2,1)S(1)}, bf16[256,2048]{1,0:T(8,128)(2,1)}, u32[]{:S(2)}) %copy-start.3) | copy-done | bytes 1048600
  5.0 2.1 %deal.1 = (bf16[2,256,256]{2,1,0:T(8,128)(2,1)S(1)}, bf16[2,256,256]{2,1,0:T(8,128)(2,1)S(1)}, bf16[2,256,256]{2,1,0:T(8,128)(2,1)S(1)}, bf16[2,256,256]{2,1,0:T...) custom-call(s32[2]{0:T(128)S(1)} %pad_add_fusion.me, bf16[256,2048]{1,0:T(8,128)(2,1)S(1)} %copy-done, ...), custom_call_target="tpu_custom_call" | custom-call | tf_op jit(solution)/shard_map/deal/pallas_call | solution.py:53
  7.1 3.8 %collective-permute-start.1 = (bf16[2,256,256]{2,1,0:T(8,128)(2,1)S(1)}, bf16[2,256,256]{2,1,0:T(8,128)(2,1)S(1)}, u32[]{:S(2)}, u32[]{:S(2)}) collective-permute-start(bf16[2,256,256]{2,1,0:T(8,128)(2,1)S(1)} %get-tuple-element.13), channel_id=1, source_target_pairs={{0,4},{2,6},{4,0},{6,2},{8,12},{10,14},{12,8},{14,10},{16,20},{18,... | collective-permute-start | bytes 786440 | tf_op jit(solution)/shard_map/ppermute | solution.py:153
  10.9 0.1 collective-permute-start.2
  11.0 4.0 %collective-permute-start.3 = (bf16[2,256,256]{2,1,0:T(8,128)(2,1)S(1)}, bf16[2,256,256]{2,1,0:T(8,128)(2,1)S(1)}, u32[]{:S(2)}, u32[]{:S(2)}) collective-permute-start(bf16[2,256,256]{2,1,0:T(8,128)(2,1)S(1)} %get-tuple-element.15), channel_id=1, source_target_pairs={{0,6},{2,4},{4,2},{6,0},{8,14},{10,12},{12,10},{14,8},{16,22},{18,... | collective-permute-start | bytes 786440 | tf_op jit(solution)/shard_map/ppermute | solution.py:153
  15.0 0.0 collective-permute-start.4
  15.0 2.2 %collective-permute-start = (bf16[2,256,512]{2,1,0:T(8,128)(2,1)S(1)}, bf16[2,256,512]{2,1,0:T(8,128)(2,1)S(1)}, u32[]{:S(2)}, u32[]{:S(2)}) collective-permute-start(bf16[2,256,512]{2,1,0:T(8,128)(2,1)S(1)} %get-tuple-element.12), channel_id=1, source_target_pairs={{0,2},{2,0},{4,6},{6,4},{8,10},{10,8},{12,14},{14,12},{16,18},{18,... | collective-permute-start | bytes 1572872 | tf_op jit(solution)/shard_map/ppermute | solution.py:153
  17.2 0.0 collective-permute-done.1.near1
  17.3 14.6 %collective-permute-done.3.far1 = bf16[2,256,256]{2,1,0:T(8,128)(2,1)S(1)} collective-permute-done((bf16[2,256,256]{2,1,0:T(8,128)(2,1)S(1)}, bf16[2,256,256]{2,1,0:T(8,128)(2,1)S(1)}, u32[]{:S(2)}, u32[]{:S(2)}) %collective-permute-start.3) | collective-permute-done | bytes 262176 | tf_op jit(solution)/shard_map/ppermute | solution.py:153
  31.9 1.9 %collective-permute-start.6 = (bf16[2,256,256]{2,1,0:T(8,128)(2,1)S(1)}, bf16[2,256,256]{2,1,0:T(8,128)(2,1)S(1)}, u32[]{:S(2)}, u32[]{:S(2)}) collective-permute-start(bf16[2,256,256]{2,1,0:T(8,128)(2,1)S(1)} %pad_maximum_fusion.1), channel_id=1, source_target_pairs={{0,8},{2,10},{4,12},{6,14},{8,16},{10,18},{12,20},{14,22},{16,24},... | collective-permute-start | bytes 786440 | tf_op jit(solution)/shard_map/ppermute | solution.py:161
  33.9 1.3 %collective-permute-start.8 = (bf16[2,256,256]{2,1,0:T(8,128)(2,1)S(1)}, bf16[2,256,256]{2,1,0:T(8,128)(2,1)S(1)}, u32[]{:S(2)}, u32[]{:S(2)}) collective-permute-start(bf16[2,256,256]{2,1,0:T(8,128)(2,1)S(1)} %pad_maximum_fusion.3), channel_id=1, source_target_pairs={{8,0},{10,2},{12,4},{14,6},{16,8},{18,10},{20,12},{22,14},{24,16},... | collective-permute-start | bytes 786440 | tf_op jit(solution)/shard_map/ppermute | solution.py:161
  35.2 0.0 collective-permute-done.flip
  35.2 4.2 %collective-permute-start.5 = (bf16[2,256,256]{2,1,0:T(8,128)(2,1)S(1)}, bf16[2,256,256]{2,1,0:T(8,128)(2,1)S(1)}, u32[]{:S(2)}, u32[]{:S(2)}) collective-permute-start(bf16[2,256,256]{2,1,0:T(8,128)(2,1)S(1)} %pad_maximum_fusion), channel_id=1, source_target_pairs={{0,8},{2,10},{4,12},{6,14},{8,16},{10,18},{12,20},{14,22},{16,24},... | collective-permute-start | bytes 786440 | tf_op jit(solution)/shard_map/ppermute | solution.py:161
  39.5 0.0 collective-permute-done.2.near2
  39.5 1.3 %collective-permute-start.7 = (bf16[2,256,256]{2,1,0:T(8,128)(2,1)S(1)}, bf16[2,256,256]{2,1,0:T(8,128)(2,1)S(1)}, u32[]{:S(2)}, u32[]{:S(2)}) collective-permute-start(bf16[2,256,256]{2,1,0:T(8,128)(2,1)S(1)} %pad_maximum_fusion.2), channel_id=1, source_target_pairs={{8,0},{10,2},{12,4},{14,6},{16,8},{18,10},{20,12},{22,14},{24,16},... | collective-permute-start | bytes 786440 | tf_op jit(solution)/shard_map/ppermute | solution.py:161
  40.8 0.0 collective-permute-done.4.far2
  40.8 0.0 collective-permute-done.6.mix_l
  40.8 3.3 %collective-permute-done.8.wei_l = bf16[2,256,256]{2,1,0:T(8,128)(2,1)S(1)} collective-permute-done((bf16[2,256,256]{2,1,0:T(8,128)(2,1)S(1)}, bf16[2,256,256]{2,1,0:T(8,128)(2,1)S(1)}, u32[]{:S(2)}, u32[]{:S(2)}) %collective-permute-start.8) | collective-permute-done | bytes 262176 | tf_op jit(solution)/shard_map/ppermute | solution.py:161
  44.1 1.1 %collective-permute-done.5.mix_e = bf16[2,256,256]{2,1,0:T(8,128)(2,1)S(1)} collective-permute-done((bf16[2,256,256]{2,1,0:T(8,128)(2,1)S(1)}, bf16[2,256,256]{2,1,0:T(8,128)(2,1)S(1)}, u32[]{:S(2)}, u32[]{:S(2)}) %collective-permute-start.5) | collective-permute-done | bytes 262176 | tf_op jit(solution)/shard_map/ppermute | solution.py:161
  45.2 4.2 %collective-permute-done.7.wei_e = bf16[2,256,256]{2,1,0:T(8,128)(2,1)S(1)} collective-permute-done((bf16[2,256,256]{2,1,0:T(8,128)(2,1)S(1)}, bf16[2,256,256]{2,1,0:T(8,128)(2,1)S(1)}, u32[]{:S(2)}, u32[]{:S(2)}) %collective-permute-start.7) | collective-permute-done | bytes 262176 | tf_op jit(solution)/shard_map/ppermute | solution.py:161
  49.4 3.3 %correlate.1 = f32[8,128]{1,0:T(8,128)S(1)} custom-call(s32[2]{0:T(128)S(1)} %pad_add_fusion.me, bf16[2,256,512]{2,1,0:T(8,128)(2,1)S(1)} %get-tuple-element.11.own, bf16[2,256,512]{2,1,0:T(8,128)(2,1)S(1)} %collective-permute-done.flip, bf16[2,256,256]{2,1,0:T(8,128)(2,1)S(1)} %collective-permute-done.1.near1, ...), custom_call_target="tpu_custom_call" | custom-call | tf_op jit(solution)/shard_map/correlate/pallas_call | solution.py:130
  52.7 2.2 %collective-permute-start.9 = (f32[8,128]{1,0:T(8,128)S(1)}, f32[8,128]{1,0:T(8,128)S(1)}, u32[]{:S(2)}, u32[]{:S(2)}) collective-permute-start(f32[8,128]{1,0:T(8,128)S(1)} %correlate.1), channel_id=1, source_target_pairs={{0,4},{2,6},{4,0},{6,2},{8,12},{10,14},{12,8},{14,10},{16,20},{18,... | collective-permute-start | bytes 12296 | tf_op jit(solution)/shard_map/ppermute | solution.py:153
  54.9 1.8 %collective-permute-done.9 = f32[8,128]{1,0:T(8,128)S(1)} collective-permute-done((f32[8,128]{1,0:T(8,128)S(1)}, f32[8,128]{1,0:T(8,128)S(1)}, u32[]{:S(2)}, u32[]{:S(2)}) %collective-permute-start.9) | collective-permute-done | bytes 4128 | tf_op jit(solution)/shard_map/ppermute | solution.py:153
  56.8 20.8 %all_to_all.5 = f32[32,8,128]{2,1,0:T(8,128)S(1)} all-to-all(f32[32,8,128]{2,1,0:T(8,128)S(1)} %broadcast_in_dim.2), channel_id=1, replica_groups={{0,8,16,24,32,40,48,56,64,72,80,88,96,104,112,120,128,136,144,152,160,1..., dimensions={0} | all-to-all | bytes 262144 | tf_op jit(solution)/shard_map/all_to_all | solution.py:184
  77.6 3.7 %collective-permute-start.10 = (f32[1,1024]{1,0:T(1,128)S(1)}, f32[1,1024]{1,0:T(1,128)S(1)}, u32[]{:S(2)}, u32[]{:S(2)}) collective-permute-start(f32[1,1024]{1,0:T(1,128)S(1)} %bitcast.3), channel_id=1, source_target_pairs={{0,2},{2,0},{4,6},{6,4},{8,10},{10,8},{12,14},{14,12},{16,18},{18,... | collective-permute-start | bytes 12296 | tf_op jit(solution)/shard_map/ppermute | solution.py:153
  81.3 0.8 collective-permute-done.10
  82.1 0.6 pad_maximum_fusion.4
  (12 shorter events, 0.2 us)
Async XLA Ops:
  0.1 1.2 %copy-start = (bf16[256,2048]{1,0:T(8,128)(2,1)S(1)}, bf16[256,2048]{1,0:T(8,128)(2,1)}, u32[]{:S(2)}) copy-start(bf16[256,2048]{1,0:T(8,128)(2,1)} %q.1) | copy-start | bytes 3145732
  1.3 1.2 %copy-start.1 = (bf16[256,2048]{1,0:T(8,128)(2,1)S(1)}, bf16[256,2048]{1,0:T(8,128)(2,1)}, u32[]{:S(2)}) copy-start(bf16[256,2048]{1,0:T(8,128)(2,1)} %k.1) | copy-start | bytes 3145732
  2.5 1.2 %copy-start.2 = (bf16[256,2048]{1,0:T(8,128)(2,1)S(1)}, bf16[256,2048]{1,0:T(8,128)(2,1)}, u32[]{:S(2)}) copy-start(bf16[256,2048]{1,0:T(8,128)(2,1)} %v.1) | copy-start | bytes 3145732
  3.8 1.2 %copy-start.3 = (bf16[256,2048]{1,0:T(8,128)(2,1)S(1)}, bf16[256,2048]{1,0:T(8,128)(2,1)}, u32[]{:S(2)}) copy-start(bf16[256,2048]{1,0:T(8,128)(2,1)} %g.1) | copy-start | bytes 3145732
  7.1 10.1 %collective-permute-start.1 = (bf16[2,256,256]{2,1,0:T(8,128)(2,1)S(1)}, bf16[2,256,256]{2,1,0:T(8,128)(2,1)S(1)}, u32[]{:S(2)}, u32[]{:S(2)}) collective-permute-start(bf16[2,256,256]{2,1,0:T(8,128)(2,1)S(1)} %get-tuple-element.13), channel_id=1, source_target_pairs={{0,4},{2,6},{4,0},{6,2},{8,12},{10,14},{12,8},{14,10},{16,20},{18,... | collective-permute-start | bytes 786440 | tf_op jit(solution)/shard_map/ppermute | solution.py:153
  10.9 28.5 %collective-permute-start.2 = (bf16[2,256,256]{2,1,0:T(8,128)(2,1)S(1)}, bf16[2,256,256]{2,1,0:T(8,128)(2,1)S(1)}, u32[]{:S(2)}, u32[]{:S(2)}) collective-permute-start(bf16[2,256,256]{2,1,0:T(8,128)(2,1)S(1)} %get-tuple-element.14), channel_id=1, source_target_pairs={{0,4},{2,6},{4,0},{6,2},{8,12},{10,14},{12,8},{14,10},{16,20},{18,... | collective-permute-start | bytes 786440 | tf_op jit(solution)/shard_map/ppermute | solution.py:153
  11.0 20.9 %collective-permute-start.3 = (bf16[2,256,256]{2,1,0:T(8,128)(2,1)S(1)}, bf16[2,256,256]{2,1,0:T(8,128)(2,1)S(1)}, u32[]{:S(2)}, u32[]{:S(2)}) collective-permute-start(bf16[2,256,256]{2,1,0:T(8,128)(2,1)S(1)} %get-tuple-element.15), channel_id=1, source_target_pairs={{0,6},{2,4},{4,2},{6,0},{8,14},{10,12},{12,10},{14,8},{16,22},{18,... | collective-permute-start | bytes 786440 | tf_op jit(solution)/shard_map/ppermute | solution.py:153
  15.0 25.8 %collective-permute-start.4 = (bf16[2,256,256]{2,1,0:T(8,128)(2,1)S(1)}, bf16[2,256,256]{2,1,0:T(8,128)(2,1)S(1)}, u32[]{:S(2)}, u32[]{:S(2)}) collective-permute-start(bf16[2,256,256]{2,1,0:T(8,128)(2,1)S(1)} %get-tuple-element.16), channel_id=1, source_target_pairs={{0,6},{2,4},{4,2},{6,0},{8,14},{10,12},{12,10},{14,8},{16,22},{18,... | collective-permute-start | bytes 786440 | tf_op jit(solution)/shard_map/ppermute | solution.py:153
  15.0 20.1 %collective-permute-start = (bf16[2,256,512]{2,1,0:T(8,128)(2,1)S(1)}, bf16[2,256,512]{2,1,0:T(8,128)(2,1)S(1)}, u32[]{:S(2)}, u32[]{:S(2)}) collective-permute-start(bf16[2,256,512]{2,1,0:T(8,128)(2,1)S(1)} %get-tuple-element.12), channel_id=1, source_target_pairs={{0,2},{2,0},{4,6},{6,4},{8,10},{10,8},{12,14},{14,12},{16,18},{18,... | collective-permute-start | bytes 1572872 | tf_op jit(solution)/shard_map/ppermute | solution.py:153
  31.9 8.8 %collective-permute-start.6 = (bf16[2,256,256]{2,1,0:T(8,128)(2,1)S(1)}, bf16[2,256,256]{2,1,0:T(8,128)(2,1)S(1)}, u32[]{:S(2)}, u32[]{:S(2)}) collective-permute-start(bf16[2,256,256]{2,1,0:T(8,128)(2,1)S(1)} %pad_maximum_fusion.1), channel_id=1, source_target_pairs={{0,8},{2,10},{4,12},{6,14},{8,16},{10,18},{12,20},{14,22},{16,24},... | collective-permute-start | bytes 786440 | tf_op jit(solution)/shard_map/ppermute | solution.py:161
  33.9 10.2 %collective-permute-start.8 = (bf16[2,256,256]{2,1,0:T(8,128)(2,1)S(1)}, bf16[2,256,256]{2,1,0:T(8,128)(2,1)S(1)}, u32[]{:S(2)}, u32[]{:S(2)}) collective-permute-start(bf16[2,256,256]{2,1,0:T(8,128)(2,1)S(1)} %pad_maximum_fusion.3), channel_id=1, source_target_pairs={{8,0},{10,2},{12,4},{14,6},{16,8},{18,10},{20,12},{22,14},{24,16},... | collective-permute-start | bytes 786440 | tf_op jit(solution)/shard_map/ppermute | solution.py:161
  35.2 10.0 %collective-permute-start.5 = (bf16[2,256,256]{2,1,0:T(8,128)(2,1)S(1)}, bf16[2,256,256]{2,1,0:T(8,128)(2,1)S(1)}, u32[]{:S(2)}, u32[]{:S(2)}) collective-permute-start(bf16[2,256,256]{2,1,0:T(8,128)(2,1)S(1)} %pad_maximum_fusion), channel_id=1, source_target_pairs={{0,8},{2,10},{4,12},{6,14},{8,16},{10,18},{12,20},{14,22},{16,24},... | collective-permute-start | bytes 786440 | tf_op jit(solution)/shard_map/ppermute | solution.py:161
  39.5 9.9 %collective-permute-start.7 = (bf16[2,256,256]{2,1,0:T(8,128)(2,1)S(1)}, bf16[2,256,256]{2,1,0:T(8,128)(2,1)S(1)}, u32[]{:S(2)}, u32[]{:S(2)}) collective-permute-start(bf16[2,256,256]{2,1,0:T(8,128)(2,1)S(1)} %pad_maximum_fusion.2), channel_id=1, source_target_pairs={{8,0},{10,2},{12,4},{14,6},{16,8},{18,10},{20,12},{22,14},{24,16},... | collective-permute-start | bytes 786440 | tf_op jit(solution)/shard_map/ppermute | solution.py:161
  52.7 4.0 %collective-permute-start.9 = (f32[8,128]{1,0:T(8,128)S(1)}, f32[8,128]{1,0:T(8,128)S(1)}, u32[]{:S(2)}, u32[]{:S(2)}) collective-permute-start(f32[8,128]{1,0:T(8,128)S(1)} %correlate.1), channel_id=1, source_target_pairs={{0,4},{2,6},{4,0},{6,2},{8,12},{10,14},{12,8},{14,10},{16,20},{18,... | collective-permute-start | bytes 12296 | tf_op jit(solution)/shard_map/ppermute | solution.py:153
  77.6 4.5 %collective-permute-start.10 = (f32[1,1024]{1,0:T(1,128)S(1)}, f32[1,1024]{1,0:T(1,128)S(1)}, u32[]{:S(2)}, u32[]{:S(2)}) collective-permute-start(f32[1,1024]{1,0:T(1,128)S(1)} %bitcast.3), channel_id=1, source_target_pairs={{0,2},{2,0},{4,6},{6,4},{8,10},{10,8},{12,14},{14,12},{16,18},{18,... | collective-permute-start | bytes 12296 | tf_op jit(solution)/shard_map/ppermute | solution.py:153

commit v2 on v0

v2 whole, which is shorter than its diff:
```python
import jax
import jax.numpy as jnp
from jax import lax
from jax.experimental import pallas as pl
from jax.experimental.pallas import tpu as pltpu
from jax.sharding import PartitionSpec as P

BLK = 256
CH = 512
LAGS = 1024
MIB = 1024 * 1024
DEAL_MIB = 56
NT = (((1,), (1,)), ((), ()))
BF16 = jnp.bfloat16


def columns(yh, core):
    return pl.ds(pl.multiple_of(yh * 2 * CH + core * CH, CH), CH)


def product(a, b):
    return (a.astype(jnp.float32) * b.astype(jnp.float32)).astype(BF16)


def fetch(core, slots, sems, arrays, wanted):
    queries, keys, values, grad_out = arrays
    mixed, weighted = (keys, values), (queries, grad_out)

    def start(here):
        for i, (same, moving, cols) in enumerate(wanted):
            target = here if same else 1 - here
            pair = mixed if (target == 0) == moving else weighted
            for j in range(2):
                pltpu.make_async_copy(
                    pair[j].at[:, cols], slots.at[2 * i + j], sems.at[2 * i + j]
                ).start()

    pl.when(core == 0)(lambda: start(0))
    pl.when(core == 1)(lambda: start(1))

    def get(i):
        for j in range(2):
            pltpu.make_async_copy(
                keys.at[:, wanted[i][2]], slots.at[2 * i + j], sems.at[2 * i + j]
            ).wait()
        return product(slots[2 * i], slots[2 * i + 1])

    return get


def position():
    place = lax.axis_index("ctx")
    return (place // 2) % 2, place % 2


def deal_first(q, k, v, g, keep, give, slots, sems):
    yh, core = position()
    wanted = (
        (False, True, columns(1 - yh, 1 - core)),
        (False, True, columns(yh, 1 - core)),
        (True, True, columns(1 - yh, core)),
    )
    get = fetch(core, slots, sems, (q, k, v, g), wanted)
    give[0] = get(0)
    give[1] = get(1)
    keep[...] = get(2)


def deal_second(q, k, v, g, moving, keep, give, fixed, slots, sems):
    yh, core = position()
    wanted = (
        (False, False, columns(1 - yh, 1 - core)),
        (False, False, columns(yh, 1 - core)),
        (True, False, columns(1 - yh, core)),
        (True, True, columns(yh, core)),
        (True, False, columns(yh, core)),
    )
    get = fetch(core, slots, sems, (q, k, v, g), wanted)
    give[0] = get(0)
    give[1] = get(1)
    keep[...] = get(2)
    moving[...] = get(3)
    fixed[...] = get(4)


def deal(body, name, outs, pieces, arrays):
    vmem = pl.BlockSpec(memory_space=pltpu.VMEM)
    return pl.pallas_call(
        body,
        in_specs=[pl.BlockSpec(memory_space=pl.ANY)] * 4,
        out_specs=[vmem] * len(outs),
        out_shape=[pltpu.VMEM(shape, BF16) for shape in outs],
        scratch_shapes=[
            pltpu.VMEM((2 * pieces, BLK, CH), BF16),
            pltpu.SemaphoreType.DMA((2 * pieces,)),
        ],
        compiler_params=pltpu.CompilerParams(vmem_limit_bytes=DEAL_MIB * MIB),
        name=name,
    )(*arrays)


def gather_kernel(beyond, near, far, onto, moving):
    onto[...] = far[...]
    moving[0:2] = beyond[...]
    moving[4:6] = near[...]
    moving[6:8] = far[...]


def gather(beyond, near, far):
    vmem = pl.BlockSpec(memory_space=pltpu.VMEM)
    return pl.pallas_call(
        gather_kernel,
        in_specs=[vmem] * 3,
        out_specs=[vmem] * 2,
        out_shape=[
            jax.ShapeDtypeStruct((2, BLK, CH), BF16),
            jax.ShapeDtypeStruct((8, BLK, CH), BF16),
        ],
        compiler_params=pltpu.CompilerParams(vmem_limit_bytes=40 * MIB),
        name="gather",
    )(beyond, near, far)


def lag_sums(table):
    wide = 5 * BLK
    rows = BLK
    while rows > 1:
        half = rows // 2
        low, high = table[:half], table[half:rows]
        if half % 128 == 0:
            wide = wide - half
            table = low[:, :wide] + high[:, half : half + wide]
        else:
            table = low + pltpu.roll(high, wide - half, 1)
        rows = half
    return table


def correlate_kernel(moving_in, onto, own, flip, far, out, moving, table):
    yh, core = position()
    home = 2 * yh + core
    moving[2:4] = onto[...]

    def fill(here):
        for d in range(5):
            total = None
            for i, fixed in enumerate((own, flip.at[1], far.at[0], far.at[1])):
                if here == 0:
                    at = 4 + (home ^ i) - d
                    there = jnp.where(at >= 4, 4, 0) + ((at & 3) ^ home)
                    pair = moving[there], fixed[...]
                else:
                    at = (home ^ i) + d
                    there = jnp.where(at < 4, 4, 0) + ((at & 3) ^ home)
                    pair = fixed[...], moving[there]
                dot = lax.dot_general(*pair, NT, preferred_element_type=jnp.float32)
                total = dot if total is None else total + dot
            table[:, pl.ds(d * BLK, BLK)] = total

    pl.when(core == 0)(lambda: fill(0))
    pl.when(core == 1)(lambda: fill(1))
    sums = lag_sums(table[...])
    for i in range(8):
        out[i : i + 1, :] = sums[:, i * 128 : (i + 1) * 128]


def correlate(moving, *arrays):
    vmem = pl.BlockSpec(memory_space=pltpu.VMEM)
    return pl.pallas_call(
        correlate_kernel,
        in_specs=[vmem] * (1 + len(arrays)),
        out_specs=[vmem, vmem],
        out_shape=[
            jax.ShapeDtypeStruct((8, 128), jnp.float32),
            jax.ShapeDtypeStruct(moving.shape, BF16),
        ],
        input_output_aliases={0: 1},
        scratch_shapes=[pltpu.VMEM((BLK, 5 * BLK), jnp.float32)],
        compiler_params=pltpu.CompilerParams(vmem_limit_bytes=40 * MIB),
        name="correlate",
    )(moving, *arrays)[0]


def swap(value, quads, far, flip):
    pairs = [
        ((q * 2 + y) * 2 + c, (q * 2 + (y ^ far)) * 2 + (c ^ flip))
        for q in range(quads) for y in range(2) for c in range(2)
    ]
    return lax.ppermute(value, "ctx", pairs)


def onward(value, quads):
    pairs = [
        (q * 4 + e, (q + 1 - 2 * (e % 2)) * 4 + e)
        for q in range(quads) for e in range(4) if 0 <= q + 1 - 2 * (e % 2) < quads
    ]
    return lax.ppermute(value, "ctx", pairs)


def on_device(queries, keys, values, grad_out):
    quads = lax.axis_size("ctx") // 4
    arrays = (queries, keys, values, grad_out)
    one, two = (BLK, CH), (2, BLK, CH)
    keep, give = deal(deal_first, "deal_first", [one, two], 3, arrays)
    got = swap(give, quads, 0, 1)
    far_moving = swap(jnp.stack([keep, got[0]]), quads, 1, 0)
    moving, keep, give, fixed = deal(
        deal_second, "deal_second", [one, one, two, one], 5, arrays
    )
    near_moving = jnp.stack([moving, got[1]])
    got = swap(give, quads, 0, 1)
    far_fixed = swap(jnp.stack([keep, got[0]]), quads, 1, 0)
    beyond = onward(near_moving, quads)
    onto, table = gather(beyond, near_moving, far_moving)
    onto = onward(onto, quads)
    part = correlate(table, onto, fixed, got, far_fixed)
    part = part + swap(part, quads, 0, 1)
    groups = [[q * 4 + y * 2 + c for q in range(quads) for y in range(2)] for c in range(2)]
    spread = jnp.broadcast_to(part[None], (2 * quads, 8, 128))
    gathered = lax.all_to_all(spread, "ctx", 0, 0, axis_index_groups=groups)
    return jnp.sum(gathered.reshape(quads, 2, 8, 128), axis=0).reshape(2, LAGS)


def solution(mesh):
    spec = P("ctx", "ch")
    return jax.shard_map(
        on_device, mesh=mesh, in_specs=(spec,) * 4, out_specs=P("ch", None), check_vma=False
    )
```

time: 451 us -> 64.9 us (0.14)
  blocking collectives: 329 us -> 26.5 us
  local copies, waits for them, and re-layouts: 73.4 us -> 0.68 us
  starting transfers between devices: 20.3 us -> 10.5 us
  other arithmetic: 8.06 us -> 0.19 us
  waiting for transfers between devices: 13.1 us -> 20.7 us
  Pallas kernels: 0 us -> 5.51 us
    psum x1 -> x0, blocking collectives: 329 us -> none  [on_device(): return lax.psum(partial_value, 'ctx')]
    rev x5 -> x0, local copies, waits for them, and re-layouts: 60.8 us -> none  [on_device(): flipped = blocks[distance][::-1].reshape(tok_rows, groups_here, GROUP_CH)]
    all_to_all x0 -> x1, blocking collectives: none -> 26.5 us  [on_device(): gathered = lax.all_to_all(spread, 'ctx', 0, 0, axis_index_groups=groups)]
    ppermute x4 -> x7, starting transfers between devices: 20.3 us -> 10.5 us  [the longest x5 7.94 us: swap(): return lax.ppermute(value, 'ctx', pairs)]
    ppermute x4 -> x7, waiting for transfers between devices: 13.1 us -> 20.7 us  [the longest x5 20.7 us: swap(): return lax.ppermute(value, 'ctx', pairs)]
    reshape x5 -> x0, local copies, waits for them, and re-layouts: 6.16 us -> none  [lag_sums(): return jnp.sum(flat.reshape(count, tok_rows, 2 * tok_rows - 1), axis=1)]
    pallas_call x0 -> x4, Pallas kernels: none -> 5.51 us  [the longest x2 3.29 us: deal(): pl.pallas_call(body, in_specs=[pl.BlockSpec(memory_space=pl.ANY)] * 4, ou...]
    another operation x8 -> x3, other arithmetic: 5.26 us -> 0.15 us  [the longest x1 0.05 us: on_device(): far_moving = swap(jnp.stack([keep, got[0]]), quads, 1, 0)]
  transfers between devices with their start and end apart: 4 -> 7, of which waited for: 2 -> 3; matrix products, arithmetic and copies ran while one was open for 15% -> 0% of each run, Pallas kernels for 0% -> 3%
where the time goes in v2:
time: 64.9 us; the launch traced here: 64.1 us
  blocking collectives  26.5 us (41%)
  waiting for transfers between devices  20.7 us (32%)
  starting transfers between devices  10.5 us (16%)
  Pallas kernels  5.51 us (8%)
  local copies, waits for them, and re-layouts  0.68 us (1%)
    all_to_all x1, blocking collectives, on_device(): gathered = lax.all_to_all(spread, 'ctx', 0, 0, axis_index_groups=groups)  26.5 us
    ppermute x5, waiting for transfers between devices, swap(): return lax.ppermute(value, 'ctx', pairs)  20.7 us
    ppermute x5, starting transfers between devices, swap(): return lax.ppermute(value, 'ctx', pairs)  7.94 us
    pallas_call x2, Pallas kernels, deal(): pl.pallas_call(body, in_specs=[pl.BlockSpec(memory_space=pl.ANY)] * 4, ou...  3.29 us
    ppermute x2, starting transfers between devices, onward(): return lax.ppermute(value, 'ctx', pairs)  2.58 us
    pallas_call x1, Pallas kernels, correlate(): pl.pallas_call(correlate_kernel, in_specs=[vmem] * (1 + len(arrays)), out...  2.08 us
  transfers between devices with their start and end apart: 7, of which 3 were waited for; matrix products, arithmetic and copies ran while one was open for 0% of the time, Pallas kernels for 3%

profile of v2, /device:TPU:1, one launch (start us, length us, event | category | flops | bytes accessed | tf_op | source)
XLA Modules:
  0.0 64.1 jit_solution(5459042505159835162)
XLA Ops:
  0.0 1.5 %deal_first.1 = (bf16[256,512]{1,0:T(8,128)(2,1)S(1)}, bf16[2,256,512]{2,1,0:T(8,128)(2,1)S(1)}) custom-call(bf16[256,2048]{1,0:T(8,128)(2,1)} %q.3, bf16[256,2048]{1,0:T(8,128)(2,1)} %k.3, bf16[256,2048]{1,0:T(8,128)(2,1)} %v.3, bf16[256,2048]{1,0:T(8,128)(2,1)} %g.3), custom_call_target="tpu_custom_call" | custom-call | tf_op jit(solution)/shard_map/deal_first/pallas_call | solution.py:88
  1.5 3.3 %collective-permute-start = (bf16[2,256,512]{2,1,0:T(8,128)(2,1)S(1)}, bf16[2,256,512]{2,1,0:T(8,128)(2,1)S(1)}, u32[]{:S(2)}, u32[]{:S(2)}) collective-permute-start(bf16[2,256,512]{2,1,0:T(8,128)(2,1)S(1)} %get-tuple-element.15), channel_id=1, source_target_pairs={{0,2},{2,0},{4,6},{6,4},{8,10},{10,8},{12,14},{14,12},{16,18},{18,... | collective-permute-start | bytes 1572872 | tf_op jit(solution)/shard_map/ppermute | solution.py:189
  4.8 1.8 %deal_second.1 = (bf16[256,512]{1,0:T(8,128)(2,1)S(1)}, bf16[256,512]{1,0:T(8,128)(2,1)S(1)}, bf16[2,256,512]{2,1,0:T(8,128)(2,1)S(1)}, bf16[256,512]{1,0:T(8,128)(2,1)S(1)}) custom-call(bf16[256,2048]{1,0:T(8,128)(2,1)} %q.3, bf16[256,2048]{1,0:T(8,128)(2,1)} %k.3, bf16[256,2048]{1,0:T(8,128)(2,1)} %v.3, bf16[256,2048]{1,0:T(8,128)(2,1)} %g.3), custom_call_target="tpu_custom_call" | custom-call | tf_op jit(solution)/shard_map/deal_second/pallas_call | solution.py:88
  6.6 0.1 collective-permute-start.4
  6.8 0.0 collective-permute-done
  6.8 0.1 pad_maximum_fusion.1
  6.9 1.2 %collective-permute-start.2 = (bf16[2,256,512]{2,1,0:T(8,128)(2,1)S(1)}, bf16[2,256,512]{2,1,0:T(8,128)(2,1)S(1)}, u32[]{:S(2)}, u32[]{:S(2)}) collective-permute-start(bf16[2,256,512]{2,1,0:T(8,128)(2,1)S(1)} %pad_maximum_fusion.1), channel_id=1, source_target_pairs={{0,4},{2,6},{4,0},{6,2},{8,12},{10,14},{12,8},{14,10},{16,20},{18,... | collective-permute-start | bytes 1572872 | tf_op jit(solution)/shard_map/ppermute | solution.py:189
  8.1 0.1 pad_maximum_fusion.near
  8.2 1.3 %collective-permute-start.1 = (bf16[2,256,512]{2,1,0:T(8,128)(2,1)S(1)}, bf16[2,256,512]{2,1,0:T(8,128)(2,1)S(1)}, u32[]{:S(2)}, u32[]{:S(2)}) collective-permute-start(bf16[2,256,512]{2,1,0:T(8,128)(2,1)S(1)} %pad_maximum_fusion.near), channel_id=1, source_target_pairs={{0,8},{4,12},{8,16},{10,2},{12,20},{14,6},{16,24},{18,10},{20,28},... | collective-permute-start | bytes 1572872 | tf_op jit(solution)/shard_map/ppermute | solution.py:197
  9.5 0.0 collective-permute-done.4.flip
  9.5 0.1 pad_maximum_fusion.2
  9.6 1.9 %collective-permute-start.5 = (bf16[2,256,512]{2,1,0:T(8,128)(2,1)S(1)}, bf16[2,256,512]{2,1,0:T(8,128)(2,1)S(1)}, u32[]{:S(2)}, u32[]{:S(2)}) collective-permute-start(bf16[2,256,512]{2,1,0:T(8,128)(2,1)S(1)} %pad_maximum_fusion.2), channel_id=1, source_target_pairs={{0,4},{2,6},{4,0},{6,2},{8,12},{10,14},{12,8},{14,10},{16,20},{18,... | collective-permute-start | bytes 1572872 | tf_op jit(solution)/shard_map/ppermute | solution.py:189
  11.5 10.0 %collective-permute-done.2.far = bf16[2,256,512]{2,1,0:T(8,128)(2,1)S(1)} collective-permute-done((bf16[2,256,512]{2,1,0:T(8,128)(2,1)S(1)}, bf16[2,256,512]{2,1,0:T(8,128)(2,1)S(1)}, u32[]{:S(2)}, u32[]{:S(2)}) %collective-permute-start.2) | collective-permute-done | bytes 524320 | tf_op jit(solution)/shard_map/ppermute | solution.py:189
  21.5 0.0 collective-permute-done.1.beyond
  21.5 0.1 gather.1
  21.7 1.3 %collective-permute-start.3 = (bf16[2,256,512]{2,1,0:T(8,128)(2,1)S(1)}, bf16[2,256,512]{2,1,0:T(8,128)(2,1)S(1)}, u32[]{:S(2)}, u32[]{:S(2)}) collective-permute-start(bf16[2,256,512]{2,1,0:T(8,128)(2,1)S(1)} %get-tuple-element.18), channel_id=1, source_target_pairs={{0,8},{4,12},{8,16},{10,2},{12,20},{14,6},{16,24},{18,10},{20,28},... | collective-permute-start | bytes 1572872 | tf_op jit(solution)/shard_map/ppermute | solution.py:197
  23.0 9.8 %collective-permute-done.5.far = bf16[2,256,512]{2,1,0:T(8,128)(2,1)S(1)} collective-permute-done((bf16[2,256,512]{2,1,0:T(8,128)(2,1)S(1)}, bf16[2,256,512]{2,1,0:T(8,128)(2,1)S(1)}, u32[]{:S(2)}, u32[]{:S(2)}) %collective-permute-start.5) | collective-permute-done | bytes 524320 | tf_op jit(solution)/shard_map/ppermute | solution.py:189
  32.8 0.0 collective-permute-done.3.onto
  32.8 2.1 %correlate.1 = (f32[8,128]{1,0:T(8,128)S(1)}, bf16[8,256,512]{2,1,0:T(8,128)(2,1)S(1)}) custom-call(bf16[8,256,512]{2,1,0:T(8,128)(2,1)S(1)} %get-tuple-element.17.moving_in, bf16[2,256,512]{2,1,0:T(8,128)(2,1)S(1)} %collective-permute-done.3.onto, bf16[256,512]{1,0:T(8,128)(2,1)S(1)} %get-tuple-element.19.own, ...), custom_call_target="tpu_custom_call", output_to_operand_aliasing={{1}: (0, {})} | custom-call | tf_op jit(solution)/shard_map/correlate/pallas_call | solution.py:169
  34.8 1.3 %collective-permute-start.6 = (f32[8,128]{1,0:T(8,128)S(1)}, f32[8,128]{1,0:T(8,128)S(1)}, u32[]{:S(2)}, u32[]{:S(2)}) collective-permute-start(f32[8,128]{1,0:T(8,128)S(1)} %get-tuple-element.22), channel_id=1, source_target_pairs={{0,2},{2,0},{4,6},{6,4},{8,10},{10,8},{12,14},{14,12},{16,18},{18,... | collective-permute-start | bytes 12296 | tf_op jit(solution)/shard_map/ppermute | solution.py:189
  36.2 0.8 %collective-permute-done.6 = f32[8,128]{1,0:T(8,128)S(1)} collective-permute-done((f32[8,128]{1,0:T(8,128)S(1)}, f32[8,128]{1,0:T(8,128)S(1)}, u32[]{:S(2)}, u32[]{:S(2)}) %collective-permute-start.6) | collective-permute-done | bytes 4128 | tf_op jit(solution)/shard_map/ppermute | solution.py:189
  37.0 26.5 %all_to_all.5 = f32[64,8,128]{2,1,0:T(8,128)S(1)} all-to-all(f32[64,8,128]{2,1,0:T(8,128)S(1)} %broadcast_in_dim.2), channel_id=1, replica_groups={{0,4,8,12,16,20,24,28,32,36,40,44,48,52,56,60,64,68,72,76,80,84,88,92,9..., dimensions={0} | all-to-all | bytes 524288 | tf_op jit(solution)/shard_map/all_to_all | solution.py:220
  63.5 0.6 copy.8
  (5 shorter events, 0.1 us)
Async XLA Ops:
  1.5 5.3 %collective-permute-start = (bf16[2,256,512]{2,1,0:T(8,128)(2,1)S(1)}, bf16[2,256,512]{2,1,0:T(8,128)(2,1)S(1)}, u32[]{:S(2)}, u32[]{:S(2)}) collective-permute-start(bf16[2,256,512]{2,1,0:T(8,128)(2,1)S(1)} %get-tuple-element.15), channel_id=1, source_target_pairs={{0,2},{2,0},{4,6},{6,4},{8,10},{10,8},{12,14},{14,12},{16,18},{18,... | collective-permute-start | bytes 1572872 | tf_op jit(solution)/shard_map/ppermute | solution.py:189
  6.6 2.9 %collective-permute-start.4 = (bf16[2,256,512]{2,1,0:T(8,128)(2,1)S(1)}, bf16[2,256,512]{2,1,0:T(8,128)(2,1)S(1)}, u32[]{:S(2)}, u32[]{:S(2)}) collective-permute-start(bf16[2,256,512]{2,1,0:T(8,128)(2,1)S(1)} %get-tuple-element.20), channel_id=1, source_target_pairs={{0,2},{2,0},{4,6},{6,4},{8,10},{10,8},{12,14},{14,12},{16,18},{18,... | collective-permute-start | bytes 1572872 | tf_op jit(solution)/shard_map/ppermute | solution.py:189
  6.9 14.6 %collective-permute-start.2 = (bf16[2,256,512]{2,1,0:T(8,128)(2,1)S(1)}, bf16[2,256,512]{2,1,0:T(8,128)(2,1)S(1)}, u32[]{:S(2)}, u32[]{:S(2)}) collective-permute-start(bf16[2,256,512]{2,1,0:T(8,128)(2,1)S(1)} %pad_maximum_fusion.1), channel_id=1, source_target_pairs={{0,4},{2,6},{4,0},{6,2},{8,12},{10,14},{12,8},{14,10},{16,20},{18,... | collective-permute-start | bytes 1572872 | tf_op jit(solution)/shard_map/ppermute | solution.py:189
  8.2 13.3 %collective-permute-start.1 = (bf16[2,256,512]{2,1,0:T(8,128)(2,1)S(1)}, bf16[2,256,512]{2,1,0:T(8,128)(2,1)S(1)}, u32[]{:S(2)}, u32[]{:S(2)}) collective-permute-start(bf16[2,256,512]{2,1,0:T(8,128)(2,1)S(1)} %pad_maximum_fusion.near), channel_id=1, source_target_pairs={{0,8},{4,12},{8,16},{10,2},{12,20},{14,6},{16,24},{18,10},{20,28},... | collective-permute-start | bytes 1572872 | tf_op jit(solution)/shard_map/ppermute | solution.py:197
  9.6 23.2 %collective-permute-start.5 = (bf16[2,256,512]{2,1,0:T(8,128)(2,1)S(1)}, bf16[2,256,512]{2,1,0:T(8,128)(2,1)S(1)}, u32[]{:S(2)}, u32[]{:S(2)}) collective-permute-start(bf16[2,256,512]{2,1,0:T(8,128)(2,1)S(1)} %pad_maximum_fusion.2), channel_id=1, source_target_pairs={{0,4},{2,6},{4,0},{6,2},{8,12},{10,14},{12,8},{14,10},{16,20},{18,... | collective-permute-start | bytes 1572872 | tf_op jit(solution)/shard_map/ppermute | solution.py:189
  21.7 11.1 %collective-permute-start.3 = (bf16[2,256,512]{2,1,0:T(8,128)(2,1)S(1)}, bf16[2,256,512]{2,1,0:T(8,128)(2,1)S(1)}, u32[]{:S(2)}, u32[]{:S(2)}) collective-permute-start(bf16[2,256,512]{2,1,0:T(8,128)(2,1)S(1)} %get-tuple-element.18), channel_id=1, source_target_pairs={{0,8},{4,12},{8,16},{10,2},{12,20},{14,6},{16,24},{18,10},{20,28},... | collective-permute-start | bytes 1572872 | tf_op jit(solution)/shard_map/ppermute | solution.py:197
  34.8 2.1 %collective-permute-start.6 = (f32[8,128]{1,0:T(8,128)S(1)}, f32[8,128]{1,0:T(8,128)S(1)}, u32[]{:S(2)}, u32[]{:S(2)}) collective-permute-start(f32[8,128]{1,0:T(8,128)S(1)} %get-tuple-element.22), channel_id=1, source_target_pairs={{0,2},{2,0},{4,6},{6,4},{8,10},{10,8},{12,14},{14,12},{16,18},{18,... | collective-permute-start | bytes 12296 | tf_op jit(solution)/shard_map/ppermute | solution.py:189

commit v3 on v2

v3 whole, which is shorter than its diff:
```python
import jax
import jax.numpy as jnp
from jax import lax
from jax.experimental import pallas as pl
from jax.experimental.pallas import tpu as pltpu
from jax.sharding import PartitionSpec as P

BLK = 256
CH = 512
LAGS = 1024
MIB = 1024 * 1024
DEAL_MIB = 56
MAIN_COST = 4 * 10**9
NT = (((1,), (1,)), ((), ()))
BF16 = jnp.bfloat16


def columns(yh, core):
    return pl.ds(pl.multiple_of(yh * 2 * CH + core * CH, CH), CH)


def product(a, b):
    return (a.astype(jnp.float32) * b.astype(jnp.float32)).astype(BF16)


def fetch(core, slots, sems, arrays, wanted):
    queries, keys, values, grad_out = arrays
    mixed, weighted = (keys, values), (queries, grad_out)

    def start(here):
        for i, (same, moving, cols) in enumerate(wanted):
            target = here if same else 1 - here
            pair = mixed if (target == 0) == moving else weighted
            for j in range(2):
                pltpu.make_async_copy(
                    pair[j].at[:, cols], slots.at[2 * i + j], sems.at[2 * i + j]
                ).start()

    pl.when(core == 0)(lambda: start(0))
    pl.when(core == 1)(lambda: start(1))

    def get(i):
        for j in range(2):
            pltpu.make_async_copy(
                keys.at[:, wanted[i][2]], slots.at[2 * i + j], sems.at[2 * i + j]
            ).wait()
        return product(slots[2 * i], slots[2 * i + 1])

    return get


def position():
    place = lax.axis_index("ctx")
    return (place // 2) % 2, place % 2


def deal_first(q, k, v, g, far, give, own, slots, sems):
    yh, core = position()
    wanted = (
        (False, True, columns(yh, 1 - core)),
        (True, True, columns(1 - yh, core)),
        (False, True, columns(1 - yh, 1 - core)),
        (True, True, columns(yh, core)),
    )
    get = fetch(core, slots, sems, (q, k, v, g), wanted)
    give[...] = get(0)
    far[0] = get(1)
    far[1] = get(2)
    own[...] = get(3)


def deal_second(q, k, v, g, give, give_own, keep, own, slots, sems):
    yh, core = position()
    wanted = (
        (False, False, columns(1 - yh, 1 - core)),
        (False, False, columns(yh, 1 - core)),
        (True, False, columns(1 - yh, core)),
        (True, False, columns(yh, core)),
    )
    get = fetch(core, slots, sems, (q, k, v, g), wanted)
    give[...] = get(0)
    give_own[...] = get(1)
    keep[...] = get(2)
    own[...] = get(3)


def deal(body, name, shapes, arrays):
    vmem = pl.BlockSpec(memory_space=pltpu.VMEM)
    return pl.pallas_call(
        body,
        in_specs=[pl.BlockSpec(memory_space=pl.ANY)] * 4,
        out_specs=[vmem] * len(shapes),
        out_shape=[pltpu.VMEM(shape, BF16) for shape in shapes],
        scratch_shapes=[
            pltpu.VMEM((8, BLK, CH), BF16),
            pltpu.SemaphoreType.DMA((8,)),
        ],
        compiler_params=pltpu.CompilerParams(vmem_limit_bytes=DEAL_MIB * MIB),
        name=name,
    )(*arrays)


def gather_kernel(beyond, near, far, onto, pass_on, moving, give):
    give[0] = pass_on[...]
    give[1] = far[1]
    moving[0:2] = beyond[...]
    moving[2] = onto[...]
    moving[3] = jnp.zeros((BLK, CH), BF16)
    moving[4:6] = near[...]
    moving[6] = far[0]
    moving[7] = jnp.zeros((BLK, CH), BF16)


def gather(*arrays):
    vmem = pl.BlockSpec(memory_space=pltpu.VMEM)
    return pl.pallas_call(
        gather_kernel,
        in_specs=[vmem] * 5,
        out_specs=[vmem] * 2,
        out_shape=[
            jax.ShapeDtypeStruct((8, BLK, CH), BF16),
            jax.ShapeDtypeStruct((2, BLK, CH), BF16),
        ],
        compiler_params=pltpu.CompilerParams(vmem_limit_bytes=40 * MIB),
        name="gather",
    )(*arrays)


def lag_sums(table):
    wide = 5 * BLK
    rows = BLK
    while rows > 1:
        half = rows // 2
        low, high = table[:half], table[half:rows]
        if half % 128 == 0:
            wide = wide - half
            table = low[:, :wide] + high[:, half : half + wide]
        else:
            table = low + pltpu.roll(high, wide - half, 1)
        rows = half
    return table


def block_dot(core, moving, fixed):
    pair = (moving, fixed) if core == 0 else (fixed, moving)
    return lax.dot_general(*pair, NT, preferred_element_type=jnp.float32)


def on_core(core, body):
    pl.when(core == 0)(lambda: body(0))
    pl.when(core == 1)(lambda: body(1))


def main_kernel(moving, own, flip, far, table):
    yh, core = position()
    home = 2 * yh + core

    def body(here):
        for d in range(5):
            total = None
            for i, fixed in enumerate((own, flip, far.at[0], far.at[1])):
                if here == 0:
                    at = 4 + (home ^ i) - d
                    there = jnp.where(at >= 4, 4, 0) + ((at & 3) ^ home)
                else:
                    at = (home ^ i) + d
                    there = jnp.where(at < 4, 4, 0) + ((at & 3) ^ home)
                dot = block_dot(here, moving[there], fixed[...])
                total = dot if total is None else total + dot
            table[:, pl.ds(d * BLK, BLK)] = total

    on_core(core, body)


def tail_kernel(table_in, last, own, flip, far, out, table):
    yh, core = position()
    home = 2 * yh + core

    def body(here):
        def add(d, which, fixed):
            at = pl.ds(pl.multiple_of(d * BLK, BLK), BLK)
            table[:, at] = table_in[:, at] + block_dot(here, last[which], fixed[...])

        for i, fixed in enumerate((own, flip, far.at[0])):
            gap = (home ^ i) - (home ^ 3)
            gap = gap if here == 0 else -gap
            add(gap & 3, (gap > 0).astype(jnp.int32), fixed)
        add(0, 1, far.at[1])
        add(4, 0, far.at[1])

    on_core(core, body)
    sums = lag_sums(table[...])
    for i in range(8):
        out[i : i + 1, :] = sums[:, i * 128 : (i + 1) * 128]


def correlate(moving, last, *fixed):
    vmem = pl.BlockSpec(memory_space=pltpu.VMEM)
    params = pltpu.CompilerParams(vmem_limit_bytes=40 * MIB)
    table_t = jax.ShapeDtypeStruct((BLK, 5 * BLK), jnp.float32)
    table = pl.pallas_call(
        main_kernel,
        in_specs=[vmem] * 4,
        out_specs=vmem,
        out_shape=table_t,
        compiler_params=params,
        cost_estimate=pl.CostEstimate(
            flops=MAIN_COST, bytes_accessed=4 * MIB, transcendentals=0
        ),
        name="main",
    )(moving, *fixed)
    return pl.pallas_call(
        tail_kernel,
        in_specs=[vmem] * 5,
        out_specs=vmem,
        out_shape=jax.ShapeDtypeStruct((8, 128), jnp.float32),
        scratch_shapes=[pltpu.VMEM((BLK, 5 * BLK), jnp.float32)],
        compiler_params=params,
        name="tail",
    )(table, last, *fixed)


def swap(value, quads, far, flip):
    pairs = [
        ((q * 2 + y) * 2 + c, (q * 2 + (y ^ far)) * 2 + (c ^ flip))
        for q in range(quads) for y in range(2) for c in range(2)
    ]
    return lax.ppermute(value, "ctx", pairs)


def onward(value, quads, first=1):
    pairs = []
    for q in range(quads):
        for e in range(4):
            to = q + first * (1 - 2 * (e % 2))
            if 0 <= to < quads:
                pairs.append((q * 4 + e, to * 4 + e))
    return lax.ppermute(value, "ctx", pairs)


def on_device(queries, keys, values, grad_out):
    quads = lax.axis_size("ctx") // 4
    arrays = (queries, keys, values, grad_out)
    one, two = (BLK, CH), (2, BLK, CH)
    far_moving, give, own_moving = deal(deal_first, "deal_first", [two, one, one], arrays)
    flip_moving = swap(give, quads, 0, 1)
    far_moving = swap(far_moving, quads, 1, 0)
    near_moving = jnp.stack([own_moving, flip_moving])
    beyond = onward(near_moving, quads)
    give, give_own, keep, own_fixed = deal(deal_second, "deal_second", [one] * 4, arrays)
    far_fixed = swap(jnp.stack([keep, swap(give, quads, 0, 1)]), quads, 1, 0)
    flip_fixed = swap(give_own, quads, 0, 1)
    onto_far = onward(far_moving[1], quads, -1)
    onto_near = onward(far_moving[0], quads)
    moving, give = gather(beyond, near_moving, far_moving, onto_near, onto_far)
    last = swap(give, quads, 0, 1)
    part = correlate(moving, last, own_fixed, flip_fixed, far_fixed)
    part = part + swap(part, quads, 0, 1)
    groups = [[q * 4 + y * 2 + c for q in range(quads) for y in range(2)] for c in range(2)]
    spread = jnp.broadcast_to(part[None], (2 * quads, 8, 128))
    gathered = lax.all_to_all(spread, "ctx", 0, 0, axis_index_groups=groups)
    return jnp.sum(gathered.reshape(quads, 2, 8, 128), axis=0).reshape(2, LAGS)


def solution(mesh):
    spec = P("ctx", "ch")
    return jax.shard_map(
        on_device, mesh=mesh, in_specs=(spec,) * 4, out_specs=P("ch", None), check_vma=False
    )
```

time: 64.9 us -> 63.2 us (0.974)
  waiting for transfers between devices: 20.7 us -> 7.86 us
  starting transfers between devices: 10.5 us -> 21.6 us
    ppermute x5 -> x7, waiting for transfers between devices: 20.7 us -> 5.46 us  [swap(): return lax.ppermute(value, 'ctx', pairs)]
    ppermute x5 -> x7, starting transfers between devices: 7.94 us -> 14.1 us  [swap(): return lax.ppermute(value, 'ctx', pairs)]
    ppermute x2 -> x3, starting transfers between devices: 2.58 us -> 7.56 us  [onward(): return lax.ppermute(value, 'ctx', pairs)]
    ppermute x2 -> x3, waiting for transfers between devices: 0.01 us -> 2.4 us  [onward(): return lax.ppermute(value, 'ctx', pairs)]
    pallas_call x2 -> x3, Pallas kernels: 2.22 us -> 2.79 us  [the longest x1 1.55 us: correlate(): pl.pallas_call(main_kernel, in_specs=[vmem] * 4, out_specs=vmem, out_shap...]
  transfers between devices with their start and end apart: 7 -> 10, of which waited for: 3 -> 4; matrix products, arithmetic and copies ran while one was open for 0% -> 0% of each run, Pallas kernels for 3% -> 5%
where the time goes in v3:
time: 63.2 us; the launch traced here: 62.5 us
  blocking collectives  26 us (41%)
  starting transfers between devices  21.6 us (34%)
  waiting for transfers between devices  7.86 us (12%)
  Pallas kernels  6.09 us (10%)
  local copies, waits for them, and re-layouts  0.66 us (1%)
    all_to_all x1, blocking collectives, on_device(): gathered = lax.all_to_all(spread, 'ctx', 0, 0, axis_index_groups=groups)  26 us
    ppermute x7, starting transfers between devices, swap(): return lax.ppermute(value, 'ctx', pairs)  14.1 us
    ppermute x3, starting transfers between devices, onward(): return lax.ppermute(value, 'ctx', pairs)  7.56 us
    ppermute x7, waiting for transfers between devices, swap(): return lax.ppermute(value, 'ctx', pairs)  5.46 us
    pallas_call x2, Pallas kernels, deal(): pl.pallas_call(body, in_specs=[pl.BlockSpec(memory_space=pl.ANY)] * 4, ou...  3.3 us
    ppermute x3, waiting for transfers between devices, onward(): return lax.ppermute(value, 'ctx', pairs)  2.4 us
    pallas_call x1, Pallas kernels, correlate(): pl.pallas_call(main_kernel, in_specs=[vmem] * 4, out_specs=vmem, out_shap...  1.55 us
  transfers between devices with their start and end apart: 10, of which 4 were waited for; matrix products, arithmetic and copies ran while one was open for 0% of the time, Pallas kernels for 5%

profile of v3, /device:TPU:1, one launch (start us, length us, event | category | flops | bytes accessed | tf_op | source)
XLA Modules:
  0.0 62.5 jit_solution(4479819532458939339)
XLA Ops:
  0.0 1.7 %deal_first.1 = (bf16[2,256,512]{2,1,0:T(8,128)(2,1)S(1)}, bf16[256,512]{1,0:T(8,128)(2,1)S(1)}, bf16[256,512]{1,0:T(8,128)(2,1)S(1)}) custom-call(bf16[256,2048]{1,0:T(8,128)(2,1)} %q.3, bf16[256,2048]{1,0:T(8,128)(2,1)} %k.3, bf16[256,2048]{1,0:T(8,128)(2,1)} %v.3, bf16[256,2048]{1,0:T(8,128)(2,1)} %g.3), custom_call_target="tpu_custom_call" | custom-call | tf_op jit(solution)/shard_map/deal_first/pallas_call | solution.py:89
  1.7 3.8 %collective-permute-start.2 = (bf16[2,256,512]{2,1,0:T(8,128)(2,1)S(1)}, bf16[2,256,512]{2,1,0:T(8,128)(2,1)S(1)}, u32[]{:S(2)}, u32[]{:S(2)}) collective-permute-start(bf16[2,256,512]{2,1,0:T(8,128)(2,1)S(1)} %get-tuple-element.16), channel_id=1, source_target_pairs={{0,4},{2,6},{4,0},{6,2},{8,12},{10,14},{12,8},{14,10},{16,20},{18,... | collective-permute-start | bytes 1572872 | tf_op jit(solution)/shard_map/ppermute | solution.py:228
  5.5 1.0 %collective-permute-start = (bf16[256,512]{1,0:T(8,128)(2,1)S(1)}, bf16[256,512]{1,0:T(8,128)(2,1)S(1)}, u32[]{:S(2)}, u32[]{:S(2)}) collective-permute-start(bf16[256,512]{1,0:T(8,128)(2,1)S(1)} %get-tuple-element.15), channel_id=1, source_target_pairs={{0,2},{2,0},{4,6},{6,4},{8,10},{10,8},{12,14},{14,12},{16,18},{18,... | collective-permute-start | bytes 786440 | tf_op jit(solution)/shard_map/ppermute | solution.py:228
  6.4 1.6 %deal_second.1 = (bf16[256,512]{1,0:T(8,128)(2,1)S(1)}, bf16[256,512]{1,0:T(8,128)(2,1)S(1)}, bf16[256,512]{1,0:T(8,128)(2,1)S(1)}, bf16[256,512]{1,0:T(8,128)(2,1)S(1)}) custom-call(bf16[256,2048]{1,0:T(8,128)(2,1)} %q.3, bf16[256,2048]{1,0:T(8,128)(2,1)} %k.3, bf16[256,2048]{1,0:T(8,128)(2,1)} %v.3, bf16[256,2048]{1,0:T(8,128)(2,1)} %g.3), custom_call_target="tpu_custom_call" | custom-call | tf_op jit(solution)/shard_map/deal_second/pallas_call | solution.py:89
  8.1 0.1 collective-permute-start.6
  8.2 0.0 collective-permute-done
  8.2 0.1 pad_maximum_fusion.near
  8.3 1.3 %collective-permute-start.1 = (bf16[2,256,512]{2,1,0:T(8,128)(2,1)S(1)}, bf16[2,256,512]{2,1,0:T(8,128)(2,1)S(1)}, u32[]{:S(2)}, u32[]{:S(2)}) collective-permute-start(bf16[2,256,512]{2,1,0:T(8,128)(2,1)S(1)} %pad_maximum_fusion.near), channel_id=1, source_target_pairs={{0,8},{4,12},{8,16},{10,2},{12,20},{14,6},{16,24},{18,10},{20,28},... | collective-permute-start | bytes 1572872 | tf_op jit(solution)/shard_map/ppermute | solution.py:238
  9.6 0.2 collective-permute-done.6
  9.7 0.1 pad_maximum_fusion.1
  9.8 1.9 %collective-permute-start.7 = (bf16[2,256,512]{2,1,0:T(8,128)(2,1)S(1)}, bf16[2,256,512]{2,1,0:T(8,128)(2,1)S(1)}, u32[]{:S(2)}, u32[]{:S(2)}) collective-permute-start(bf16[2,256,512]{2,1,0:T(8,128)(2,1)S(1)} %pad_maximum_fusion.1), channel_id=1, source_target_pairs={{0,4},{2,6},{4,0},{6,2},{8,12},{10,14},{12,8},{14,10},{16,20},{18,... | collective-permute-start | bytes 1572872 | tf_op jit(solution)/shard_map/ppermute | solution.py:228
  11.7 4.4 %collective-permute-done.2.far = bf16[2,256,512]{2,1,0:T(8,128)(2,1)S(1)} collective-permute-done((bf16[2,256,512]{2,1,0:T(8,128)(2,1)S(1)}, bf16[2,256,512]{2,1,0:T(8,128)(2,1)S(1)}, u32[]{:S(2)}, u32[]{:S(2)}) %collective-permute-start.2) | collective-permute-done | bytes 524320 | tf_op jit(solution)/shard_map/ppermute | solution.py:228
  16.1 1.3 %collective-permute-start.3 = (bf16[256,512]{1,0:T(8,128)(2,1)S(1)}, bf16[256,512]{1,0:T(8,128)(2,1)S(1)}, u32[]{:S(2)}, u32[]{:S(2)}) collective-permute-start(bf16[256,512]{1,0:T(8,128)(2,1)S(1)} %get-tuple-element.24), channel_id=1, source_target_pairs={{0,8},{4,12},{8,16},{10,2},{12,20},{14,6},{16,24},{18,10},{20,28},... | collective-permute-start | bytes 786440 | tf_op jit(solution)/shard_map/ppermute | solution.py:238
  17.4 5.0 %collective-permute-start.4 = (bf16[256,512]{1,0:T(8,128)(2,1)S(1)}, bf16[256,512]{1,0:T(8,128)(2,1)S(1)}, u32[]{:S(2)}, u32[]{:S(2)}) collective-permute-start(bf16[256,512]{1,0:T(8,128)(2,1)S(1)} %get-tuple-element.23), channel_id=1, source_target_pairs={{2,10},{6,14},{8,0},{10,18},{12,4},{14,22},{16,8},{18,26},{20,12},... | collective-permute-start | bytes 786440 | tf_op jit(solution)/shard_map/ppermute | solution.py:238
  22.4 2.4 %collective-permute-start.5 = (bf16[256,512]{1,0:T(8,128)(2,1)S(1)}, bf16[256,512]{1,0:T(8,128)(2,1)S(1)}, u32[]{:S(2)}, u32[]{:S(2)}) collective-permute-start(bf16[256,512]{1,0:T(8,128)(2,1)S(1)} %get-tuple-element.19), channel_id=1, source_target_pairs={{0,2},{2,0},{4,6},{6,4},{8,10},{10,8},{12,14},{14,12},{16,18},{18,... | collective-permute-start | bytes 786440 | tf_op jit(solution)/shard_map/ppermute | solution.py:228
  24.8 0.0 collective-permute-done.1.beyond
  24.8 0.0 collective-permute-done.3.onto
  24.8 2.4 %collective-permute-done.4.pass_on = bf16[256,512]{1,0:T(8,128)(2,1)S(1)} collective-permute-done((bf16[256,512]{1,0:T(8,128)(2,1)S(1)}, bf16[256,512]{1,0:T(8,128)(2,1)S(1)}, u32[]{:S(2)}, u32[]{:S(2)}) %collective-permute-start.4) | collective-permute-done | bytes 262176 | tf_op jit(solution)/shard_map/ppermute | solution.py:238
  27.2 0.2 gather.1
  27.4 4.6 %collective-permute-start.8 = (bf16[2,256,512]{2,1,0:T(8,128)(2,1)S(1)}, bf16[2,256,512]{2,1,0:T(8,128)(2,1)S(1)}, u32[]{:S(2)}, u32[]{:S(2)}) collective-permute-start(bf16[2,256,512]{2,1,0:T(8,128)(2,1)S(1)} %get-tuple-element.22), channel_id=1, source_target_pairs={{0,2},{2,0},{4,6},{6,4},{8,10},{10,8},{12,14},{14,12},{16,18},{18,... | collective-permute-start | bytes 1572872 | tf_op jit(solution)/shard_map/ppermute | solution.py:228
  32.0 0.0 collective-permute-done.5.flip
  32.0 0.0 collective-permute-done.7.far
  32.0 1.5 %main.1.table_in = f32[256,1280]{1,0:T(8,128)S(1)} custom-call(bf16[8,256,512]{2,1,0:T(8,128)(2,1)S(1)} %get-tuple-element.17.moving, bf16[256,512]{1,0:T(8,128)(2,1)S(1)} %get-tuple-element.18.own, bf16[256,512]{1,0:T(8,128)(2,1)S(1)} %collective-permute-done.5.flip, bf16[2,256,512]{2,1,0:T(8,128)(2,1)S(1)} %collective-permute-done.7.far), custom_call_target="tpu_custom_call" | custom-call | flops 4000000000 | bytes 4194304 | tf_op jit(solution)/shard_map/main/pallas_call | solution.py:201
  33.5 0.0 collective-permute-done.8.last
  33.6 1.1 %tail.1 = f32[8,128]{1,0:T(8,128)S(1)} custom-call(f32[256,1280]{1,0:T(8,128)S(1)} %main.1.table_in, bf16[2,256,512]{2,1,0:T(8,128)(2,1)S(1)} %collective-permute-done.8.last, bf16[256,512]{1,0:T(8,128)(2,1)S(1)} %get-tuple-element.18.own, bf16[256,512]{1,0:T(8,128)(2,1)S(1)} %collective-permute-done.5.flip, bf16[2,256,512]{2,1,0:T(8,128)(2,1)S(1)} %collective-permute-done.7.far), custom_call_target="tpu_custom_call" | custom-call | tf_op jit(solution)/shard_map/tail/pallas_call | solution.py:212
  34.6 0.3 collective-permute-start.9
  35.0 0.9 %collective-permute-done.9 = f32[8,128]{1,0:T(8,128)S(1)} collective-permute-done((f32[8,128]{1,0:T(8,128)S(1)}, f32[8,128]{1,0:T(8,128)S(1)}, u32[]{:S(2)}, u32[]{:S(2)}) %collective-permute-start.9) | collective-permute-done | bytes 4128 | tf_op jit(solution)/shard_map/ppermute | solution.py:228
  35.9 26.0 %all_to_all.5 = f32[64,8,128]{2,1,0:T(8,128)S(1)} all-to-all(f32[64,8,128]{2,1,0:T(8,128)S(1)} %broadcast_in_dim.2), channel_id=1, replica_groups={{0,4,8,12,16,20,24,28,32,36,40,44,48,52,56,60,64,68,72,76,80,84,88,92,9..., dimensions={0} | all-to-all | bytes 524288 | tf_op jit(solution)/shard_map/all_to_all | solution.py:261
  61.9 0.6 copy.7
  (4 shorter events, 0.1 us)
Async XLA Ops:
  1.7 14.4 %collective-permute-start.2 = (bf16[2,256,512]{2,1,0:T(8,128)(2,1)S(1)}, bf16[2,256,512]{2,1,0:T(8,128)(2,1)S(1)}, u32[]{:S(2)}, u32[]{:S(2)}) collective-permute-start(bf16[2,256,512]{2,1,0:T(8,128)(2,1)S(1)} %get-tuple-element.16), channel_id=1, source_target_pairs={{0,4},{2,6},{4,0},{6,2},{8,12},{10,14},{12,8},{14,10},{16,20},{18,... | collective-permute-start | bytes 1572872 | tf_op jit(solution)/shard_map/ppermute | solution.py:228
  5.5 2.7 %collective-permute-start = (bf16[256,512]{1,0:T(8,128)(2,1)S(1)}, bf16[256,512]{1,0:T(8,128)(2,1)S(1)}, u32[]{:S(2)}, u32[]{:S(2)}) collective-permute-start(bf16[256,512]{1,0:T(8,128)(2,1)S(1)} %get-tuple-element.15), channel_id=1, source_target_pairs={{0,2},{2,0},{4,6},{6,4},{8,10},{10,8},{12,14},{14,12},{16,18},{18,... | collective-permute-start | bytes 786440 | tf_op jit(solution)/shard_map/ppermute | solution.py:228
  8.1 1.6 %collective-permute-start.6 = (bf16[256,512]{1,0:T(8,128)(2,1)S(1)}, bf16[256,512]{1,0:T(8,128)(2,1)S(1)}, u32[]{:S(2)}, u32[]{:S(2)}) collective-permute-start(bf16[256,512]{1,0:T(8,128)(2,1)S(1)} %get-tuple-element.21), channel_id=1, source_target_pairs={{0,2},{2,0},{4,6},{6,4},{8,10},{10,8},{12,14},{14,12},{16,18},{18,... | collective-permute-start | bytes 786440 | tf_op jit(solution)/shard_map/ppermute | solution.py:228
  8.3 16.6 %collective-permute-start.1 = (bf16[2,256,512]{2,1,0:T(8,128)(2,1)S(1)}, bf16[2,256,512]{2,1,0:T(8,128)(2,1)S(1)}, u32[]{:S(2)}, u32[]{:S(2)}) collective-permute-start(bf16[2,256,512]{2,1,0:T(8,128)(2,1)S(1)} %pad_maximum_fusion.near), channel_id=1, source_target_pairs={{0,8},{4,12},{8,16},{10,2},{12,20},{14,6},{16,24},{18,10},{20,28},... | collective-permute-start | bytes 1572872 | tf_op jit(solution)/shard_map/ppermute | solution.py:238
  9.8 22.2 %collective-permute-start.7 = (bf16[2,256,512]{2,1,0:T(8,128)(2,1)S(1)}, bf16[2,256,512]{2,1,0:T(8,128)(2,1)S(1)}, u32[]{:S(2)}, u32[]{:S(2)}) collective-permute-start(bf16[2,256,512]{2,1,0:T(8,128)(2,1)S(1)} %pad_maximum_fusion.1), channel_id=1, source_target_pairs={{0,4},{2,6},{4,0},{6,2},{8,12},{10,14},{12,8},{14,10},{16,20},{18,... | collective-permute-start | bytes 1572872 | tf_op jit(solution)/shard_map/ppermute | solution.py:228
  16.1 8.7 %collective-permute-start.3 = (bf16[256,512]{1,0:T(8,128)(2,1)S(1)}, bf16[256,512]{1,0:T(8,128)(2,1)S(1)}, u32[]{:S(2)}, u32[]{:S(2)}) collective-permute-start(bf16[256,512]{1,0:T(8,128)(2,1)S(1)} %get-tuple-element.24), channel_id=1, source_target_pairs={{0,8},{4,12},{8,16},{10,2},{12,20},{14,6},{16,24},{18,10},{20,28},... | collective-permute-start | bytes 786440 | tf_op jit(solution)/shard_map/ppermute | solution.py:238
  17.4 9.8 %collective-permute-start.4 = (bf16[256,512]{1,0:T(8,128)(2,1)S(1)}, bf16[256,512]{1,0:T(8,128)(2,1)S(1)}, u32[]{:S(2)}, u32[]{:S(2)}) collective-permute-start(bf16[256,512]{1,0:T(8,128)(2,1)S(1)} %get-tuple-element.23), channel_id=1, source_target_pairs={{2,10},{6,14},{8,0},{10,18},{12,4},{14,22},{16,8},{18,26},{20,12},... | collective-permute-start | bytes 786440 | tf_op jit(solution)/shard_map/ppermute | solution.py:238
  22.4 9.6 %collective-permute-start.5 = (bf16[256,512]{1,0:T(8,128)(2,1)S(1)}, bf16[256,512]{1,0:T(8,128)(2,1)S(1)}, u32[]{:S(2)}, u32[]{:S(2)}) collective-permute-start(bf16[256,512]{1,0:T(8,128)(2,1)S(1)} %get-tuple-element.19), channel_id=1, source_target_pairs={{0,2},{2,0},{4,6},{6,4},{8,10},{10,8},{12,14},{14,12},{16,18},{18,... | collective-permute-start | bytes 786440 | tf_op jit(solution)/shard_map/ppermute | solution.py:228
  27.4 6.1 %collective-permute-start.8 = (bf16[2,256,512]{2,1,0:T(8,128)(2,1)S(1)}, bf16[2,256,512]{2,1,0:T(8,128)(2,1)S(1)}, u32[]{:S(2)}, u32[]{:S(2)}) collective-permute-start(bf16[2,256,512]{2,1,0:T(8,128)(2,1)S(1)} %get-tuple-element.22), channel_id=1, source_target_pairs={{0,2},{2,0},{4,6},{6,4},{8,10},{10,8},{12,14},{14,12},{16,18},{18,... | collective-permute-start | bytes 1572872 | tf_op jit(solution)/shard_map/ppermute | solution.py:228
  34.6 1.2 %collective-permute-start.9 = (f32[8,128]{1,0:T(8,128)S(1)}, f32[8,128]{1,0:T(8,128)S(1)}, u32[]{:S(2)}, u32[]{:S(2)}) collective-permute-start(f32[8,128]{1,0:T(8,128)S(1)} %tail.1), channel_id=1, source_target_pairs={{0,2},{2,0},{4,6},{6,4},{8,10},{10,8},{12,14},{14,12},{16,18},{18,... | collective-permute-start | bytes 12296 | tf_op jit(solution)/shard_map/ppermute | solution.py:228

commit v4 on v3

v4 whole, which is shorter than its diff:
```python
import functools

import jax
import jax.numpy as jnp
from jax import lax
from jax.experimental import pallas as pl
from jax.experimental.pallas import tpu as pltpu
from jax.sharding import PartitionSpec as P

BLK = 256
CH = 512
LAGS = 1024
MIB = 1024 * 1024
DEAL_MIB = 56
MAIN_COST = 15 * 2 * BLK * BLK * CH
NT = (((1,), (1,)), ((), ()))
BF16 = jnp.bfloat16


def columns(yh, core):
    return pl.ds(pl.multiple_of(yh * 2 * CH + core * CH, CH), CH)


def product(a, b):
    return (a.astype(jnp.float32) * b.astype(jnp.float32)).astype(BF16)


def fetch(core, slots, sems, arrays, wanted):
    queries, keys, values, grad_out = arrays
    mixed, weighted = (keys, values), (queries, grad_out)

    def start(here):
        for i, (same, moving, cols) in enumerate(wanted):
            target = here if same else 1 - here
            pair = mixed if (target == 0) == moving else weighted
            for j in range(2):
                pltpu.make_async_copy(
                    pair[j].at[:, cols], slots.at[2 * i + j], sems.at[2 * i + j]
                ).start()

    pl.when(core == 0)(lambda: start(0))
    pl.when(core == 1)(lambda: start(1))

    def get(i):
        for j in range(2):
            pltpu.make_async_copy(
                keys.at[:, wanted[i][2]], slots.at[2 * i + j], sems.at[2 * i + j]
            ).wait()
        return product(slots[2 * i], slots[2 * i + 1])

    return get


def position():
    place = lax.axis_index("ctx")
    return (place // 2) % 2, place % 2


def deal_first(q, k, v, g, far, give, own, slots, sems):
    yh, core = position()
    wanted = (
        (False, True, columns(yh, 1 - core)),
        (True, True, columns(1 - yh, core)),
        (False, True, columns(1 - yh, 1 - core)),
        (True, True, columns(yh, core)),
    )
    get = fetch(core, slots, sems, (q, k, v, g), wanted)
    give[...] = get(0)
    far[0] = get(1)
    far[1] = get(2)
    own[...] = get(3)


def deal_second(q, k, v, g, top, low, give_own, keep, own, slots, sems):
    yh, core = position()
    wanted = (
        (False, False, columns(1 - yh, 1 - core)),
        (False, False, columns(yh, 1 - core)),
        (True, False, columns(1 - yh, core)),
        (True, False, columns(yh, core)),
    )
    get = fetch(core, slots, sems, (q, k, v, g), wanted)
    give = get(0)
    top[...] = give[: BLK // 2]
    low[...] = give[BLK // 2 :]
    give_own[...] = get(1)
    keep[...] = get(2)
    own[...] = get(3)


def deal(body, name, shapes, arrays):
    vmem = pl.BlockSpec(memory_space=pltpu.VMEM)
    return pl.pallas_call(
        body,
        in_specs=[pl.BlockSpec(memory_space=pl.ANY)] * 4,
        out_specs=[vmem] * len(shapes),
        out_shape=[pltpu.VMEM(shape, BF16) for shape in shapes],
        scratch_shapes=[
            pltpu.VMEM((8, BLK, CH), BF16),
            pltpu.SemaphoreType.DMA((8,)),
        ],
        compiler_params=pltpu.CompilerParams(vmem_limit_bytes=DEAL_MIB * MIB),
        name=name,
    )(*arrays)


def lag_sums(table):
    wide = 5 * BLK - 128
    table = table[:128, :wide] + table[128:, 128:]
    total = table[:8]
    for row in range(8, 128, 8):
        total = total + pltpu.roll(table[row : row + 8], wide - row, 1)
    sums = total[:1]
    for row in range(1, 8):
        sums = sums + pltpu.roll(total[row : row + 1], wide - row, 1)
    return sums


def block_dot(core, moving, fixed):
    pair = (moving, fixed) if core == 0 else (fixed, moving)
    return lax.dot_general(*pair, NT, preferred_element_type=jnp.float32)


def by_home(body):
    place = lax.rem(lax.axis_index("ctx"), 4)
    for home in range(4):
        pl.when(place == home)(functools.partial(body, home))


def columns_of(d):
    return pl.ds(d * BLK, BLK)


def main_kernel(beyond, near, far, last, onto, own, flip, fixed, table):
    def body(home):
        core = home & 1
        here = {home: near.at[0], home ^ 1: near.at[1], home ^ 2: far.at[0], home ^ 3: last}
        there = {home: beyond.at[0], home ^ 1: beyond.at[1], home ^ 2: onto}
        stay = {home: own, home ^ 1: flip, home ^ 2: fixed.at[0], home ^ 3: fixed.at[1]}
        for d in range(5):
            total = None
            for block, ref in stay.items():
                other = block - d if core == 0 else block + d
                source = here if 0 <= other < 4 else there
                if (other & 3) in source:
                    dot = block_dot(core, source[other & 3][...], ref[...])
                    total = dot if total is None else total + dot
            table[:, columns_of(d)] = total

    by_home(body)


def tail_kernel(table_in, onto, own, flip, fixed, out, table):
    def body(home):
        core = home & 1
        stay = {home: own, home ^ 1: flip, home ^ 2: fixed.at[0], home ^ 3: fixed.at[1]}
        for d in range(5):
            block = (home ^ 3) + (d - 4 if core == 0 else 4 - d)
            total = table_in[:, columns_of(d)]
            if 0 <= block < 4:
                total = total + block_dot(core, onto[...], stay[block][...])
            table[:, columns_of(d)] = total

    by_home(body)
    sums = lag_sums(table[...])
    for i in range(8):
        out[i : i + 1, :] = sums[:, i * 128 : (i + 1) * 128]


def correlate(moving, onto_far, *fixed):
    vmem = pl.BlockSpec(memory_space=pltpu.VMEM)
    params = pltpu.CompilerParams(vmem_limit_bytes=40 * MIB)
    table = pl.pallas_call(
        main_kernel,
        in_specs=[vmem] * (len(moving) + len(fixed)),
        out_specs=vmem,
        out_shape=jax.ShapeDtypeStruct((BLK, 5 * BLK), jnp.float32),
        compiler_params=params,
        cost_estimate=pl.CostEstimate(
            flops=MAIN_COST, bytes_accessed=4 * MIB, transcendentals=0
        ),
        name="main",
    )(*moving, *fixed)
    return pl.pallas_call(
        tail_kernel,
        in_specs=[vmem] * (2 + len(fixed)),
        out_specs=vmem,
        out_shape=jax.ShapeDtypeStruct((8, 128), jnp.float32),
        scratch_shapes=[pltpu.VMEM((BLK, 5 * BLK), jnp.float32)],
        compiler_params=params,
        name="tail",
    )(table, onto_far, *fixed)


def swap(value, quads, far, flip):
    pairs = [
        ((q * 2 + y) * 2 + c, (q * 2 + (y ^ far)) * 2 + (c ^ flip))
        for q in range(quads) for y in range(2) for c in range(2)
    ]
    return lax.ppermute(value, "ctx", pairs)


def onward(value, quads, flip=0):
    pairs = []
    for q in range(quads):
        for e in range(4):
            core = e % 2 ^ flip
            to = q + 1 - 2 * core
            if 0 <= to < quads:
                pairs.append((q * 4 + e, to * 4 + (e ^ flip)))
    return lax.ppermute(value, "ctx", pairs)


def on_device(queries, keys, values, grad_out):
    quads = lax.axis_size("ctx") // 4
    arrays = (queries, keys, values, grad_out)
    one, two = (BLK, CH), (2, BLK, CH)
    far_moving, give, own_moving = deal(deal_first, "deal_first", [two, one, one], arrays)
    flip_moving = swap(give, quads, 0, 1)
    far_moving = swap(far_moving, quads, 1, 0)
    near_moving = jnp.stack([own_moving, flip_moving])
    beyond = onward(near_moving, quads)
    top, low, give_own, keep, own_fixed = deal(
        deal_second, "deal_second", [(BLK // 2, CH)] * 2 + [one] * 3, arrays
    )
    got = jnp.concatenate([swap(top, quads, 0, 1), swap(low, quads, 0, 1)])
    far_fixed = swap(jnp.stack([keep, got]), quads, 1, 0)
    flip_fixed = swap(give_own, quads, 0, 1)
    last = swap(far_moving[1], quads, 0, 1)
    onto_near = onward(far_moving[0], quads)
    onto_far = onward(far_moving[1], quads, 1)
    moving = (beyond, near_moving, far_moving, last, onto_near)
    part = correlate(moving, onto_far, own_fixed, flip_fixed, far_fixed)
    part = part + swap(part, quads, 0, 1)
    groups = [[q * 4 + y * 2 + c for q in range(quads) for y in range(2)] for c in range(2)]
    spread = jnp.broadcast_to(part[None], (2 * quads, 8, 128))
    gathered = lax.all_to_all(spread, "ctx", 0, 0, axis_index_groups=groups)
    return jnp.sum(gathered.reshape(quads, 2, 8, 128), axis=0).reshape(2, LAGS)


def solution(mesh):
    spec = P("ctx", "ch")
    return jax.shard_map(
        on_device, mesh=mesh, in_specs=(spec,) * 4, out_specs=P("ch", None), check_vma=False
    )
```

time: 63.2 us -> 61.1 us (0.967)
  waiting for transfers between devices: 7.86 us -> 6.62 us
  starting transfers between devices: 21.6 us -> 20.9 us
    ppermute x3, starting transfers between devices: 7.56 us -> 6.02 us  [onward(): return lax.ppermute(value, 'ctx', pairs)]
    ppermute x7 -> x8, waiting for transfers between devices: 5.46 us -> 4.17 us  [swap(): return lax.ppermute(value, 'ctx', pairs)]
    ppermute x7 -> x8, starting transfers between devices: 14.1 us -> 14.9 us  [swap(): return lax.ppermute(value, 'ctx', pairs)]
    pallas_call x3 -> x2, Pallas kernels: 2.79 us -> 2.16 us  [the longest x1 1.44 us: correlate(): pl.pallas_call(main_kernel, in_specs=[vmem] * (len(moving) + len(fixed)),...]
  transfers between devices with their start and end apart: 10 -> 11, of which waited for: 4 -> 6; matrix products, arithmetic and copies ran while one was open for 0% -> 0% of each run, Pallas kernels for 5% -> 5%
where the time goes in v4:
time: 61.1 us; the launch traced here: 60.3 us
  blocking collectives  26.4 us (43%)
  starting transfers between devices  20.9 us (34%)
  waiting for transfers between devices  6.62 us (11%)
  Pallas kernels  5.46 us (9%)
  local copies, waits for them, and re-layouts  0.66 us (1%)
    all_to_all x1, blocking collectives, on_device(): gathered = lax.all_to_all(spread, 'ctx', 0, 0, axis_index_groups=groups)  26.4 us
    ppermute x8, starting transfers between devices, swap(): return lax.ppermute(value, 'ctx', pairs)  14.9 us
    ppermute x3, starting transfers between devices, onward(): return lax.ppermute(value, 'ctx', pairs)  6.02 us
    ppermute x8, waiting for transfers between devices, swap(): return lax.ppermute(value, 'ctx', pairs)  4.17 us
    pallas_call x2, Pallas kernels, deal(): pl.pallas_call(body, in_specs=[pl.BlockSpec(memory_space=pl.ANY)] * 4, ou...  3.3 us
    ppermute x3, waiting for transfers between devices, onward(): return lax.ppermute(value, 'ctx', pairs)  2.44 us
    pallas_call x1, Pallas kernels, correlate(): pl.pallas_call(main_kernel, in_specs=[vmem] * (len(moving) + len(fixed)),...  1.44 us
  transfers between devices with their start and end apart: 11, of which 6 were waited for; matrix products, arithmetic and copies ran while one was open for 0% of the time, Pallas kernels for 5%

profile of v4, /device:TPU:1, one launch (start us, length us, event | category | flops | bytes accessed | tf_op | source)
XLA Modules:
  0.0 60.3 jit_solution(1023036749654643735)
XLA Ops:
  0.0 1.7 %deal_first.1 = (bf16[2,256,512]{2,1,0:T(8,128)(2,1)S(1)}, bf16[256,512]{1,0:T(8,128)(2,1)S(1)}, bf16[256,512]{1,0:T(8,128)(2,1)S(1)}) custom-call(bf16[256,2048]{1,0:T(8,128)(2,1)} %q.3, bf16[256,2048]{1,0:T(8,128)(2,1)} %k.3, bf16[256,2048]{1,0:T(8,128)(2,1)} %v.3, bf16[256,2048]{1,0:T(8,128)(2,1)} %g.3), custom_call_target="tpu_custom_call" | custom-call | tf_op jit(solution)/shard_map/deal_first/pallas_call | solution.py:93
  1.7 3.8 %collective-permute-start.2 = (bf16[2,256,512]{2,1,0:T(8,128)(2,1)S(1)}, bf16[2,256,512]{2,1,0:T(8,128)(2,1)S(1)}, u32[]{:S(2)}, u32[]{:S(2)}) collective-permute-start(bf16[2,256,512]{2,1,0:T(8,128)(2,1)S(1)} %get-tuple-element.15), channel_id=1, source_target_pairs={{0,4},{2,6},{4,0},{6,2},{8,12},{10,14},{12,8},{14,10},{16,20},{18,... | collective-permute-start | bytes 1572872 | tf_op jit(solution)/shard_map/ppermute | solution.py:200
  5.5 1.6 %deal_second.1 = (bf16[128,512]{1,0:T(8,128)(2,1)S(1)}, bf16[128,512]{1,0:T(8,128)(2,1)S(1)}, bf16[256,512]{1,0:T(8,128)(2,1)S(1)}, bf16[256,512]{1,0:T(8,128)(2,1)S(1)}, bf16[256,512]{1,0:T(8,128)(2,1)S(1)}) custom-call(bf16[256,2048]{1,0:T(8,128)(2,1)} %q.3, bf16[256,2048]{1,0:T(8,128)(2,1)} %k.3, bf16[256,2048]{1,0:T(8,128)(2,1)} %v.3, bf16[256,2048]{1,0:T(8,128)(2,1)} %g.3), custom_call_target="tpu_custom_call" | custom-call | tf_op jit(solution)/shard_map/deal_second/pallas_call | solution.py:93
  7.1 1.0 %collective-permute-start.6 = (bf16[128,512]{1,0:T(8,128)(2,1)S(1)}, bf16[128,512]{1,0:T(8,128)(2,1)S(1)}, u32[]{:S(2)}, u32[]{:S(2)}) collective-permute-start(bf16[128,512]{1,0:T(8,128)(2,1)S(1)} %get-tuple-element.19), channel_id=1, source_target_pairs={{0,2},{2,0},{4,6},{6,4},{8,10},{10,8},{12,14},{14,12},{16,18},{18,... | collective-permute-start | bytes 393224 | tf_op jit(solution)/shard_map/ppermute | solution.py:200
  8.2 0.1 collective-permute-start.7
  8.3 0.4 collective-permute-start
  8.7 0.5 collective-permute-done.6
  9.2 0.4 collective-permute-done.7
  9.6 0.1 pad_maximum_fusion.1
  9.6 1.9 %collective-permute-start.8 = (bf16[2,256,512]{2,1,0:T(8,128)(2,1)S(1)}, bf16[2,256,512]{2,1,0:T(8,128)(2,1)S(1)}, u32[]{:S(2)}, u32[]{:S(2)}) collective-permute-start(bf16[2,256,512]{2,1,0:T(8,128)(2,1)S(1)} %pad_maximum_fusion.1), channel_id=1, source_target_pairs={{0,4},{2,6},{4,0},{6,2},{8,12},{10,14},{12,8},{14,10},{16,20},{18,... | collective-permute-start | bytes 1572872 | tf_op jit(solution)/shard_map/ppermute | solution.py:200
  11.5 0.0 collective-permute-done
  11.5 0.1 pad_maximum_fusion.near
  11.6 1.3 %collective-permute-start.1 = (bf16[2,256,512]{2,1,0:T(8,128)(2,1)S(1)}, bf16[2,256,512]{2,1,0:T(8,128)(2,1)S(1)}, u32[]{:S(2)}, u32[]{:S(2)}) collective-permute-start(bf16[2,256,512]{2,1,0:T(8,128)(2,1)S(1)} %pad_maximum_fusion.near), channel_id=1, source_target_pairs={{0,8},{4,12},{8,16},{10,2},{12,20},{14,6},{16,24},{18,10},{20,28},... | collective-permute-start | bytes 1572872 | tf_op jit(solution)/shard_map/ppermute | solution.py:211
  12.9 1.4 %collective-permute-start.5 = (bf16[256,512]{1,0:T(8,128)(2,1)S(1)}, bf16[256,512]{1,0:T(8,128)(2,1)S(1)}, u32[]{:S(2)}, u32[]{:S(2)}) collective-permute-start(bf16[256,512]{1,0:T(8,128)(2,1)S(1)} %get-tuple-element.17), channel_id=1, source_target_pairs={{0,2},{2,0},{4,6},{6,4},{8,10},{10,8},{12,14},{14,12},{16,18},{18,... | collective-permute-start | bytes 786440 | tf_op jit(solution)/shard_map/ppermute | solution.py:200
  14.2 1.8 %collective-permute-done.2.far = bf16[2,256,512]{2,1,0:T(8,128)(2,1)S(1)} collective-permute-done((bf16[2,256,512]{2,1,0:T(8,128)(2,1)S(1)}, bf16[2,256,512]{2,1,0:T(8,128)(2,1)S(1)}, u32[]{:S(2)}, u32[]{:S(2)}) %collective-permute-start.2) | collective-permute-done | bytes 524320 | tf_op jit(solution)/shard_map/ppermute | solution.py:200
  16.1 1.3 %collective-permute-start.4 = (bf16[256,512]{1,0:T(8,128)(2,1)S(1)}, bf16[256,512]{1,0:T(8,128)(2,1)S(1)}, u32[]{:S(2)}, u32[]{:S(2)}) collective-permute-start(bf16[256,512]{1,0:T(8,128)(2,1)S(1)} %get-tuple-element.21), channel_id=1, source_target_pairs={{0,8},{4,12},{8,16},{10,2},{12,20},{14,6},{16,24},{18,10},{20,28},... | collective-permute-start | bytes 786440 | tf_op jit(solution)/shard_map/ppermute | solution.py:211
  17.4 6.1 %collective-permute-start.3 = (bf16[256,512]{1,0:T(8,128)(2,1)S(1)}, bf16[256,512]{1,0:T(8,128)(2,1)S(1)}, u32[]{:S(2)}, u32[]{:S(2)}) collective-permute-start(bf16[256,512]{1,0:T(8,128)(2,1)S(1)} %get-tuple-element.22), channel_id=1, source_target_pairs={{0,2},{2,0},{4,6},{6,4},{8,10},{10,8},{12,14},{14,12},{16,18},{18,... | collective-permute-start | bytes 786440 | tf_op jit(solution)/shard_map/ppermute | solution.py:200
  23.5 0.0 collective-permute-done.5.flip
  23.5 3.4 %collective-permute-start.9 = (bf16[256,512]{1,0:T(8,128)(2,1)S(1)}, bf16[256,512]{1,0:T(8,128)(2,1)S(1)}, u32[]{:S(2)}, u32[]{:S(2)}) collective-permute-start(bf16[256,512]{1,0:T(8,128)(2,1)S(1)} %get-tuple-element.22), channel_id=1, source_target_pairs={{2,8},{6,12},{8,2},{10,16},{12,6},{14,20},{16,10},{18,24},{20,14},... | collective-permute-start | bytes 786440 | tf_op jit(solution)/shard_map/ppermute | solution.py:211
  27.0 0.3 collective-permute-done.8.fixed
  27.3 0.0 collective-permute-done.1.beyond
  27.3 0.0 collective-permute-done.4.onto
  27.3 0.0 collective-permute-done.3.last
  27.3 1.4 %main.1.table_in = f32[256,1280]{1,0:T(8,128)S(1)} custom-call(bf16[2,256,512]{2,1,0:T(8,128)(2,1)S(1)} %collective-permute-done.1.beyond, bf16[2,256,512]{2,1,0:T(8,128)(2,1)S(1)} %pad_maximum_fusion.near, bf16[2,256,512]{2,1,0:T(8,128)(2,1)S(1)} %collective-permute-done.2.far, bf16[256,512]{1,0:T(8,128)(2,1)S(1)} %collective-permute-done.3.last, ...), custom_call_target="tpu_custom_call" | custom-call | flops 1006632960 | bytes 4194304 | tf_op jit(solution)/shard_map/main/pallas_call | solution.py:173
  28.8 2.4 %collective-permute-done.9.onto = bf16[256,512]{1,0:T(8,128)(2,1)S(1)} collective-permute-done((bf16[256,512]{1,0:T(8,128)(2,1)S(1)}, bf16[256,512]{1,0:T(8,128)(2,1)S(1)}, u32[]{:S(2)}, u32[]{:S(2)}) %collective-permute-start.9) | collective-permute-done | bytes 262176 | tf_op jit(solution)/shard_map/ppermute | solution.py:211
  31.2 0.7 %tail.1 = f32[8,128]{1,0:T(8,128)S(1)} custom-call(f32[256,1280]{1,0:T(8,128)S(1)} %main.1.table_in, bf16[256,512]{1,0:T(8,128)(2,1)S(1)} %collective-permute-done.9.onto, bf16[256,512]{1,0:T(8,128)(2,1)S(1)} %get-tuple-element.16.own, bf16[256,512]{1,0:T(8,128)(2,1)S(1)} %collective-permute-done.5.flip, bf16[2,256,512]{2,1,0:T(8,128)(2,1)S(1)} %collective-permute-done.8.fixed), custom_call_target="tpu_custom_call" | custom-call | tf_op jit(solution)/shard_map/tail/pallas_call | solution.py:184
  31.9 0.1 collective-permute-start.10
  32.0 1.2 %collective-permute-done.10 = f32[8,128]{1,0:T(8,128)S(1)} collective-permute-done((f32[8,128]{1,0:T(8,128)S(1)}, f32[8,128]{1,0:T(8,128)S(1)}, u32[]{:S(2)}, u32[]{:S(2)}) %collective-permute-start.10) | collective-permute-done | bytes 4128 | tf_op jit(solution)/shard_map/ppermute | solution.py:200
  33.2 26.4 %all_to_all.5 = f32[64,8,128]{2,1,0:T(8,128)S(1)} all-to-all(f32[64,8,128]{2,1,0:T(8,128)S(1)} %broadcast_in_dim.2), channel_id=1, replica_groups={{0,4,8,12,16,20,24,28,32,36,40,44,48,52,56,60,64,68,72,76,80,84,88,92,9..., dimensions={0} | all-to-all | bytes 524288 | tf_op jit(solution)/shard_map/all_to_all | solution.py:237
  59.7 0.6 %copy.7 = f32[1,2,8,128]{3,1,2,0:T(2,128)} copy(f32[1,2,8,128]{3,2,1,0:T(8,128)S(1)} %bitcast.18) | data formatting | bytes 16384
  (5 shorter events, 0.1 us)
Async XLA Ops:
  1.7 14.4 %collective-permute-start.2 = (bf16[2,256,512]{2,1,0:T(8,128)(2,1)S(1)}, bf16[2,256,512]{2,1,0:T(8,128)(2,1)S(1)}, u32[]{:S(2)}, u32[]{:S(2)}) collective-permute-start(bf16[2,256,512]{2,1,0:T(8,128)(2,1)S(1)} %get-tuple-element.15), channel_id=1, source_target_pairs={{0,4},{2,6},{4,0},{6,2},{8,12},{10,14},{12,8},{14,10},{16,20},{18,... | collective-permute-start | bytes 1572872 | tf_op jit(solution)/shard_map/ppermute | solution.py:200
  7.1 2.0 %collective-permute-start.6 = (bf16[128,512]{1,0:T(8,128)(2,1)S(1)}, bf16[128,512]{1,0:T(8,128)(2,1)S(1)}, u32[]{:S(2)}, u32[]{:S(2)}) collective-permute-start(bf16[128,512]{1,0:T(8,128)(2,1)S(1)} %get-tuple-element.19), channel_id=1, source_target_pairs={{0,2},{2,0},{4,6},{6,4},{8,10},{10,8},{12,14},{14,12},{16,18},{18,... | collective-permute-start | bytes 393224 | tf_op jit(solution)/shard_map/ppermute | solution.py:200
  8.2 1.3 %collective-permute-start.7 = (bf16[128,512]{1,0:T(8,128)(2,1)S(1)}, bf16[128,512]{1,0:T(8,128)(2,1)S(1)}, u32[]{:S(2)}, u32[]{:S(2)}) collective-permute-start(bf16[128,512]{1,0:T(8,128)(2,1)S(1)} %get-tuple-element.20), channel_id=1, source_target_pairs={{0,2},{2,0},{4,6},{6,4},{8,10},{10,8},{12,14},{14,12},{16,18},{18,... | collective-permute-start | bytes 393224 | tf_op jit(solution)/shard_map/ppermute | solution.py:200
  8.3 3.2 %collective-permute-start = (bf16[256,512]{1,0:T(8,128)(2,1)S(1)}, bf16[256,512]{1,0:T(8,128)(2,1)S(1)}, u32[]{:S(2)}, u32[]{:S(2)}) collective-permute-start(bf16[256,512]{1,0:T(8,128)(2,1)S(1)} %get-tuple-element.14), channel_id=1, source_target_pairs={{0,2},{2,0},{4,6},{6,4},{8,10},{10,8},{12,14},{14,12},{16,18},{18,... | collective-permute-start | bytes 786440 | tf_op jit(solution)/shard_map/ppermute | solution.py:200
  9.6 17.7 %collective-permute-start.8 = (bf16[2,256,512]{2,1,0:T(8,128)(2,1)S(1)}, bf16[2,256,512]{2,1,0:T(8,128)(2,1)S(1)}, u32[]{:S(2)}, u32[]{:S(2)}) collective-permute-start(bf16[2,256,512]{2,1,0:T(8,128)(2,1)S(1)} %pad_maximum_fusion.1), channel_id=1, source_target_pairs={{0,4},{2,6},{4,0},{6,2},{8,12},{10,14},{12,8},{14,10},{16,20},{18,... | collective-permute-start | bytes 1572872 | tf_op jit(solution)/shard_map/ppermute | solution.py:200
  11.6 15.8 %collective-permute-start.1 = (bf16[2,256,512]{2,1,0:T(8,128)(2,1)S(1)}, bf16[2,256,512]{2,1,0:T(8,128)(2,1)S(1)}, u32[]{:S(2)}, u32[]{:S(2)}) collective-permute-start(bf16[2,256,512]{2,1,0:T(8,128)(2,1)S(1)} %pad_maximum_fusion.near), channel_id=1, source_target_pairs={{0,8},{4,12},{8,16},{10,2},{12,20},{14,6},{16,24},{18,10},{20,28},... | collective-permute-start | bytes 1572872 | tf_op jit(solution)/shard_map/ppermute | solution.py:211
  12.9 10.7 %collective-permute-start.5 = (bf16[256,512]{1,0:T(8,128)(2,1)S(1)}, bf16[256,512]{1,0:T(8,128)(2,1)S(1)}, u32[]{:S(2)}, u32[]{:S(2)}) collective-permute-start(bf16[256,512]{1,0:T(8,128)(2,1)S(1)} %get-tuple-element.17), channel_id=1, source_target_pairs={{0,2},{2,0},{4,6},{6,4},{8,10},{10,8},{12,14},{14,12},{16,18},{18,... | collective-permute-start | bytes 786440 | tf_op jit(solution)/shard_map/ppermute | solution.py:200
  16.1 11.2 %collective-permute-start.4 = (bf16[256,512]{1,0:T(8,128)(2,1)S(1)}, bf16[256,512]{1,0:T(8,128)(2,1)S(1)}, u32[]{:S(2)}, u32[]{:S(2)}) collective-permute-start(bf16[256,512]{1,0:T(8,128)(2,1)S(1)} %get-tuple-element.21), channel_id=1, source_target_pairs={{0,8},{4,12},{8,16},{10,2},{12,20},{14,6},{16,24},{18,10},{20,28},... | collective-permute-start | bytes 786440 | tf_op jit(solution)/shard_map/ppermute | solution.py:211
  17.4 9.9 %collective-permute-start.3 = (bf16[256,512]{1,0:T(8,128)(2,1)S(1)}, bf16[256,512]{1,0:T(8,128)(2,1)S(1)}, u32[]{:S(2)}, u32[]{:S(2)}) collective-permute-start(bf16[256,512]{1,0:T(8,128)(2,1)S(1)} %get-tuple-element.22), channel_id=1, source_target_pairs={{0,2},{2,0},{4,6},{6,4},{8,10},{10,8},{12,14},{14,12},{16,18},{18,... | collective-permute-start | bytes 786440 | tf_op jit(solution)/shard_map/ppermute | solution.py:200
  23.5 7.7 %collective-permute-start.9 = (bf16[256,512]{1,0:T(8,128)(2,1)S(1)}, bf16[256,512]{1,0:T(8,128)(2,1)S(1)}, u32[]{:S(2)}, u32[]{:S(2)}) collective-permute-start(bf16[256,512]{1,0:T(8,128)(2,1)S(1)} %get-tuple-element.22), channel_id=1, source_target_pairs={{2,8},{6,12},{8,2},{10,16},{12,6},{14,20},{16,10},{18,24},{20,14},... | collective-permute-start | bytes 786440 | tf_op jit(solution)/shard_map/ppermute | solution.py:211
  31.9 1.3 %collective-permute-start.10 = (f32[8,128]{1,0:T(8,128)S(1)}, f32[8,128]{1,0:T(8,128)S(1)}, u32[]{:S(2)}, u32[]{:S(2)}) collective-permute-start(f32[8,128]{1,0:T(8,128)S(1)} %tail.1), channel_id=1, source_target_pairs={{0,2},{2,0},{4,6},{6,4},{8,10},{10,8},{12,14},{14,12},{16,18},{18,... | collective-permute-start | bytes 12296 | tf_op jit(solution)/shard_map/ppermute | solution.py:200

commit v5 on v4

--- a/solution.py
+++ b/solution.py
@@ -12,7 +12,7 @@
 LAGS = 1024
 MIB = 1024 * 1024
 DEAL_MIB = 56
-MAIN_COST = 15 * 2 * BLK * BLK * CH
+MAIN_COST = 0
 NT = (((1,), (1,)), ((), ()))
 BF16 = jnp.bfloat16
 
@@ -56,22 +56,29 @@
     return (place // 2) % 2, place % 2
 
 
-def deal_first(q, k, v, g, far, give, own, slots, sems):
+def deal_first(q, k, v, g, far, slots, sems):
+    yh, core = position()
+    wanted = (
+        (True, True, columns(1 - yh, core)),
+        (False, True, columns(1 - yh, 1 - core)),
+    )
+    get = fetch(core, slots, sems, (q, k, v, g), wanted)
+    far[0] = get(0)
+    far[1] = get(1)
+
+
+def deal_moving(q, k, v, g, give, own, slots, sems):
     yh, core = position()
     wanted = (
         (False, True, columns(yh, 1 - core)),
-        (True, True, columns(1 - yh, core)),
-        (False, True, columns(1 - yh, 1 - core)),
         (True, True, columns(yh, core)),
     )
     get = fetch(core, slots, sems, (q, k, v, g), wanted)
     give[...] = get(0)
-    far[0] = get(1)
-    far[1] = get(2)
-    own[...] = get(3)
-
-
-def deal_second(q, k, v, g, top, low, give_own, keep, own, slots, sems):
+    own[...] = get(1)
+
+
+def deal_fixed(q, k, v, g, top, low, give_own, keep, stay, slots, sems):
     yh, core = position()
     wanted = (
         (False, False, columns(1 - yh, 1 - core)),
@@ -80,12 +87,12 @@
         (True, False, columns(yh, core)),
     )
     get = fetch(core, slots, sems, (q, k, v, g), wanted)
-    give = get(0)
-    top[...] = give[: BLK // 2]
-    low[...] = give[BLK // 2 :]
+    halves = get(0)
+    top[...] = halves[: BLK // 2]
+    low[...] = halves[BLK // 2 :]
     give_own[...] = get(1)
     keep[...] = get(2)
-    own[...] = get(3)
+    stay[...] = get(3)
 
 
 def deal(body, name, shapes, arrays):
@@ -131,34 +138,61 @@
     return pl.ds(d * BLK, BLK)
 
 
-def main_kernel(beyond, near, far, last, onto, own, flip, fixed, table):
-    def body(home):
-        core = home & 1
-        here = {home: near.at[0], home ^ 1: near.at[1], home ^ 2: far.at[0], home ^ 3: last}
-        there = {home: beyond.at[0], home ^ 1: beyond.at[1], home ^ 2: onto}
-        stay = {home: own, home ^ 1: flip, home ^ 2: fixed.at[0], home ^ 3: fixed.at[1]}
-        for d in range(5):
-            total = None
-            for block, ref in stay.items():
-                other = block - d if core == 0 else block + d
-                source = here if 0 <= other < 4 else there
-                if (other & 3) in source:
-                    dot = block_dot(core, source[other & 3][...], ref[...])
-                    total = dot if total is None else total + dot
-            table[:, columns_of(d)] = total
-
-    by_home(body)
-
-
-def tail_kernel(table_in, onto, own, flip, fixed, out, table):
+def early_products(home, table, stay, near, beyond, far, before=None):
+    core = home & 1
+    here = {home: near.at[0], home ^ 1: near.at[1], home ^ 2: far.at[0]}
+    there = {home: beyond.at[0], home ^ 1: beyond.at[1]}
+    for d in range(5):
+        total = None if before is None else before[:, columns_of(d)]
+        for block, ref in stay.items():
+            other = block - d if core == 0 else block + d
+            source = here if 0 <= other < 4 else there
+            if (other & 3) in source:
+                dot = block_dot(core, source[other & 3][...], ref[...])
+                total = dot if total is None else total + dot
+        if total is None:
+            total = jnp.zeros((BLK, BLK), jnp.float32)
+        table[:, columns_of(d)] = total
+
+
+def early_kernel(own, flip, beyond, near, far, table):
+    by_home(
+        lambda home: early_products(
+            home, table, {home: own, home ^ 1: flip}, near, beyond, far
+        )
+    )
+
+
+def main_kernel(before, fixed, beyond, near, far, table):
+    by_home(
+        lambda home: early_products(
+            home, table, {home ^ 2: fixed.at[0], home ^ 3: fixed.at[1]},
+            near, beyond, far, before,
+        )
+    )
+
+
+def tail_kernel(
+    table_in, on_far, on_near, top, low, own, flip, fixed, out, last, table
+):
+    last[: BLK // 2] = top[...]
+    last[BLK // 2 :] = low[...]
+
     def body(home):
         core = home & 1
         stay = {home: own, home ^ 1: flip, home ^ 2: fixed.at[0], home ^ 3: fixed.at[1]}
         for d in range(5):
-            block = (home ^ 3) + (d - 4 if core == 0 else 4 - d)
             total = table_in[:, columns_of(d)]
-            if 0 <= block < 4:
-                total = total + block_dot(core, onto[...], stay[block][...])
+            for block, ref in stay.items():
+                other = block - d if core == 0 else block + d
+                inside = 0 <= other < 4
+                moving = None
+                if other & 3 == home ^ 3:
+                    moving = last if inside else on_far
+                elif other & 3 == home ^ 2 and not inside:
+                    moving = on_near
+                if moving is not None:
+                    total = total + block_dot(core, moving[...], ref[...])
             table[:, columns_of(d)] = total
 
     by_home(body)
@@ -167,29 +201,37 @@
         out[i : i + 1, :] = sums[:, i * 128 : (i + 1) * 128]
 
 
-def correlate(moving, onto_far, *fixed):
+def correlate(moving, late, own, flip, fixed):
     vmem = pl.BlockSpec(memory_space=pltpu.VMEM)
     params = pltpu.CompilerParams(vmem_limit_bytes=40 * MIB)
-    table = pl.pallas_call(
-        main_kernel,
-        in_specs=[vmem] * (len(moving) + len(fixed)),
-        out_specs=vmem,
-        out_shape=jax.ShapeDtypeStruct((BLK, 5 * BLK), jnp.float32),
-        compiler_params=params,
-        cost_estimate=pl.CostEstimate(
-            flops=MAIN_COST, bytes_accessed=4 * MIB, transcendentals=0
-        ),
-        name="main",
-    )(*moving, *fixed)
+
+    def table_call(body, name, *operands):
+        return pl.pallas_call(
+            body,
+            in_specs=[vmem] * len(operands),
+            out_specs=vmem,
+            out_shape=jax.ShapeDtypeStruct((BLK, 5 * BLK), jnp.float32),
+            compiler_params=params,
+            cost_estimate=pl.CostEstimate(
+                flops=MAIN_COST, bytes_accessed=4 * MIB, transcendentals=0
+            ),
+            name=name,
+        )(*operands)
+
+    table = table_call(early_kernel, "early", own, flip, *moving)
+    table = table_call(main_kernel, "main", table, fixed, *moving)
     return pl.pallas_call(
         tail_kernel,
-        in_specs=[vmem] * (2 + len(fixed)),
+        in_specs=[vmem] * (4 + len(late)),
         out_specs=vmem,
         out_shape=jax.ShapeDtypeStruct((8, 128), jnp.float32),
-        scratch_shapes=[pltpu.VMEM((BLK, 5 * BLK), jnp.float32)],
+        scratch_shapes=[
+            pltpu.VMEM((BLK, CH), BF16),
+            pltpu.VMEM((BLK, 5 * BLK), jnp.float32),
+        ],
         compiler_params=params,
         name="tail",
-    )(table, onto_far, *fixed)
+    )(table, *late, own, flip, fixed)
 
 
 def swap(value, quads, far, flip):
@@ -214,23 +256,22 @@
 def on_device(queries, keys, values, grad_out):
     quads = lax.axis_size("ctx") // 4
     arrays = (queries, keys, values, grad_out)
-    one, two = (BLK, CH), (2, BLK, CH)
-    far_moving, give, own_moving = deal(deal_first, "deal_first", [two, one, one], arrays)
-    flip_moving = swap(give, quads, 0, 1)
-    far_moving = swap(far_moving, quads, 1, 0)
-    near_moving = jnp.stack([own_moving, flip_moving])
+    one, two, half = (BLK, CH), (2, BLK, CH), (BLK // 2, CH)
+    far_moving = swap(deal(deal_first, "deal_first", [two], arrays)[0], quads, 1, 0)
+    give, own_moving = deal(deal_moving, "deal_moving", [one, one], arrays)
+    top, low, give_own, keep, own_fixed = deal(
+        deal_fixed, "deal_fixed", [half, half, one, one, one], arrays
+    )
+    near_moving = jnp.stack([own_moving, swap(give, quads, 0, 1)])
     beyond = onward(near_moving, quads)
-    top, low, give_own, keep, own_fixed = deal(
-        deal_second, "deal_second", [(BLK // 2, CH)] * 2 + [one] * 3, arrays
-    )
     got = jnp.concatenate([swap(top, quads, 0, 1), swap(low, quads, 0, 1)])
     far_fixed = swap(jnp.stack([keep, got]), quads, 1, 0)
     flip_fixed = swap(give_own, quads, 0, 1)
-    last = swap(far_moving[1], quads, 0, 1)
-    onto_near = onward(far_moving[0], quads)
-    onto_far = onward(far_moving[1], quads, 1)
-    moving = (beyond, near_moving, far_moving, last, onto_near)
-    part = correlate(moving, onto_far, own_fixed, flip_fixed, far_fixed)
+    last = [swap(far_moving[1, i : i + BLK // 2], quads, 0, 1) for i in (0, BLK // 2)]
+    on_near = onward(far_moving[0], quads)
+    on_far = onward(far_moving[1], quads, 1)
+    moving, late = (beyond, near_moving, far_moving), (on_far, on_near, *last)
+    part = correlate(moving, late, own_fixed, flip_fixed, far_fixed)
     part = part + swap(part, quads, 0, 1)
     groups = [[q * 4 + y * 2 + c for q in range(quads) for y in range(2)] for c in range(2)]
     spread = jnp.broadcast_to(part[None], (2 * quads, 8, 128))

time: 61.1 us -> 60.4 us (0.989)
  starting transfers between devices: 20.9 us -> 18.3 us
  Pallas kernels: 5.46 us -> 6.6 us
    ppermute x8 -> x9, starting transfers between devices: 14.9 us -> 9.54 us  [swap(): return lax.ppermute(value, 'ctx', pairs)]
    ppermute x3, starting transfers between devices: 6.02 us -> 8.79 us  [onward(): return lax.ppermute(value, 'ctx', pairs)]
    pallas_call x2 -> x3, Pallas kernels: 3.3 us -> 4.29 us  [deal(): pl.pallas_call(body, in_specs=[pl.BlockSpec(memory_space=pl.ANY)] * 4, ou...]
    ppermute x8 -> x9, waiting for transfers between devices: 4.17 us -> 5.03 us  [swap(): return lax.ppermute(value, 'ctx', pairs)]
    ppermute x3, waiting for transfers between devices: 2.44 us -> 1.67 us  [onward(): return lax.ppermute(value, 'ctx', pairs)]
    pallas_call x2 -> x3, Pallas kernels: 2.16 us -> 2.31 us  [the longest x2 1.35 us: table_call(): pl.pallas_call(body, in_specs=[vmem] * len(operands), out_specs=vmem, out...]
  transfers between devices with their start and end apart: 11 -> 12, of which waited for: 6 -> 6; matrix products, arithmetic and copies ran while one was open for 0% -> 0% of each run, Pallas kernels for 5% -> 7%
where the time goes in v5:
time: 60.4 us; the launch traced here: 59.6 us
  blocking collectives  27 us (45%)
  starting transfers between devices  18.3 us (30%)
  waiting for transfers between devices  6.7 us (11%)
  Pallas kernels  6.6 us (11%)
  local copies, waits for them, and re-layouts  0.68 us (1%)
    all_to_all x1, blocking collectives, on_device(): gathered = lax.all_to_all(spread, 'ctx', 0, 0, axis_index_groups=groups)  27 us
    ppermute x9, starting transfers between devices, swap(): return lax.ppermute(value, 'ctx', pairs)  9.54 us
    ppermute x3, starting transfers between devices, onward(): return lax.ppermute(value, 'ctx', pairs)  8.79 us
    ppermute x9, waiting for transfers between devices, swap(): return lax.ppermute(value, 'ctx', pairs)  5.03 us
    pallas_call x3, Pallas kernels, deal(): pl.pallas_call(body, in_specs=[pl.BlockSpec(memory_space=pl.ANY)] * 4, ou...  4.29 us
    ppermute x3, waiting for transfers between devices, onward(): return lax.ppermute(value, 'ctx', pairs)  1.67 us
    pallas_call x2, Pallas kernels, table_call(): pl.pallas_call(body, in_specs=[vmem] * len(operands), out_specs=vmem, out...  1.35 us
  transfers between devices with their start and end apart: 12, of which 6 were waited for; matrix products, arithmetic and copies ran while one was open for 0% of the time, Pallas kernels for 7%

profile of v5, /device:TPU:1, one launch (start us, length us, event | category | flops | bytes accessed | tf_op | source)
XLA Modules:
  0.0 59.6 jit_solution(11155285899463240142)
XLA Ops:
  0.0 1.3 %deal_first.1 = bf16[2,256,512]{2,1,0:T(8,128)(2,1)S(1)} custom-call(bf16[256,2048]{1,0:T(8,128)(2,1)} %q.5, bf16[256,2048]{1,0:T(8,128)(2,1)} %k.5, bf16[256,2048]{1,0:T(8,128)(2,1)} %v.5, bf16[256,2048]{1,0:T(8,128)(2,1)} %g.5), custom_call_target="tpu_custom_call" | custom-call | tf_op jit(solution)/shard_map/deal_first/pallas_call | solution.py:100
  1.3 3.8 %collective-permute-start.3 = (bf16[2,256,512]{2,1,0:T(8,128)(2,1)S(1)}, bf16[2,256,512]{2,1,0:T(8,128)(2,1)S(1)}, u32[]{:S(2)}, u32[]{:S(2)}) collective-permute-start(bf16[2,256,512]{2,1,0:T(8,128)(2,1)S(1)} %deal_first.1), channel_id=1, source_target_pairs={{0,4},{2,6},{4,0},{6,2},{8,12},{10,14},{12,8},{14,10},{16,20},{18,... | collective-permute-start | bytes 1572872 | tf_op jit(solution)/shard_map/ppermute | solution.py:242
  5.2 1.3 %deal_moving.1 = (bf16[256,512]{1,0:T(8,128)(2,1)S(1)}, bf16[256,512]{1,0:T(8,128)(2,1)S(1)}) custom-call(bf16[256,2048]{1,0:T(8,128)(2,1)} %q.5, bf16[256,2048]{1,0:T(8,128)(2,1)} %k.5, bf16[256,2048]{1,0:T(8,128)(2,1)} %v.5, bf16[256,2048]{1,0:T(8,128)(2,1)} %g.5), custom_call_target="tpu_custom_call" | custom-call | tf_op jit(solution)/shard_map/deal_moving/pallas_call | solution.py:100
  6.5 1.0 %collective-permute-start.1 = (bf16[256,512]{1,0:T(8,128)(2,1)S(1)}, bf16[256,512]{1,0:T(8,128)(2,1)S(1)}, u32[]{:S(2)}, u32[]{:S(2)}) collective-permute-start(bf16[256,512]{1,0:T(8,128)(2,1)S(1)} %get-tuple-element.15), channel_id=1, source_target_pairs={{0,2},{2,0},{4,6},{6,4},{8,10},{10,8},{12,14},{14,12},{16,18},{18,... | collective-permute-start | bytes 786440 | tf_op jit(solution)/shard_map/ppermute | solution.py:242
  7.5 1.6 %deal_fixed.1 = (bf16[128,512]{1,0:T(8,128)(2,1)S(1)}, bf16[128,512]{1,0:T(8,128)(2,1)S(1)}, bf16[256,512]{1,0:T(8,128)(2,1)S(1)}, bf16[256,512]{1,0:T(8,128)(2,1)S(1)}, bf16[256,512]{1,0:T(8,128)(2,1)S(1)}) custom-call(bf16[256,2048]{1,0:T(8,128)(2,1)} %q.5, bf16[256,2048]{1,0:T(8,128)(2,1)} %k.5, bf16[256,2048]{1,0:T(8,128)(2,1)} %v.5, bf16[256,2048]{1,0:T(8,128)(2,1)} %g.5), custom_call_target="tpu_custom_call" | custom-call | tf_op jit(solution)/shard_map/deal_fixed/pallas_call | solution.py:100
  9.2 0.1 collective-permute-start.4
  9.3 0.5 collective-permute-start.5
  9.8 0.1 collective-permute-start
  9.9 0.7 %collective-permute-done.4 = bf16[128,512]{1,0:T(8,128)(2,1)S(1)} collective-permute-done((bf16[128,512]{1,0:T(8,128)(2,1)S(1)}, bf16[128,512]{1,0:T(8,128)(2,1)S(1)}, u32[]{:S(2)}, u32[]{:S(2)}) %collective-permute-start.4) | collective-permute-done | bytes 131104 | tf_op jit(solution)/shard_map/ppermute | solution.py:242
  10.6 0.2 collective-permute-done.5
  10.8 0.0 collective-permute-done.1
  10.8 0.1 pad_maximum_fusion.near
  10.9 1.3 %collective-permute-start.2 = (bf16[2,256,512]{2,1,0:T(8,128)(2,1)S(1)}, bf16[2,256,512]{2,1,0:T(8,128)(2,1)S(1)}, u32[]{:S(2)}, u32[]{:S(2)}) collective-permute-start(bf16[2,256,512]{2,1,0:T(8,128)(2,1)S(1)} %pad_maximum_fusion.near), channel_id=1, source_target_pairs={{0,8},{4,12},{8,16},{10,2},{12,20},{14,6},{16,24},{18,10},{20,28},... | collective-permute-start | bytes 1572872 | tf_op jit(solution)/shard_map/ppermute | solution.py:253
  12.2 0.1 pad_maximum_fusion.1
  12.3 1.9 %collective-permute-start.6 = (bf16[2,256,512]{2,1,0:T(8,128)(2,1)S(1)}, bf16[2,256,512]{2,1,0:T(8,128)(2,1)S(1)}, u32[]{:S(2)}, u32[]{:S(2)}) collective-permute-start(bf16[2,256,512]{2,1,0:T(8,128)(2,1)S(1)} %pad_maximum_fusion.1), channel_id=1, source_target_pairs={{0,4},{2,6},{4,0},{6,2},{8,12},{10,14},{12,8},{14,10},{16,20},{18,... | collective-permute-start | bytes 1572872 | tf_op jit(solution)/shard_map/ppermute | solution.py:242
  14.1 1.6 %collective-permute-done.3.far = bf16[2,256,512]{2,1,0:T(8,128)(2,1)S(1)} collective-permute-done((bf16[2,256,512]{2,1,0:T(8,128)(2,1)S(1)}, bf16[2,256,512]{2,1,0:T(8,128)(2,1)S(1)}, u32[]{:S(2)}, u32[]{:S(2)}) %collective-permute-start.3) | collective-permute-done | bytes 524320 | tf_op jit(solution)/shard_map/ppermute | solution.py:242
  15.8 6.2 %collective-permute-start.7 = (bf16[256,512]{1,0:T(8,128)(2,1)S(1)}, bf16[256,512]{1,0:T(8,128)(2,1)S(1)}, u32[]{:S(2)}, u32[]{:S(2)}) collective-permute-start(bf16[256,512]{1,0:T(8,128)(2,1)S(1)} %get-tuple-element.22), channel_id=1, source_target_pairs={{2,8},{6,12},{8,2},{10,16},{12,6},{14,20},{16,10},{18,24},{20,14},... | collective-permute-start | bytes 786440 | tf_op jit(solution)/shard_map/ppermute | solution.py:253
  22.0 1.3 %collective-permute-start.8 = (bf16[256,512]{1,0:T(8,128)(2,1)S(1)}, bf16[256,512]{1,0:T(8,128)(2,1)S(1)}, u32[]{:S(2)}, u32[]{:S(2)}) collective-permute-start(bf16[256,512]{1,0:T(8,128)(2,1)S(1)} %get-tuple-element.21), channel_id=1, source_target_pairs={{0,8},{4,12},{8,16},{10,2},{12,20},{14,6},{16,24},{18,10},{20,28},... | collective-permute-start | bytes 786440 | tf_op jit(solution)/shard_map/ppermute | solution.py:253
  23.3 0.0 collective-permute-done.flip
  23.3 1.1 %collective-permute-start.10 = (bf16[128,512]{1,0:T(8,128)(2,1)S(1)}, bf16[128,512]{1,0:T(8,128)(2,1)S(1)}, u32[]{:S(2)}, u32[]{:S(2)}) collective-permute-start(bf16[128,512]{1,0:T(8,128)(2,1)S(1)} %get-tuple-element.19), channel_id=1, source_target_pairs={{0,2},{2,0},{4,6},{6,4},{8,10},{10,8},{12,14},{14,12},{16,18},{18,... | collective-permute-start | bytes 393224 | tf_op jit(solution)/shard_map/ppermute | solution.py:242
  24.5 0.0 collective-permute-done.2.beyond
  24.5 0.1 collective-permute-start.9
  24.6 0.7 %early.1.before = f32[256,1280]{1,0:T(8,128)S(1)} custom-call(bf16[256,512]{1,0:T(8,128)(2,1)S(1)} %get-tuple-element.12.own, bf16[256,512]{1,0:T(8,128)(2,1)S(1)} %collective-permute-done.flip, bf16[2,256,512]{2,1,0:T(8,128)(2,1)S(1)} %collective-permute-done.2.beyond, bf16[2,256,512]{2,1,0:T(8,128)(2,1)S(1)} %pad_maximum_fusion.near, ...), custom_call_target="tpu_custom_call" | custom-call | bytes 4194304 | tf_op jit(solution)/shard_map/early/pallas_call | solution.py:209
  25.3 1.7 %collective-permute-done.6.fixed = bf16[2,256,512]{2,1,0:T(8,128)(2,1)S(1)} collective-permute-done((bf16[2,256,512]{2,1,0:T(8,128)(2,1)S(1)}, bf16[2,256,512]{2,1,0:T(8,128)(2,1)S(1)}, u32[]{:S(2)}, u32[]{:S(2)}) %collective-permute-start.6) | collective-permute-done | bytes 524320 | tf_op jit(solution)/shard_map/ppermute | solution.py:242
  27.0 0.6 %main.1.table_in = f32[256,1280]{1,0:T(8,128)S(1)} custom-call(f32[256,1280]{1,0:T(8,128)S(1)} %early.1.before, bf16[2,256,512]{2,1,0:T(8,128)(2,1)S(1)} %collective-permute-done.6.fixed, bf16[2,256,512]{2,1,0:T(8,128)(2,1)S(1)} %collective-permute-done.2.beyond, bf16[2,256,512]{2,1,0:T(8,128)(2,1)S(1)} %pad_maximum_fusion.near, ...), custom_call_target="tpu_custom_call" | custom-call | bytes 4194304 | tf_op jit(solution)/shard_map/main/pallas_call | solution.py:209
  27.6 0.0 collective-permute-done.10.low
  27.6 0.0 collective-permute-done.9.top
  27.6 0.0 collective-permute-done.7.on_far
  27.6 1.7 %collective-permute-done.8.on_near = bf16[256,512]{1,0:T(8,128)(2,1)S(1)} collective-permute-done((bf16[256,512]{1,0:T(8,128)(2,1)S(1)}, bf16[256,512]{1,0:T(8,128)(2,1)S(1)}, u32[]{:S(2)}, u32[]{:S(2)}) %collective-permute-start.8) | collective-permute-done | bytes 262176 | tf_op jit(solution)/shard_map/ppermute | solution.py:253
  29.3 1.0 %tail.1 = f32[8,128]{1,0:T(8,128)S(1)} custom-call(f32[256,1280]{1,0:T(8,128)S(1)} %main.1.table_in, bf16[256,512]{1,0:T(8,128)(2,1)S(1)} %collective-permute-done.7.on_far, bf16[256,512]{1,0:T(8,128)(2,1)S(1)} %collective-permute-done.8.on_near, bf16[128,512]{1,0:T(8,128)(2,1)S(1)} %collective-permute-done.9.top, ...), custom_call_target="tpu_custom_call" | custom-call | tf_op jit(solution)/shard_map/tail/pallas_call | solution.py:223
  30.3 0.9 %collective-permute-start.11 = (f32[8,128]{1,0:T(8,128)S(1)}, f32[8,128]{1,0:T(8,128)S(1)}, u32[]{:S(2)}, u32[]{:S(2)}) collective-permute-start(f32[8,128]{1,0:T(8,128)S(1)} %tail.1), channel_id=1, source_target_pairs={{0,2},{2,0},{4,6},{6,4},{8,10},{10,8},{12,14},{14,12},{16,18},{18,... | collective-permute-start | bytes 12296 | tf_op jit(solution)/shard_map/ppermute | solution.py:242
  31.1 0.8 %collective-permute-done.11 = f32[8,128]{1,0:T(8,128)S(1)} collective-permute-done((f32[8,128]{1,0:T(8,128)S(1)}, f32[8,128]{1,0:T(8,128)S(1)}, u32[]{:S(2)}, u32[]{:S(2)}) %collective-permute-start.11) | collective-permute-done | bytes 4128 | tf_op jit(solution)/shard_map/ppermute | solution.py:242
  32.0 27.0 %all_to_all.5 = f32[64,8,128]{2,1,0:T(8,128)S(1)} all-to-all(f32[64,8,128]{2,1,0:T(8,128)S(1)} %broadcast_in_dim.2), channel_id=1, replica_groups={{0,4,8,12,16,20,24,28,32,36,40,44,48,52,56,60,64,68,72,76,80,84,88,92,9..., dimensions={0} | all-to-all | bytes 524288 | tf_op jit(solution)/shard_map/all_to_all | solution.py:278
  59.0 0.6 %copy.7 = f32[1,2,8,128]{3,1,2,0:T(2,128)} copy(f32[1,2,8,128]{3,2,1,0:T(8,128)S(1)} %bitcast.22) | data formatting | bytes 16384
  (6 shorter events, 0.1 us)
Async XLA Ops:
  1.3 14.4 %collective-permute-start.3 = (bf16[2,256,512]{2,1,0:T(8,128)(2,1)S(1)}, bf16[2,256,512]{2,1,0:T(8,128)(2,1)S(1)}, u32[]{:S(2)}, u32[]{:S(2)}) collective-permute-start(bf16[2,256,512]{2,1,0:T(8,128)(2,1)S(1)} %deal_first.1), channel_id=1, source_target_pairs={{0,4},{2,6},{4,0},{6,2},{8,12},{10,14},{12,8},{14,10},{16,20},{18,... | collective-permute-start | bytes 1572872 | tf_op jit(solution)/shard_map/ppermute | solution.py:242
  6.5 4.3 %collective-permute-start.1 = (bf16[256,512]{1,0:T(8,128)(2,1)S(1)}, bf16[256,512]{1,0:T(8,128)(2,1)S(1)}, u32[]{:S(2)}, u32[]{:S(2)}) collective-permute-start(bf16[256,512]{1,0:T(8,128)(2,1)S(1)} %get-tuple-element.15), channel_id=1, source_target_pairs={{0,2},{2,0},{4,6},{6,4},{8,10},{10,8},{12,14},{14,12},{16,18},{18,... | collective-permute-start | bytes 786440 | tf_op jit(solution)/shard_map/ppermute | solution.py:242
  9.2 1.4 %collective-permute-start.4 = (bf16[128,512]{1,0:T(8,128)(2,1)S(1)}, bf16[128,512]{1,0:T(8,128)(2,1)S(1)}, u32[]{:S(2)}, u32[]{:S(2)}) collective-permute-start(bf16[128,512]{1,0:T(8,128)(2,1)S(1)} %get-tuple-element.17), channel_id=1, source_target_pairs={{0,2},{2,0},{4,6},{6,4},{8,10},{10,8},{12,14},{14,12},{16,18},{18,... | collective-permute-start | bytes 393224 | tf_op jit(solution)/shard_map/ppermute | solution.py:242
  9.3 1.5 %collective-permute-start.5 = (bf16[128,512]{1,0:T(8,128)(2,1)S(1)}, bf16[128,512]{1,0:T(8,128)(2,1)S(1)}, u32[]{:S(2)}, u32[]{:S(2)}) collective-permute-start(bf16[128,512]{1,0:T(8,128)(2,1)S(1)} %get-tuple-element.18), channel_id=1, source_target_pairs={{0,2},{2,0},{4,6},{6,4},{8,10},{10,8},{12,14},{14,12},{16,18},{18,... | collective-permute-start | bytes 393224 | tf_op jit(solution)/shard_map/ppermute | solution.py:242
  9.8 13.6 %collective-permute-start = (bf16[256,512]{1,0:T(8,128)(2,1)S(1)}, bf16[256,512]{1,0:T(8,128)(2,1)S(1)}, u32[]{:S(2)}, u32[]{:S(2)}) collective-permute-start(bf16[256,512]{1,0:T(8,128)(2,1)S(1)} %get-tuple-element.13), channel_id=1, source_target_pairs={{0,2},{2,0},{4,6},{6,4},{8,10},{10,8},{12,14},{14,12},{16,18},{18,... | collective-permute-start | bytes 786440 | tf_op jit(solution)/shard_map/ppermute | solution.py:242
  10.9 13.6 %collective-permute-start.2 = (bf16[2,256,512]{2,1,0:T(8,128)(2,1)S(1)}, bf16[2,256,512]{2,1,0:T(8,128)(2,1)S(1)}, u32[]{:S(2)}, u32[]{:S(2)}) collective-permute-start(bf16[2,256,512]{2,1,0:T(8,128)(2,1)S(1)} %pad_maximum_fusion.near), channel_id=1, source_target_pairs={{0,8},{4,12},{8,16},{10,2},{12,20},{14,6},{16,24},{18,10},{20,28},... | collective-permute-start | bytes 1572872 | tf_op jit(solution)/shard_map/ppermute | solution.py:253
  12.3 14.7 %collective-permute-start.6 = (bf16[2,256,512]{2,1,0:T(8,128)(2,1)S(1)}, bf16[2,256,512]{2,1,0:T(8,128)(2,1)S(1)}, u32[]{:S(2)}, u32[]{:S(2)}) collective-permute-start(bf16[2,256,512]{2,1,0:T(8,128)(2,1)S(1)} %pad_maximum_fusion.1), channel_id=1, source_target_pairs={{0,4},{2,6},{4,0},{6,2},{8,12},{10,14},{12,8},{14,10},{16,20},{18,... | collective-permute-start | bytes 1572872 | tf_op jit(solution)/shard_map/ppermute | solution.py:242
  15.8 11.8 %collective-permute-start.7 = (bf16[256,512]{1,0:T(8,128)(2,1)S(1)}, bf16[256,512]{1,0:T(8,128)(2,1)S(1)}, u32[]{:S(2)}, u32[]{:S(2)}) collective-permute-start(bf16[256,512]{1,0:T(8,128)(2,1)S(1)} %get-tuple-element.22), channel_id=1, source_target_pairs={{2,8},{6,12},{8,2},{10,16},{12,6},{14,20},{16,10},{18,24},{20,14},... | collective-permute-start | bytes 786440 | tf_op jit(solution)/shard_map/ppermute | solution.py:253
  22.0 7.3 %collective-permute-start.8 = (bf16[256,512]{1,0:T(8,128)(2,1)S(1)}, bf16[256,512]{1,0:T(8,128)(2,1)S(1)}, u32[]{:S(2)}, u32[]{:S(2)}) collective-permute-start(bf16[256,512]{1,0:T(8,128)(2,1)S(1)} %get-tuple-element.21), channel_id=1, source_target_pairs={{0,8},{4,12},{8,16},{10,2},{12,20},{14,6},{16,24},{18,10},{20,28},... | collective-permute-start | bytes 786440 | tf_op jit(solution)/shard_map/ppermute | solution.py:253
  23.3 4.3 %collective-permute-start.10 = (bf16[128,512]{1,0:T(8,128)(2,1)S(1)}, bf16[128,512]{1,0:T(8,128)(2,1)S(1)}, u32[]{:S(2)}, u32[]{:S(2)}) collective-permute-start(bf16[128,512]{1,0:T(8,128)(2,1)S(1)} %get-tuple-element.19), channel_id=1, source_target_pairs={{0,2},{2,0},{4,6},{6,4},{8,10},{10,8},{12,14},{14,12},{16,18},{18,... | collective-permute-start | bytes 393224 | tf_op jit(solution)/shard_map/ppermute | solution.py:242
  24.5 3.2 %collective-permute-start.9 = (bf16[128,512]{1,0:T(8,128)(2,1)S(1)}, bf16[128,512]{1,0:T(8,128)(2,1)S(1)}, u32[]{:S(2)}, u32[]{:S(2)}) collective-permute-start(bf16[128,512]{1,0:T(8,128)(2,1)S(1)} %get-tuple-element.20), channel_id=1, source_target_pairs={{0,2},{2,0},{4,6},{6,4},{8,10},{10,8},{12,14},{14,12},{16,18},{18,... | collective-permute-start | bytes 393224 | tf_op jit(solution)/shard_map/ppermute | solution.py:242
  30.3 1.7 %collective-permute-start.11 = (f32[8,128]{1,0:T(8,128)S(1)}, f32[8,128]{1,0:T(8,128)S(1)}, u32[]{:S(2)}, u32[]{:S(2)}) collective-permute-start(f32[8,128]{1,0:T(8,128)S(1)} %tail.1), channel_id=1, source_target_pairs={{0,2},{2,0},{4,6},{6,4},{8,10},{10,8},{12,14},{14,12},{16,18},{18,... | collective-permute-start | bytes 12296 | tf_op jit(solution)/shard_map/ppermute | solution.py:242

commit v6 on v5

--- a/solution.py
+++ b/solution.py
@@ -32,7 +32,7 @@
     def start(here):
         for i, (same, moving, cols) in enumerate(wanted):
             target = here if same else 1 - here
-            pair = mixed if (target == 0) == moving else weighted
+            pair = mixed if (target == 1) == moving else weighted
             for j in range(2):
                 pltpu.make_async_copy(
                     pair[j].at[:, cols], slots.at[2 * i + j], sems.at[2 * i + j]
@@ -123,8 +123,8 @@
     return sums
 
 
-def block_dot(core, moving, fixed):
-    pair = (moving, fixed) if core == 0 else (fixed, moving)
+def block_dot(back, moving, fixed):
+    pair = (fixed, moving) if back else (moving, fixed)
     return lax.dot_general(*pair, NT, preferred_element_type=jnp.float32)
 
 
@@ -139,16 +139,16 @@
 
 
 def early_products(home, table, stay, near, beyond, far, before=None):
-    core = home & 1
+    back = home & 1 == 0
     here = {home: near.at[0], home ^ 1: near.at[1], home ^ 2: far.at[0]}
     there = {home: beyond.at[0], home ^ 1: beyond.at[1]}
     for d in range(5):
         total = None if before is None else before[:, columns_of(d)]
         for block, ref in stay.items():
-            other = block - d if core == 0 else block + d
+            other = block + d if back else block - d
             source = here if 0 <= other < 4 else there
             if (other & 3) in source:
-                dot = block_dot(core, source[other & 3][...], ref[...])
+                dot = block_dot(back, source[other & 3][...], ref[...])
                 total = dot if total is None else total + dot
         if total is None:
             total = jnp.zeros((BLK, BLK), jnp.float32)
@@ -179,12 +179,12 @@
     last[BLK // 2 :] = low[...]
 
     def body(home):
-        core = home & 1
+        back = home & 1 == 0
         stay = {home: own, home ^ 1: flip, home ^ 2: fixed.at[0], home ^ 3: fixed.at[1]}
         for d in range(5):
             total = table_in[:, columns_of(d)]
             for block, ref in stay.items():
-                other = block - d if core == 0 else block + d
+                other = block + d if back else block - d
                 inside = 0 <= other < 4
                 moving = None
                 if other & 3 == home ^ 3:
@@ -192,7 +192,7 @@
                 elif other & 3 == home ^ 2 and not inside:
                     moving = on_near
                 if moving is not None:
-                    total = total + block_dot(core, moving[...], ref[...])
+                    total = total + block_dot(back, moving[...], ref[...])
             table[:, columns_of(d)] = total
 
     by_home(body)
@@ -247,7 +247,7 @@
     for q in range(quads):
         for e in range(4):
             core = e % 2 ^ flip
-            to = q + 1 - 2 * core
+            to = q - 1 + 2 * core
             if 0 <= to < quads:
                 pairs.append((q * 4 + e, to * 4 + (e ^ flip)))
     return lax.ppermute(value, "ctx", pairs)

time: 60.4 us -> 60.2 us (level)
    ppermute x9, starting transfers between devices: 9.54 us -> 6.39 us  [swap(): return lax.ppermute(value, 'ctx', pairs)]
    ppermute x3, starting transfers between devices: 8.79 us -> 11.4 us  [onward(): return lax.ppermute(value, 'ctx', pairs)]
    ppermute x9, waiting for transfers between devices: 5.03 us -> 6.8 us  [swap(): return lax.ppermute(value, 'ctx', pairs)]
    ppermute x3, waiting for transfers between devices: 1.67 us -> 0.01 us  [onward(): return lax.ppermute(value, 'ctx', pairs)]
  transfers between devices with their start and end apart: 12 -> 12, of which waited for: 6 -> 5; matrix products, arithmetic and copies ran while one was open for 0% -> 0% of each run, Pallas kernels for 7% -> 7%
where the time goes in v6:
time: 60.2 us; the launch traced here: 59.4 us
  blocking collectives  27.1 us (45%)
  starting transfers between devices  17.8 us (30%)
  waiting for transfers between devices  6.81 us (11%)
  Pallas kernels  6.63 us (11%)
  local copies, waits for them, and re-layouts  0.68 us (1%)
    all_to_all x1, blocking collectives, on_device(): gathered = lax.all_to_all(spread, 'ctx', 0, 0, axis_index_groups=groups)  27.1 us
    ppermute x3, starting transfers between devices, onward(): return lax.ppermute(value, 'ctx', pairs)  11.4 us
    ppermute x9, waiting for transfers between devices, swap(): return lax.ppermute(value, 'ctx', pairs)  6.8 us
    ppermute x9, starting transfers between devices, swap(): return lax.ppermute(value, 'ctx', pairs)  6.39 us
    pallas_call x3, Pallas kernels, deal(): pl.pallas_call(body, in_specs=[pl.BlockSpec(memory_space=pl.ANY)] * 4, ou...  4.3 us
  transfers between devices with their start and end apart: 12, of which 5 were waited for; matrix products, arithmetic and copies ran while one was open for 0% of the time, Pallas kernels for 7%

profile of v6, /device:TPU:1, one launch (start us, length us, event | category | flops | bytes accessed | tf_op | source)
XLA Modules:
  0.0 59.4 jit_solution(13287013613286548431)
XLA Ops:
  0.0 1.3 %deal_first.1 = bf16[2,256,512]{2,1,0:T(8,128)(2,1)S(1)} custom-call(bf16[256,2048]{1,0:T(8,128)(2,1)} %q.5, bf16[256,2048]{1,0:T(8,128)(2,1)} %k.5, bf16[256,2048]{1,0:T(8,128)(2,1)} %v.5, bf16[256,2048]{1,0:T(8,128)(2,1)} %g.5), custom_call_target="tpu_custom_call" | custom-call | tf_op jit(solution)/shard_map/deal_first/pallas_call | solution.py:100
  1.3 3.8 %collective-permute-start.3 = (bf16[2,256,512]{2,1,0:T(8,128)(2,1)S(1)}, bf16[2,256,512]{2,1,0:T(8,128)(2,1)S(1)}, u32[]{:S(2)}, u32[]{:S(2)}) collective-permute-start(bf16[2,256,512]{2,1,0:T(8,128)(2,1)S(1)} %deal_first.1), channel_id=1, source_target_pairs={{0,4},{2,6},{4,0},{6,2},{8,12},{10,14},{12,8},{14,10},{16,20},{18,... | collective-permute-start | bytes 1572872 | tf_op jit(solution)/shard_map/ppermute | solution.py:242
  5.2 1.3 %deal_moving.1 = (bf16[256,512]{1,0:T(8,128)(2,1)S(1)}, bf16[256,512]{1,0:T(8,128)(2,1)S(1)}) custom-call(bf16[256,2048]{1,0:T(8,128)(2,1)} %q.5, bf16[256,2048]{1,0:T(8,128)(2,1)} %k.5, bf16[256,2048]{1,0:T(8,128)(2,1)} %v.5, bf16[256,2048]{1,0:T(8,128)(2,1)} %g.5), custom_call_target="tpu_custom_call" | custom-call | tf_op jit(solution)/shard_map/deal_moving/pallas_call | solution.py:100
  6.5 1.0 %collective-permute-start.1 = (bf16[256,512]{1,0:T(8,128)(2,1)S(1)}, bf16[256,512]{1,0:T(8,128)(2,1)S(1)}, u32[]{:S(2)}, u32[]{:S(2)}) collective-permute-start(bf16[256,512]{1,0:T(8,128)(2,1)S(1)} %get-tuple-element.15), channel_id=1, source_target_pairs={{0,2},{2,0},{4,6},{6,4},{8,10},{10,8},{12,14},{14,12},{16,18},{18,... | collective-permute-start | bytes 786440 | tf_op jit(solution)/shard_map/ppermute | solution.py:242
  7.5 1.7 %deal_fixed.1 = (bf16[128,512]{1,0:T(8,128)(2,1)S(1)}, bf16[128,512]{1,0:T(8,128)(2,1)S(1)}, bf16[256,512]{1,0:T(8,128)(2,1)S(1)}, bf16[256,512]{1,0:T(8,128)(2,1)S(1)}, bf16[256,512]{1,0:T(8,128)(2,1)S(1)}) custom-call(bf16[256,2048]{1,0:T(8,128)(2,1)} %q.5, bf16[256,2048]{1,0:T(8,128)(2,1)} %k.5, bf16[256,2048]{1,0:T(8,128)(2,1)} %v.5, bf16[256,2048]{1,0:T(8,128)(2,1)} %g.5), custom_call_target="tpu_custom_call" | custom-call | tf_op jit(solution)/shard_map/deal_fixed/pallas_call | solution.py:100
  9.2 0.1 collective-permute-start.4
  9.3 0.5 collective-permute-start.5
  9.8 0.1 collective-permute-start
  9.9 0.7 %collective-permute-done.4 = bf16[128,512]{1,0:T(8,128)(2,1)S(1)} collective-permute-done((bf16[128,512]{1,0:T(8,128)(2,1)S(1)}, bf16[128,512]{1,0:T(8,128)(2,1)S(1)}, u32[]{:S(2)}, u32[]{:S(2)}) %collective-permute-start.4) | collective-permute-done | bytes 131104 | tf_op jit(solution)/shard_map/ppermute | solution.py:242
  10.6 0.2 collective-permute-done.5
  10.8 0.0 collective-permute-done.1
  10.9 0.1 pad_maximum_fusion.near
  10.9 3.6 %collective-permute-start.2 = (bf16[2,256,512]{2,1,0:T(8,128)(2,1)S(1)}, bf16[2,256,512]{2,1,0:T(8,128)(2,1)S(1)}, u32[]{:S(2)}, u32[]{:S(2)}) collective-permute-start(bf16[2,256,512]{2,1,0:T(8,128)(2,1)S(1)} %pad_maximum_fusion.near), channel_id=1, source_target_pairs={{2,10},{6,14},{8,0},{10,18},{12,4},{14,22},{16,8},{18,26},{20,12},... | collective-permute-start | bytes 1572872 | tf_op jit(solution)/shard_map/ppermute | solution.py:253
  14.5 0.1 pad_maximum_fusion.1
  14.6 0.1 collective-permute-start.6
  14.7 1.1 %collective-permute-done.3.far = bf16[2,256,512]{2,1,0:T(8,128)(2,1)S(1)} collective-permute-done((bf16[2,256,512]{2,1,0:T(8,128)(2,1)S(1)}, bf16[2,256,512]{2,1,0:T(8,128)(2,1)S(1)}, u32[]{:S(2)}, u32[]{:S(2)}) %collective-permute-start.3) | collective-permute-done | bytes 524320 | tf_op jit(solution)/shard_map/ppermute | solution.py:242
  15.8 0.7 %collective-permute-start.7 = (bf16[256,512]{1,0:T(8,128)(2,1)S(1)}, bf16[256,512]{1,0:T(8,128)(2,1)S(1)}, u32[]{:S(2)}, u32[]{:S(2)}) collective-permute-start(bf16[256,512]{1,0:T(8,128)(2,1)S(1)} %get-tuple-element.22), channel_id=1, source_target_pairs={{0,10},{4,14},{8,18},{10,0},{12,22},{14,4},{16,26},{18,8},{20,30},... | collective-permute-start | bytes 786440 | tf_op jit(solution)/shard_map/ppermute | solution.py:253
  16.5 7.2 %collective-permute-start.8 = (bf16[256,512]{1,0:T(8,128)(2,1)S(1)}, bf16[256,512]{1,0:T(8,128)(2,1)S(1)}, u32[]{:S(2)}, u32[]{:S(2)}) collective-permute-start(bf16[256,512]{1,0:T(8,128)(2,1)S(1)} %get-tuple-element.21), channel_id=1, source_target_pairs={{2,10},{6,14},{8,0},{10,18},{12,4},{14,22},{16,8},{18,26},{20,12},... | collective-permute-start | bytes 786440 | tf_op jit(solution)/shard_map/ppermute | solution.py:253
  23.7 0.0 collective-permute-done.flip
  23.7 0.1 collective-permute-start.10
  23.8 0.0 collective-permute-done.2.beyond
  23.8 0.5 collective-permute-start.9
  24.3 0.6 %early.1.before = f32[256,1280]{1,0:T(8,128)S(1)} custom-call(bf16[256,512]{1,0:T(8,128)(2,1)S(1)} %get-tuple-element.12.own, bf16[256,512]{1,0:T(8,128)(2,1)S(1)} %collective-permute-done.flip, bf16[2,256,512]{2,1,0:T(8,128)(2,1)S(1)} %collective-permute-done.2.beyond, bf16[2,256,512]{2,1,0:T(8,128)(2,1)S(1)} %pad_maximum_fusion.near, ...), custom_call_target="tpu_custom_call" | custom-call | bytes 4194304 | tf_op jit(solution)/shard_map/early/pallas_call | solution.py:209
  24.9 3.7 %collective-permute-done.6.fixed = bf16[2,256,512]{2,1,0:T(8,128)(2,1)S(1)} collective-permute-done((bf16[2,256,512]{2,1,0:T(8,128)(2,1)S(1)}, bf16[2,256,512]{2,1,0:T(8,128)(2,1)S(1)}, u32[]{:S(2)}, u32[]{:S(2)}) %collective-permute-start.6) | collective-permute-done | bytes 524320 | tf_op jit(solution)/shard_map/ppermute | solution.py:242
  28.6 0.6 main.1.table_in
  29.1 0.0 collective-permute-done.10.low
  29.2 0.0 collective-permute-done.9.top
  29.2 0.0 collective-permute-done.7.on_far
  29.2 0.0 collective-permute-done.8.on_near
  29.2 1.2 %tail.1 = f32[8,128]{1,0:T(8,128)S(1)} custom-call(f32[256,1280]{1,0:T(8,128)S(1)} %main.1.table_in, bf16[256,512]{1,0:T(8,128)(2,1)S(1)} %collective-permute-done.7.on_far, bf16[256,512]{1,0:T(8,128)(2,1)S(1)} %collective-permute-done.8.on_near, bf16[128,512]{1,0:T(8,128)(2,1)S(1)} %collective-permute-done.9.top, ...), custom_call_target="tpu_custom_call" | custom-call | tf_op jit(solution)/shard_map/tail/pallas_call | solution.py:223
  30.4 0.1 collective-permute-start.11
  30.5 1.2 %collective-permute-done.11 = f32[8,128]{1,0:T(8,128)S(1)} collective-permute-done((f32[8,128]{1,0:T(8,128)S(1)}, f32[8,128]{1,0:T(8,128)S(1)}, u32[]{:S(2)}, u32[]{:S(2)}) %collective-permute-start.11) | collective-permute-done | bytes 4128 | tf_op jit(solution)/shard_map/ppermute | solution.py:242
  31.7 27.1 %all_to_all.5 = f32[64,8,128]{2,1,0:T(8,128)S(1)} all-to-all(f32[64,8,128]{2,1,0:T(8,128)S(1)} %broadcast_in_dim.2), channel_id=1, replica_groups={{0,4,8,12,16,20,24,28,32,36,40,44,48,52,56,60,64,68,72,76,80,84,88,92,9..., dimensions={0} | all-to-all | bytes 524288 | tf_op jit(solution)/shard_map/all_to_all | solution.py:278
  58.8 0.6 %copy.7 = f32[1,2,8,128]{3,1,2,0:T(2,128)} copy(f32[1,2,8,128]{3,2,1,0:T(8,128)S(1)} %bitcast.22) | data formatting | bytes 16384
  (6 shorter events, 0.1 us)
Async XLA Ops:
  1.3 14.4 %collective-permute-start.3 = (bf16[2,256,512]{2,1,0:T(8,128)(2,1)S(1)}, bf16[2,256,512]{2,1,0:T(8,128)(2,1)S(1)}, u32[]{:S(2)}, u32[]{:S(2)}) collective-permute-start(bf16[2,256,512]{2,1,0:T(8,128)(2,1)S(1)} %deal_first.1), channel_id=1, source_target_pairs={{0,4},{2,6},{4,0},{6,2},{8,12},{10,14},{12,8},{14,10},{16,20},{18,... | collective-permute-start | bytes 1572872 | tf_op jit(solution)/shard_map/ppermute | solution.py:242
  6.5 4.4 %collective-permute-start.1 = (bf16[256,512]{1,0:T(8,128)(2,1)S(1)}, bf16[256,512]{1,0:T(8,128)(2,1)S(1)}, u32[]{:S(2)}, u32[]{:S(2)}) collective-permute-start(bf16[256,512]{1,0:T(8,128)(2,1)S(1)} %get-tuple-element.15), channel_id=1, source_target_pairs={{0,2},{2,0},{4,6},{6,4},{8,10},{10,8},{12,14},{14,12},{16,18},{18,... | collective-permute-start | bytes 786440 | tf_op jit(solution)/shard_map/ppermute | solution.py:242
  9.2 1.4 %collective-permute-start.4 = (bf16[128,512]{1,0:T(8,128)(2,1)S(1)}, bf16[128,512]{1,0:T(8,128)(2,1)S(1)}, u32[]{:S(2)}, u32[]{:S(2)}) collective-permute-start(bf16[128,512]{1,0:T(8,128)(2,1)S(1)} %get-tuple-element.17), channel_id=1, source_target_pairs={{0,2},{2,0},{4,6},{6,4},{8,10},{10,8},{12,14},{14,12},{16,18},{18,... | collective-permute-start | bytes 393224 | tf_op jit(solution)/shard_map/ppermute | solution.py:242
  9.3 1.5 %collective-permute-start.5 = (bf16[128,512]{1,0:T(8,128)(2,1)S(1)}, bf16[128,512]{1,0:T(8,128)(2,1)S(1)}, u32[]{:S(2)}, u32[]{:S(2)}) collective-permute-start(bf16[128,512]{1,0:T(8,128)(2,1)S(1)} %get-tuple-element.18), channel_id=1, source_target_pairs={{0,2},{2,0},{4,6},{6,4},{8,10},{10,8},{12,14},{14,12},{16,18},{18,... | collective-permute-start | bytes 393224 | tf_op jit(solution)/shard_map/ppermute | solution.py:242
  9.8 13.9 %collective-permute-start = (bf16[256,512]{1,0:T(8,128)(2,1)S(1)}, bf16[256,512]{1,0:T(8,128)(2,1)S(1)}, u32[]{:S(2)}, u32[]{:S(2)}) collective-permute-start(bf16[256,512]{1,0:T(8,128)(2,1)S(1)} %get-tuple-element.13), channel_id=1, source_target_pairs={{0,2},{2,0},{4,6},{6,4},{8,10},{10,8},{12,14},{14,12},{16,18},{18,... | collective-permute-start | bytes 786440 | tf_op jit(solution)/shard_map/ppermute | solution.py:242
  10.9 12.9 %collective-permute-start.2 = (bf16[2,256,512]{2,1,0:T(8,128)(2,1)S(1)}, bf16[2,256,512]{2,1,0:T(8,128)(2,1)S(1)}, u32[]{:S(2)}, u32[]{:S(2)}) collective-permute-start(bf16[2,256,512]{2,1,0:T(8,128)(2,1)S(1)} %pad_maximum_fusion.near), channel_id=1, source_target_pairs={{2,10},{6,14},{8,0},{10,18},{12,4},{14,22},{16,8},{18,26},{20,12},... | collective-permute-start | bytes 1572872 | tf_op jit(solution)/shard_map/ppermute | solution.py:253
  14.6 14.0 %collective-permute-start.6 = (bf16[2,256,512]{2,1,0:T(8,128)(2,1)S(1)}, bf16[2,256,512]{2,1,0:T(8,128)(2,1)S(1)}, u32[]{:S(2)}, u32[]{:S(2)}) collective-permute-start(bf16[2,256,512]{2,1,0:T(8,128)(2,1)S(1)} %pad_maximum_fusion.1), channel_id=1, source_target_pairs={{0,4},{2,6},{4,0},{6,2},{8,12},{10,14},{12,8},{14,10},{16,20},{18,... | collective-permute-start | bytes 1572872 | tf_op jit(solution)/shard_map/ppermute | solution.py:242
  15.8 13.4 %collective-permute-start.7 = (bf16[256,512]{1,0:T(8,128)(2,1)S(1)}, bf16[256,512]{1,0:T(8,128)(2,1)S(1)}, u32[]{:S(2)}, u32[]{:S(2)}) collective-permute-start(bf16[256,512]{1,0:T(8,128)(2,1)S(1)} %get-tuple-element.22), channel_id=1, source_target_pairs={{0,10},{4,14},{8,18},{10,0},{12,22},{14,4},{16,26},{18,8},{20,30},... | collective-permute-start | bytes 786440 | tf_op jit(solution)/shard_map/ppermute | solution.py:253
  16.5 12.7 %collective-permute-start.8 = (bf16[256,512]{1,0:T(8,128)(2,1)S(1)}, bf16[256,512]{1,0:T(8,128)(2,1)S(1)}, u32[]{:S(2)}, u32[]{:S(2)}) collective-permute-start(bf16[256,512]{1,0:T(8,128)(2,1)S(1)} %get-tuple-element.21), channel_id=1, source_target_pairs={{2,10},{6,14},{8,0},{10,18},{12,4},{14,22},{16,8},{18,26},{20,12},... | collective-permute-start | bytes 786440 | tf_op jit(solution)/shard_map/ppermute | solution.py:253
  23.7 5.4 %collective-permute-start.10 = (bf16[128,512]{1,0:T(8,128)(2,1)S(1)}, bf16[128,512]{1,0:T(8,128)(2,1)S(1)}, u32[]{:S(2)}, u32[]{:S(2)}) collective-permute-start(bf16[128,512]{1,0:T(8,128)(2,1)S(1)} %get-tuple-element.19), channel_id=1, source_target_pairs={{0,2},{2,0},{4,6},{6,4},{8,10},{10,8},{12,14},{14,12},{16,18},{18,... | collective-permute-start | bytes 393224 | tf_op jit(solution)/shard_map/ppermute | solution.py:242
  23.8 5.3 %collective-permute-start.9 = (bf16[128,512]{1,0:T(8,128)(2,1)S(1)}, bf16[128,512]{1,0:T(8,128)(2,1)S(1)}, u32[]{:S(2)}, u32[]{:S(2)}) collective-permute-start(bf16[128,512]{1,0:T(8,128)(2,1)S(1)} %get-tuple-element.20), channel_id=1, source_target_pairs={{0,2},{2,0},{4,6},{6,4},{8,10},{10,8},{12,14},{14,12},{16,18},{18,... | collective-permute-start | bytes 393224 | tf_op jit(solution)/shard_map/ppermute | solution.py:242
  30.4 1.3 %collective-permute-start.11 = (f32[8,128]{1,0:T(8,128)S(1)}, f32[8,128]{1,0:T(8,128)S(1)}, u32[]{:S(2)}, u32[]{:S(2)}) collective-permute-start(f32[8,128]{1,0:T(8,128)S(1)} %tail.1), channel_id=1, source_target_pairs={{0,2},{2,0},{4,6},{6,4},{8,10},{10,8},{12,14},{14,12},{16,18},{18,... | collective-permute-start | bytes 12296 | tf_op jit(solution)/shard_map/ppermute | solution.py:242

commit v7 on v6

--- a/solution.py
+++ b/solution.py
@@ -138,7 +138,7 @@
     return pl.ds(d * BLK, BLK)
 
 
-def early_products(home, table, stay, near, beyond, far, before=None):
+def early_products(home, table, stay, near, beyond, far, before=None, last=None, others=()):
     back = home & 1 == 0
     here = {home: near.at[0], home ^ 1: near.at[1], home ^ 2: far.at[0]}
     there = {home: beyond.at[0], home ^ 1: beyond.at[1]}
@@ -150,6 +150,12 @@
             if (other & 3) in source:
                 dot = block_dot(back, source[other & 3][...], ref[...])
                 total = dot if total is None else total + dot
+            elif last is not None and 0 <= other < 4:
+                total = total + block_dot(back, last[...], ref[...])
+        for block, ref in others:
+            other = block + d if back else block - d
+            if other == home ^ 3:
+                total = total + block_dot(back, last[...], ref[...])
         if total is None:
             total = jnp.zeros((BLK, BLK), jnp.float32)
         table[:, columns_of(d)] = total
@@ -163,21 +169,20 @@
     )
 
 
-def main_kernel(before, fixed, beyond, near, far, table):
+def main_kernel(before, top, low, own, flip, fixed, beyond, near, far, table, last):
+    last[: BLK // 2] = top[...]
+    last[BLK // 2 :] = low[...]
     by_home(
         lambda home: early_products(
             home, table, {home ^ 2: fixed.at[0], home ^ 3: fixed.at[1]},
-            near, beyond, far, before,
+            near, beyond, far, before, last, ((home, own), (home ^ 1, flip)),
         )
     )
 
 
 def tail_kernel(
-    table_in, on_far, on_near, top, low, own, flip, fixed, out, last, table
+    table_in, on_near, on_far, own, flip, fixed, out, table
 ):
-    last[: BLK // 2] = top[...]
-    last[BLK // 2 :] = low[...]
-
     def body(home):
         back = home & 1 == 0
         stay = {home: own, home ^ 1: flip, home ^ 2: fixed.at[0], home ^ 3: fixed.at[1]}
@@ -187,8 +192,8 @@
                 other = block + d if back else block - d
                 inside = 0 <= other < 4
                 moving = None
-                if other & 3 == home ^ 3:
-                    moving = last if inside else on_far
+                if other & 3 == home ^ 3 and not inside:
+                    moving = on_far
                 elif other & 3 == home ^ 2 and not inside:
                     moving = on_near
                 if moving is not None:
@@ -201,16 +206,17 @@
         out[i : i + 1, :] = sums[:, i * 128 : (i + 1) * 128]
 
 
-def correlate(moving, late, own, flip, fixed):
+def correlate(moving, last, late, own, flip, fixed):
     vmem = pl.BlockSpec(memory_space=pltpu.VMEM)
     params = pltpu.CompilerParams(vmem_limit_bytes=40 * MIB)
 
-    def table_call(body, name, *operands):
+    def table_call(body, name, scratch, *operands):
         return pl.pallas_call(
             body,
             in_specs=[vmem] * len(operands),
             out_specs=vmem,
             out_shape=jax.ShapeDtypeStruct((BLK, 5 * BLK), jnp.float32),
+            scratch_shapes=scratch,
             compiler_params=params,
             cost_estimate=pl.CostEstimate(
                 flops=MAIN_COST, bytes_accessed=4 * MIB, transcendentals=0
@@ -218,17 +224,17 @@
             name=name,
         )(*operands)
 
-    table = table_call(early_kernel, "early", own, flip, *moving)
-    table = table_call(main_kernel, "main", table, fixed, *moving)
+    table = table_call(early_kernel, "early", [], own, flip, *moving)
+    table = table_call(
+        main_kernel, "main", [pltpu.VMEM((BLK, CH), BF16)],
+        table, *last, own, flip, fixed, *moving,
+    )
     return pl.pallas_call(
         tail_kernel,
         in_specs=[vmem] * (4 + len(late)),
         out_specs=vmem,
         out_shape=jax.ShapeDtypeStruct((8, 128), jnp.float32),
-        scratch_shapes=[
-            pltpu.VMEM((BLK, CH), BF16),
-            pltpu.VMEM((BLK, 5 * BLK), jnp.float32),
-        ],
+        scratch_shapes=[pltpu.VMEM((BLK, 5 * BLK), jnp.float32)],
         compiler_params=params,
         name="tail",
     )(table, *late, own, flip, fixed)
@@ -270,8 +276,8 @@
     last = [swap(far_moving[1, i : i + BLK // 2], quads, 0, 1) for i in (0, BLK // 2)]
     on_near = onward(far_moving[0], quads)
     on_far = onward(far_moving[1], quads, 1)
-    moving, late = (beyond, near_moving, far_moving), (on_far, on_near, *last)
-    part = correlate(moving, late, own_fixed, flip_fixed, far_fixed)
+    moving, late = (beyond, near_moving, far_moving), (on_near, on_far)
+    part = correlate(moving, last, late, own_fixed, flip_fixed, far_fixed)
     part = part + swap(part, quads, 0, 1)
     groups = [[q * 4 + y * 2 + c for q in range(quads) for y in range(2)] for c in range(2)]
     spread = jnp.broadcast_to(part[None], (2 * quads, 8, 128))

time: 60.2 us -> 60.1 us (level)
  no operation moved by 1% of the time
where the time goes in v7:
time: 60.1 us; the launch traced here: 59.3 us
  blocking collectives  27 us (45%)
  starting transfers between devices  17.8 us (30%)
  waiting for transfers between devices  6.81 us (11%)
  Pallas kernels  6.65 us (11%)
  local copies, waits for them, and re-layouts  0.68 us (1%)
    all_to_all x1, blocking collectives, on_device(): gathered = lax.all_to_all(spread, 'ctx', 0, 0, axis_index_groups=groups)  27 us
    ppermute x3, starting transfers between devices, onward(): return lax.ppermute(value, 'ctx', pairs)  11.4 us
    ppermute x9, waiting for transfers between devices, swap(): return lax.ppermute(value, 'ctx', pairs)  6.8 us
    ppermute x9, starting transfers between devices, swap(): return lax.ppermute(value, 'ctx', pairs)  6.39 us
    pallas_call x3, Pallas kernels, deal(): pl.pallas_call(body, in_specs=[pl.BlockSpec(memory_space=pl.ANY)] * 4, ou...  4.3 us
    pallas_call x2, Pallas kernels, table_call(): pl.pallas_call(body, in_specs=[vmem] * len(operands), out_specs=vmem, out...  1.31 us
  transfers between devices with their start and end apart: 12, of which 5 were waited for; matrix products, arithmetic and copies ran while one was open for 0% of the time, Pallas kernels for 7%

profile of v7, /device:TPU:1, one launch (start us, length us, event | category | flops | bytes accessed | tf_op | source)
XLA Modules:
  0.0 59.3 jit_solution(10790342528485216781)
XLA Ops:
  0.0 1.3 %deal_first.1 = bf16[2,256,512]{2,1,0:T(8,128)(2,1)S(1)} custom-call(bf16[256,2048]{1,0:T(8,128)(2,1)} %q.5, bf16[256,2048]{1,0:T(8,128)(2,1)} %k.5, bf16[256,2048]{1,0:T(8,128)(2,1)} %v.5, bf16[256,2048]{1,0:T(8,128)(2,1)} %g.5), custom_call_target="tpu_custom_call" | custom-call | tf_op jit(solution)/shard_map/deal_first/pallas_call | solution.py:100
  1.3 3.8 %collective-permute-start.3 = (bf16[2,256,512]{2,1,0:T(8,128)(2,1)S(1)}, bf16[2,256,512]{2,1,0:T(8,128)(2,1)S(1)}, u32[]{:S(2)}, u32[]{:S(2)}) collective-permute-start(bf16[2,256,512]{2,1,0:T(8,128)(2,1)S(1)} %deal_first.1), channel_id=1, source_target_pairs={{0,4},{2,6},{4,0},{6,2},{8,12},{10,14},{12,8},{14,10},{16,20},{18,... | collective-permute-start | bytes 1572872 | tf_op jit(solution)/shard_map/ppermute | solution.py:248
  5.2 1.3 %deal_moving.1 = (bf16[256,512]{1,0:T(8,128)(2,1)S(1)}, bf16[256,512]{1,0:T(8,128)(2,1)S(1)}) custom-call(bf16[256,2048]{1,0:T(8,128)(2,1)} %q.5, bf16[256,2048]{1,0:T(8,128)(2,1)} %k.5, bf16[256,2048]{1,0:T(8,128)(2,1)} %v.5, bf16[256,2048]{1,0:T(8,128)(2,1)} %g.5), custom_call_target="tpu_custom_call" | custom-call | tf_op jit(solution)/shard_map/deal_moving/pallas_call | solution.py:100
  6.5 1.0 %collective-permute-start.1 = (bf16[256,512]{1,0:T(8,128)(2,1)S(1)}, bf16[256,512]{1,0:T(8,128)(2,1)S(1)}, u32[]{:S(2)}, u32[]{:S(2)}) collective-permute-start(bf16[256,512]{1,0:T(8,128)(2,1)S(1)} %get-tuple-element.15), channel_id=1, source_target_pairs={{0,2},{2,0},{4,6},{6,4},{8,10},{10,8},{12,14},{14,12},{16,18},{18,... | collective-permute-start | bytes 786440 | tf_op jit(solution)/shard_map/ppermute | solution.py:248
  7.5 1.7 %deal_fixed.1 = (bf16[128,512]{1,0:T(8,128)(2,1)S(1)}, bf16[128,512]{1,0:T(8,128)(2,1)S(1)}, bf16[256,512]{1,0:T(8,128)(2,1)S(1)}, bf16[256,512]{1,0:T(8,128)(2,1)S(1)}, bf16[256,512]{1,0:T(8,128)(2,1)S(1)}) custom-call(bf16[256,2048]{1,0:T(8,128)(2,1)} %q.5, bf16[256,2048]{1,0:T(8,128)(2,1)} %k.5, bf16[256,2048]{1,0:T(8,128)(2,1)} %v.5, bf16[256,2048]{1,0:T(8,128)(2,1)} %g.5), custom_call_target="tpu_custom_call" | custom-call | tf_op jit(solution)/shard_map/deal_fixed/pallas_call | solution.py:100
  9.2 0.1 collective-permute-start.6
  9.3 0.5 collective-permute-start.7
  9.8 0.1 collective-permute-start
  9.9 0.7 %collective-permute-done.6 = bf16[128,512]{1,0:T(8,128)(2,1)S(1)} collective-permute-done((bf16[128,512]{1,0:T(8,128)(2,1)S(1)}, bf16[128,512]{1,0:T(8,128)(2,1)S(1)}, u32[]{:S(2)}, u32[]{:S(2)}) %collective-permute-start.6) | collective-permute-done | bytes 131104 | tf_op jit(solution)/shard_map/ppermute | solution.py:248
  10.6 0.2 collective-permute-done.7
  10.8 0.0 collective-permute-done.1
  10.9 0.1 pad_maximum_fusion.near
  10.9 3.6 %collective-permute-start.2 = (bf16[2,256,512]{2,1,0:T(8,128)(2,1)S(1)}, bf16[2,256,512]{2,1,0:T(8,128)(2,1)S(1)}, u32[]{:S(2)}, u32[]{:S(2)}) collective-permute-start(bf16[2,256,512]{2,1,0:T(8,128)(2,1)S(1)} %pad_maximum_fusion.near), channel_id=1, source_target_pairs={{2,10},{6,14},{8,0},{10,18},{12,4},{14,22},{16,8},{18,26},{20,12},... | collective-permute-start | bytes 1572872 | tf_op jit(solution)/shard_map/ppermute | solution.py:259
  14.5 0.1 pad_maximum_fusion.1
  14.6 0.1 collective-permute-start.8
  14.7 1.1 %collective-permute-done.3.far = bf16[2,256,512]{2,1,0:T(8,128)(2,1)S(1)} collective-permute-done((bf16[2,256,512]{2,1,0:T(8,128)(2,1)S(1)}, bf16[2,256,512]{2,1,0:T(8,128)(2,1)S(1)}, u32[]{:S(2)}, u32[]{:S(2)}) %collective-permute-start.3) | collective-permute-done | bytes 524320 | tf_op jit(solution)/shard_map/ppermute | solution.py:248
  15.8 0.7 %collective-permute-start.10 = (bf16[256,512]{1,0:T(8,128)(2,1)S(1)}, bf16[256,512]{1,0:T(8,128)(2,1)S(1)}, u32[]{:S(2)}, u32[]{:S(2)}) collective-permute-start(bf16[256,512]{1,0:T(8,128)(2,1)S(1)} %get-tuple-element.19), channel_id=1, source_target_pairs={{0,10},{4,14},{8,18},{10,0},{12,22},{14,4},{16,26},{18,8},{20,30},... | collective-permute-start | bytes 786440 | tf_op jit(solution)/shard_map/ppermute | solution.py:259
  16.5 7.2 %collective-permute-start.9 = (bf16[256,512]{1,0:T(8,128)(2,1)S(1)}, bf16[256,512]{1,0:T(8,128)(2,1)S(1)}, u32[]{:S(2)}, u32[]{:S(2)}) collective-permute-start(bf16[256,512]{1,0:T(8,128)(2,1)S(1)} %get-tuple-element.20), channel_id=1, source_target_pairs={{2,10},{6,14},{8,0},{10,18},{12,4},{14,22},{16,8},{18,26},{20,12},... | collective-permute-start | bytes 786440 | tf_op jit(solution)/shard_map/ppermute | solution.py:259
  23.7 0.0 collective-permute-done.flip
  23.7 0.1 collective-permute-start.4
  23.8 0.0 collective-permute-done.2.beyond
  23.8 0.5 collective-permute-start.5
  24.3 0.6 %early.1.before = f32[256,1280]{1,0:T(8,128)S(1)} custom-call(bf16[256,512]{1,0:T(8,128)(2,1)S(1)} %get-tuple-element.12.own, bf16[256,512]{1,0:T(8,128)(2,1)S(1)} %collective-permute-done.flip, bf16[2,256,512]{2,1,0:T(8,128)(2,1)S(1)} %collective-permute-done.2.beyond, bf16[2,256,512]{2,1,0:T(8,128)(2,1)S(1)} %pad_maximum_fusion.near, ...), custom_call_target="tpu_custom_call" | custom-call | bytes 4194304 | tf_op jit(solution)/shard_map/early/pallas_call | solution.py:214
  24.9 3.7 %collective-permute-done.8.fixed = bf16[2,256,512]{2,1,0:T(8,128)(2,1)S(1)} collective-permute-done((bf16[2,256,512]{2,1,0:T(8,128)(2,1)S(1)}, bf16[2,256,512]{2,1,0:T(8,128)(2,1)S(1)}, u32[]{:S(2)}, u32[]{:S(2)}) %collective-permute-start.8) | collective-permute-done | bytes 524320 | tf_op jit(solution)/shard_map/ppermute | solution.py:248
  28.6 0.0 collective-permute-done.4.top
  28.6 0.0 collective-permute-done.5.low
  28.6 0.7 %main.1.table_in = f32[256,1280]{1,0:T(8,128)S(1)} custom-call(f32[256,1280]{1,0:T(8,128)S(1)} %early.1.before, bf16[128,512]{1,0:T(8,128)(2,1)S(1)} %collective-permute-done.4.top, bf16[128,512]{1,0:T(8,128)(2,1)S(1)} %collective-permute-done.5.low, bf16[256,512]{1,0:T(8,128)(2,1)S(1)} %get-tuple-element.12.own, ...), custom_call_target="tpu_custom_call" | custom-call | bytes 4194304 | tf_op jit(solution)/shard_map/main/pallas_call | solution.py:214
  29.3 0.0 collective-permute-done.10.on_far
  29.3 0.0 collective-permute-done.9.on_near
  29.3 1.0 %tail.1 = f32[8,128]{1,0:T(8,128)S(1)} custom-call(f32[256,1280]{1,0:T(8,128)S(1)} %main.1.table_in, bf16[256,512]{1,0:T(8,128)(2,1)S(1)} %collective-permute-done.9.on_near, bf16[256,512]{1,0:T(8,128)(2,1)S(1)} %collective-permute-done.10.on_far, bf16[256,512]{1,0:T(8,128)(2,1)S(1)} %get-tuple-element.12.own, ...), custom_call_target="tpu_custom_call" | custom-call | tf_op jit(solution)/shard_map/tail/pallas_call | solution.py:232
  30.4 0.1 collective-permute-start.11
  30.5 1.2 %collective-permute-done.11 = f32[8,128]{1,0:T(8,128)S(1)} collective-permute-done((f32[8,128]{1,0:T(8,128)S(1)}, f32[8,128]{1,0:T(8,128)S(1)}, u32[]{:S(2)}, u32[]{:S(2)}) %collective-permute-start.11) | collective-permute-done | bytes 4128 | tf_op jit(solution)/shard_map/ppermute | solution.py:248
  31.7 27.0 %all_to_all.5 = f32[64,8,128]{2,1,0:T(8,128)S(1)} all-to-all(f32[64,8,128]{2,1,0:T(8,128)S(1)} %broadcast_in_dim.2), channel_id=1, replica_groups={{0,4,8,12,16,20,24,28,32,36,40,44,48,52,56,60,64,68,72,76,80,84,88,92,9..., dimensions={0} | all-to-all | bytes 524288 | tf_op jit(solution)/shard_map/all_to_all | solution.py:284
  58.7 0.6 %copy.7 = f32[1,2,8,128]{3,1,2,0:T(2,128)} copy(f32[1,2,8,128]{3,2,1,0:T(8,128)S(1)} %bitcast.22) | data formatting | bytes 16384
  (6 shorter events, 0.1 us)
Async XLA Ops:
  1.3 14.4 %collective-permute-start.3 = (bf16[2,256,512]{2,1,0:T(8,128)(2,1)S(1)}, bf16[2,256,512]{2,1,0:T(8,128)(2,1)S(1)}, u32[]{:S(2)}, u32[]{:S(2)}) collective-permute-start(bf16[2,256,512]{2,1,0:T(8,128)(2,1)S(1)} %deal_first.1), channel_id=1, source_target_pairs={{0,4},{2,6},{4,0},{6,2},{8,12},{10,14},{12,8},{14,10},{16,20},{18,... | collective-permute-start | bytes 1572872 | tf_op jit(solution)/shard_map/ppermute | solution.py:248
  6.5 4.4 %collective-permute-start.1 = (bf16[256,512]{1,0:T(8,128)(2,1)S(1)}, bf16[256,512]{1,0:T(8,128)(2,1)S(1)}, u32[]{:S(2)}, u32[]{:S(2)}) collective-permute-start(bf16[256,512]{1,0:T(8,128)(2,1)S(1)} %get-tuple-element.15), channel_id=1, source_target_pairs={{0,2},{2,0},{4,6},{6,4},{8,10},{10,8},{12,14},{14,12},{16,18},{18,... | collective-permute-start | bytes 786440 | tf_op jit(solution)/shard_map/ppermute | solution.py:248
  9.2 1.4 %collective-permute-start.6 = (bf16[128,512]{1,0:T(8,128)(2,1)S(1)}, bf16[128,512]{1,0:T(8,128)(2,1)S(1)}, u32[]{:S(2)}, u32[]{:S(2)}) collective-permute-start(bf16[128,512]{1,0:T(8,128)(2,1)S(1)} %get-tuple-element.17), channel_id=1, source_target_pairs={{0,2},{2,0},{4,6},{6,4},{8,10},{10,8},{12,14},{14,12},{16,18},{18,... | collective-permute-start | bytes 393224 | tf_op jit(solution)/shard_map/ppermute | solution.py:248
  9.3 1.5 %collective-permute-start.7 = (bf16[128,512]{1,0:T(8,128)(2,1)S(1)}, bf16[128,512]{1,0:T(8,128)(2,1)S(1)}, u32[]{:S(2)}, u32[]{:S(2)}) collective-permute-start(bf16[128,512]{1,0:T(8,128)(2,1)S(1)} %get-tuple-element.18), channel_id=1, source_target_pairs={{0,2},{2,0},{4,6},{6,4},{8,10},{10,8},{12,14},{14,12},{16,18},{18,... | collective-permute-start | bytes 393224 | tf_op jit(solution)/shard_map/ppermute | solution.py:248
  9.8 13.9 %collective-permute-start = (bf16[256,512]{1,0:T(8,128)(2,1)S(1)}, bf16[256,512]{1,0:T(8,128)(2,1)S(1)}, u32[]{:S(2)}, u32[]{:S(2)}) collective-permute-start(bf16[256,512]{1,0:T(8,128)(2,1)S(1)} %get-tuple-element.13), channel_id=1, source_target_pairs={{0,2},{2,0},{4,6},{6,4},{8,10},{10,8},{12,14},{14,12},{16,18},{18,... | collective-permute-start | bytes 786440 | tf_op jit(solution)/shard_map/ppermute | solution.py:248
  10.9 12.9 %collective-permute-start.2 = (bf16[2,256,512]{2,1,0:T(8,128)(2,1)S(1)}, bf16[2,256,512]{2,1,0:T(8,128)(2,1)S(1)}, u32[]{:S(2)}, u32[]{:S(2)}) collective-permute-start(bf16[2,256,512]{2,1,0:T(8,128)(2,1)S(1)} %pad_maximum_fusion.near), channel_id=1, source_target_pairs={{2,10},{6,14},{8,0},{10,18},{12,4},{14,22},{16,8},{18,26},{20,12},... | collective-permute-start | bytes 1572872 | tf_op jit(solution)/shard_map/ppermute | solution.py:259
  14.6 14.0 %collective-permute-start.8 = (bf16[2,256,512]{2,1,0:T(8,128)(2,1)S(1)}, bf16[2,256,512]{2,1,0:T(8,128)(2,1)S(1)}, u32[]{:S(2)}, u32[]{:S(2)}) collective-permute-start(bf16[2,256,512]{2,1,0:T(8,128)(2,1)S(1)} %pad_maximum_fusion.1), channel_id=1, source_target_pairs={{0,4},{2,6},{4,0},{6,2},{8,12},{10,14},{12,8},{14,10},{16,20},{18,... | collective-permute-start | bytes 1572872 | tf_op jit(solution)/shard_map/ppermute | solution.py:248
  15.8 13.5 %collective-permute-start.10 = (bf16[256,512]{1,0:T(8,128)(2,1)S(1)}, bf16[256,512]{1,0:T(8,128)(2,1)S(1)}, u32[]{:S(2)}, u32[]{:S(2)}) collective-permute-start(bf16[256,512]{1,0:T(8,128)(2,1)S(1)} %get-tuple-element.19), channel_id=1, source_target_pairs={{0,10},{4,14},{8,18},{10,0},{12,22},{14,4},{16,26},{18,8},{20,30},... | collective-permute-start | bytes 786440 | tf_op jit(solution)/shard_map/ppermute | solution.py:259
  16.5 12.8 %collective-permute-start.9 = (bf16[256,512]{1,0:T(8,128)(2,1)S(1)}, bf16[256,512]{1,0:T(8,128)(2,1)S(1)}, u32[]{:S(2)}, u32[]{:S(2)}) collective-permute-start(bf16[256,512]{1,0:T(8,128)(2,1)S(1)} %get-tuple-element.20), channel_id=1, source_target_pairs={{2,10},{6,14},{8,0},{10,18},{12,4},{14,22},{16,8},{18,26},{20,12},... | collective-permute-start | bytes 786440 | tf_op jit(solution)/shard_map/ppermute | solution.py:259
  23.7 4.9 %collective-permute-start.4 = (bf16[128,512]{1,0:T(8,128)(2,1)S(1)}, bf16[128,512]{1,0:T(8,128)(2,1)S(1)}, u32[]{:S(2)}, u32[]{:S(2)}) collective-permute-start(bf16[128,512]{1,0:T(8,128)(2,1)S(1)} %get-tuple-element.22), channel_id=1, source_target_pairs={{0,2},{2,0},{4,6},{6,4},{8,10},{10,8},{12,14},{14,12},{16,18},{18,... | collective-permute-start | bytes 393224 | tf_op jit(solution)/shard_map/ppermute | solution.py:248
  23.8 4.8 %collective-permute-start.5 = (bf16[128,512]{1,0:T(8,128)(2,1)S(1)}, bf16[128,512]{1,0:T(8,128)(2,1)S(1)}, u32[]{:S(2)}, u32[]{:S(2)}) collective-permute-start(bf16[128,512]{1,0:T(8,128)(2,1)S(1)} %get-tuple-element.21), channel_id=1, source_target_pairs={{0,2},{2,0},{4,6},{6,4},{8,10},{10,8},{12,14},{14,12},{16,18},{18,... | collective-permute-start | bytes 393224 | tf_op jit(solution)/shard_map/ppermute | solution.py:248
  30.4 1.3 %collective-permute-start.11 = (f32[8,128]{1,0:T(8,128)S(1)}, f32[8,128]{1,0:T(8,128)S(1)}, u32[]{:S(2)}, u32[]{:S(2)}) collective-permute-start(f32[8,128]{1,0:T(8,128)S(1)} %tail.1), channel_id=1, source_target_pairs={{0,2},{2,0},{4,6},{6,4},{8,10},{10,8},{12,14},{14,12},{16,18},{18,... | collective-permute-start | bytes 12296 | tf_op jit(solution)/shard_map/ppermute | solution.py:248

commit v8 on v7

--- a/solution.py
+++ b/solution.py
@@ -278,11 +278,11 @@
     on_far = onward(far_moving[1], quads, 1)
     moving, late = (beyond, near_moving, far_moving), (on_near, on_far)
     part = correlate(moving, last, late, own_fixed, flip_fixed, far_fixed)
-    part = part + swap(part, quads, 0, 1)
     groups = [[q * 4 + y * 2 + c for q in range(quads) for y in range(2)] for c in range(2)]
     spread = jnp.broadcast_to(part[None], (2 * quads, 8, 128))
     gathered = lax.all_to_all(spread, "ctx", 0, 0, axis_index_groups=groups)
-    return jnp.sum(gathered.reshape(quads, 2, 8, 128), axis=0).reshape(2, LAGS)
+    sums = jnp.sum(gathered.reshape(quads, 2, 8, 128), axis=0)
+    return (sums + swap(sums, quads, 0, 1)).reshape(2, LAGS)
 
 
 def solution(mesh):

time: 60.1 us -> 61.1 us (1.017)
  starting transfers between devices: 17.8 us -> 21.5 us
  blocking collectives: 27 us -> 25.2 us
    ppermute x9, starting transfers between devices: 6.39 us -> 10.1 us  [swap(): return lax.ppermute(value, 'ctx', pairs)]
    all_to_all x1, blocking collectives: 27 us -> 25.2 us  [on_device(): gathered = lax.all_to_all(spread, 'ctx', 0, 0, axis_index_groups=groups)]
where the time goes in v8:
time: 61.1 us; the launch traced here: 60.9 us
  blocking collectives  25.2 us (41%)
  starting transfers between devices  21.5 us (35%)
  Pallas kernels  6.65 us (11%)
  waiting for transfers between devices  6.48 us (11%)
  local copies, waits for them, and re-layouts  0.68 us (1%)
    all_to_all x1, blocking collectives, on_device(): gathered = lax.all_to_all(spread, 'ctx', 0, 0, axis_index_groups=groups)  25.2 us
    ppermute x3, starting transfers between devices, onward(): return lax.ppermute(value, 'ctx', pairs)  11.4 us
    ppermute x9, starting transfers between devices, swap(): return lax.ppermute(value, 'ctx', pairs)  10.1 us
    ppermute x9, waiting for transfers between devices, swap(): return lax.ppermute(value, 'ctx', pairs)  6.47 us
    pallas_call x3, Pallas kernels, deal(): pl.pallas_call(body, in_specs=[pl.BlockSpec(memory_space=pl.ANY)] * 4, ou...  4.3 us
    pallas_call x2, Pallas kernels, table_call(): pl.pallas_call(body, in_specs=[vmem] * len(operands), out_specs=vmem, out...  1.31 us
  transfers between devices with their start and end apart: 12, of which 5 were waited for; matrix products, arithmetic and copies ran while one was open for 0% of the time, Pallas kernels for 7%

profile of v8, /device:TPU:1, one launch (start us, length us, event | category | flops | bytes accessed | tf_op | source)
XLA Modules:
  0.0 60.9 jit_solution(8052091190416921852)
XLA Ops:
  0.0 1.3 %deal_first.1 = bf16[2,256,512]{2,1,0:T(8,128)(2,1)S(1)} custom-call(bf16[256,2048]{1,0:T(8,128)(2,1)} %q.5, bf16[256,2048]{1,0:T(8,128)(2,1)} %k.5, bf16[256,2048]{1,0:T(8,128)(2,1)} %v.5, bf16[256,2048]{1,0:T(8,128)(2,1)} %g.5), custom_call_target="tpu_custom_call" | custom-call | tf_op jit(solution)/shard_map/deal_first/pallas_call | solution.py:100
  1.3 3.8 %collective-permute-start.3 = (bf16[2,256,512]{2,1,0:T(8,128)(2,1)S(1)}, bf16[2,256,512]{2,1,0:T(8,128)(2,1)S(1)}, u32[]{:S(2)}, u32[]{:S(2)}) collective-permute-start(bf16[2,256,512]{2,1,0:T(8,128)(2,1)S(1)} %deal_first.1), channel_id=1, source_target_pairs={{0,4},{2,6},{4,0},{6,2},{8,12},{10,14},{12,8},{14,10},{16,20},{18,... | collective-permute-start | bytes 1572872 | tf_op jit(solution)/shard_map/ppermute | solution.py:248
  5.2 1.3 %deal_moving.1 = (bf16[256,512]{1,0:T(8,128)(2,1)S(1)}, bf16[256,512]{1,0:T(8,128)(2,1)S(1)}) custom-call(bf16[256,2048]{1,0:T(8,128)(2,1)} %q.5, bf16[256,2048]{1,0:T(8,128)(2,1)} %k.5, bf16[256,2048]{1,0:T(8,128)(2,1)} %v.5, bf16[256,2048]{1,0:T(8,128)(2,1)} %g.5), custom_call_target="tpu_custom_call" | custom-call | tf_op jit(solution)/shard_map/deal_moving/pallas_call | solution.py:100
  6.5 1.0 %collective-permute-start.1 = (bf16[256,512]{1,0:T(8,128)(2,1)S(1)}, bf16[256,512]{1,0:T(8,128)(2,1)S(1)}, u32[]{:S(2)}, u32[]{:S(2)}) collective-permute-start(bf16[256,512]{1,0:T(8,128)(2,1)S(1)} %get-tuple-element.15), channel_id=1, source_target_pairs={{0,2},{2,0},{4,6},{6,4},{8,10},{10,8},{12,14},{14,12},{16,18},{18,... | collective-permute-start | bytes 786440 | tf_op jit(solution)/shard_map/ppermute | solution.py:248
  7.5 1.7 %deal_fixed.1 = (bf16[128,512]{1,0:T(8,128)(2,1)S(1)}, bf16[128,512]{1,0:T(8,128)(2,1)S(1)}, bf16[256,512]{1,0:T(8,128)(2,1)S(1)}, bf16[256,512]{1,0:T(8,128)(2,1)S(1)}, bf16[256,512]{1,0:T(8,128)(2,1)S(1)}) custom-call(bf16[256,2048]{1,0:T(8,128)(2,1)} %q.5, bf16[256,2048]{1,0:T(8,128)(2,1)} %k.5, bf16[256,2048]{1,0:T(8,128)(2,1)} %v.5, bf16[256,2048]{1,0:T(8,128)(2,1)} %g.5), custom_call_target="tpu_custom_call" | custom-call | tf_op jit(solution)/shard_map/deal_fixed/pallas_call | solution.py:100
  9.2 0.1 collective-permute-start.6
  9.3 0.5 collective-permute-start.7
  9.8 0.1 collective-permute-start
  9.9 0.7 %collective-permute-done.6 = bf16[128,512]{1,0:T(8,128)(2,1)S(1)} collective-permute-done((bf16[128,512]{1,0:T(8,128)(2,1)S(1)}, bf16[128,512]{1,0:T(8,128)(2,1)S(1)}, u32[]{:S(2)}, u32[]{:S(2)}) %collective-permute-start.6) | collective-permute-done | bytes 131104 | tf_op jit(solution)/shard_map/ppermute | solution.py:248
  10.6 0.2 collective-permute-done.7
  10.8 0.0 collective-permute-done.1
  10.9 0.1 pad_maximum_fusion.near
  10.9 3.6 %collective-permute-start.2 = (bf16[2,256,512]{2,1,0:T(8,128)(2,1)S(1)}, bf16[2,256,512]{2,1,0:T(8,128)(2,1)S(1)}, u32[]{:S(2)}, u32[]{:S(2)}) collective-permute-start(bf16[2,256,512]{2,1,0:T(8,128)(2,1)S(1)} %pad_maximum_fusion.near), channel_id=1, source_target_pairs={{2,10},{6,14},{8,0},{10,18},{12,4},{14,22},{16,8},{18,26},{20,12},... | collective-permute-start | bytes 1572872 | tf_op jit(solution)/shard_map/ppermute | solution.py:259
  14.5 0.1 pad_maximum_fusion.1
  14.6 0.1 collective-permute-start.8
  14.7 1.1 %collective-permute-done.3.far = bf16[2,256,512]{2,1,0:T(8,128)(2,1)S(1)} collective-permute-done((bf16[2,256,512]{2,1,0:T(8,128)(2,1)S(1)}, bf16[2,256,512]{2,1,0:T(8,128)(2,1)S(1)}, u32[]{:S(2)}, u32[]{:S(2)}) %collective-permute-start.3) | collective-permute-done | bytes 524320 | tf_op jit(solution)/shard_map/ppermute | solution.py:248
  15.8 0.7 %collective-permute-start.10 = (bf16[256,512]{1,0:T(8,128)(2,1)S(1)}, bf16[256,512]{1,0:T(8,128)(2,1)S(1)}, u32[]{:S(2)}, u32[]{:S(2)}) collective-permute-start(bf16[256,512]{1,0:T(8,128)(2,1)S(1)} %get-tuple-element.19), channel_id=1, source_target_pairs={{0,10},{4,14},{8,18},{10,0},{12,22},{14,4},{16,26},{18,8},{20,30},... | collective-permute-start | bytes 786440 | tf_op jit(solution)/shard_map/ppermute | solution.py:259
  16.5 7.2 %collective-permute-start.9 = (bf16[256,512]{1,0:T(8,128)(2,1)S(1)}, bf16[256,512]{1,0:T(8,128)(2,1)S(1)}, u32[]{:S(2)}, u32[]{:S(2)}) collective-permute-start(bf16[256,512]{1,0:T(8,128)(2,1)S(1)} %get-tuple-element.20), channel_id=1, source_target_pairs={{2,10},{6,14},{8,0},{10,18},{12,4},{14,22},{16,8},{18,26},{20,12},... | collective-permute-start | bytes 786440 | tf_op jit(solution)/shard_map/ppermute | solution.py:259
  23.7 0.0 collective-permute-done.flip
  23.7 0.1 collective-permute-start.4
  23.8 0.0 collective-permute-done.2.beyond
  23.8 0.5 collective-permute-start.5
  24.3 0.6 early.1.before
  24.9 3.7 %collective-permute-done.8.fixed = bf16[2,256,512]{2,1,0:T(8,128)(2,1)S(1)} collective-permute-done((bf16[2,256,512]{2,1,0:T(8,128)(2,1)S(1)}, bf16[2,256,512]{2,1,0:T(8,128)(2,1)S(1)}, u32[]{:S(2)}, u32[]{:S(2)}) %collective-permute-start.8) | collective-permute-done | bytes 524320 | tf_op jit(solution)/shard_map/ppermute | solution.py:248
  28.6 0.0 collective-permute-done.4.top
  28.6 0.0 collective-permute-done.5.low
  28.6 0.7 %main.1.table_in = f32[256,1280]{1,0:T(8,128)S(1)} custom-call(f32[256,1280]{1,0:T(8,128)S(1)} %early.1.before, bf16[128,512]{1,0:T(8,128)(2,1)S(1)} %collective-permute-done.4.top, bf16[128,512]{1,0:T(8,128)(2,1)S(1)} %collective-permute-done.5.low, bf16[256,512]{1,0:T(8,128)(2,1)S(1)} %get-tuple-element.12.own, ...), custom_call_target="tpu_custom_call" | custom-call | bytes 4194304 | tf_op jit(solution)/shard_map/main/pallas_call | solution.py:214
  29.3 0.0 collective-permute-done.10.on_far
  29.3 0.0 collective-permute-done.9.on_near
  29.3 1.0 %tail.1 = f32[8,128]{1,0:T(8,128)S(1)} custom-call(f32[256,1280]{1,0:T(8,128)S(1)} %main.1.table_in, bf16[256,512]{1,0:T(8,128)(2,1)S(1)} %collective-permute-done.9.on_near, bf16[256,512]{1,0:T(8,128)(2,1)S(1)} %collective-permute-done.10.on_far, bf16[256,512]{1,0:T(8,128)(2,1)S(1)} %get-tuple-element.12.own, ...), custom_call_target="tpu_custom_call" | custom-call | tf_op jit(solution)/shard_map/tail/pallas_call | solution.py:232
  30.4 25.2 %all_to_all.5 = f32[64,8,128]{2,1,0:T(8,128)S(1)} all-to-all(f32[64,8,128]{2,1,0:T(8,128)S(1)} %broadcast_in_dim.2), channel_id=1, replica_groups={{0,4,8,12,16,20,24,28,32,36,40,44,48,52,56,60,64,68,72,76,80,84,88,92,9..., dimensions={0} | all-to-all | bytes 524288 | tf_op jit(solution)/shard_map/all_to_all | solution.py:283
  55.7 3.8 %collective-permute-start.11 = (f32[2,8,128]{2,1,0:T(8,128)S(1)}, f32[2,8,128]{2,1,0:T(8,128)S(1)}, u32[]{:S(2)}, u32[]{:S(2)}) collective-permute-start(f32[2,8,128]{2,1,0:T(8,128)S(1)} %reduce_sum.9), channel_id=1, source_target_pairs={{0,2},{2,0},{4,6},{6,4},{8,10},{10,8},{12,14},{14,12},{16,18},{18,... | collective-permute-start | bytes 24584 | tf_op jit(solution)/shard_map/ppermute | solution.py:248
  59.4 0.8 %collective-permute-done.11 = f32[2,8,128]{2,1,0:T(8,128)S(1)} collective-permute-done((f32[2,8,128]{2,1,0:T(8,128)S(1)}, f32[2,8,128]{2,1,0:T(8,128)S(1)}, u32[]{:S(2)}, u32[]{:S(2)}) %collective-permute-start.11) | collective-permute-done | bytes 8224 | tf_op jit(solution)/shard_map/ppermute | solution.py:248
  60.3 0.6 copy.7
  (6 shorter events, 0.1 us)
Async XLA Ops:
  1.3 14.4 %collective-permute-start.3 = (bf16[2,256,512]{2,1,0:T(8,128)(2,1)S(1)}, bf16[2,256,512]{2,1,0:T(8,128)(2,1)S(1)}, u32[]{:S(2)}, u32[]{:S(2)}) collective-permute-start(bf16[2,256,512]{2,1,0:T(8,128)(2,1)S(1)} %deal_first.1), channel_id=1, source_target_pairs={{0,4},{2,6},{4,0},{6,2},{8,12},{10,14},{12,8},{14,10},{16,20},{18,... | collective-permute-start | bytes 1572872 | tf_op jit(solution)/shard_map/ppermute | solution.py:248
  6.5 4.4 %collective-permute-start.1 = (bf16[256,512]{1,0:T(8,128)(2,1)S(1)}, bf16[256,512]{1,0:T(8,128)(2,1)S(1)}, u32[]{:S(2)}, u32[]{:S(2)}) collective-permute-start(bf16[256,512]{1,0:T(8,128)(2,1)S(1)} %get-tuple-element.15), channel_id=1, source_target_pairs={{0,2},{2,0},{4,6},{6,4},{8,10},{10,8},{12,14},{14,12},{16,18},{18,... | collective-permute-start | bytes 786440 | tf_op jit(solution)/shard_map/ppermute | solution.py:248
  9.2 1.4 %collective-permute-start.6 = (bf16[128,512]{1,0:T(8,128)(2,1)S(1)}, bf16[128,512]{1,0:T(8,128)(2,1)S(1)}, u32[]{:S(2)}, u32[]{:S(2)}) collective-permute-start(bf16[128,512]{1,0:T(8,128)(2,1)S(1)} %get-tuple-element.17), channel_id=1, source_target_pairs={{0,2},{2,0},{4,6},{6,4},{8,10},{10,8},{12,14},{14,12},{16,18},{18,... | collective-permute-start | bytes 393224 | tf_op jit(solution)/shard_map/ppermute | solution.py:248
  9.3 1.5 %collective-permute-start.7 = (bf16[128,512]{1,0:T(8,128)(2,1)S(1)}, bf16[128,512]{1,0:T(8,128)(2,1)S(1)}, u32[]{:S(2)}, u32[]{:S(2)}) collective-permute-start(bf16[128,512]{1,0:T(8,128)(2,1)S(1)} %get-tuple-element.18), channel_id=1, source_target_pairs={{0,2},{2,0},{4,6},{6,4},{8,10},{10,8},{12,14},{14,12},{16,18},{18,... | collective-permute-start | bytes 393224 | tf_op jit(solution)/shard_map/ppermute | solution.py:248
  9.8 13.9 %collective-permute-start = (bf16[256,512]{1,0:T(8,128)(2,1)S(1)}, bf16[256,512]{1,0:T(8,128)(2,1)S(1)}, u32[]{:S(2)}, u32[]{:S(2)}) collective-permute-start(bf16[256,512]{1,0:T(8,128)(2,1)S(1)} %get-tuple-element.13), channel_id=1, source_target_pairs={{0,2},{2,0},{4,6},{6,4},{8,10},{10,8},{12,14},{14,12},{16,18},{18,... | collective-permute-start | bytes 786440 | tf_op jit(solution)/shard_map/ppermute | solution.py:248
  10.9 12.9 %collective-permute-start.2 = (bf16[2,256,512]{2,1,0:T(8,128)(2,1)S(1)}, bf16[2,256,512]{2,1,0:T(8,128)(2,1)S(1)}, u32[]{:S(2)}, u32[]{:S(2)}) collective-permute-start(bf16[2,256,512]{2,1,0:T(8,128)(2,1)S(1)} %pad_maximum_fusion.near), channel_id=1, source_target_pairs={{2,10},{6,14},{8,0},{10,18},{12,4},{14,22},{16,8},{18,26},{20,12},... | collective-permute-start | bytes 1572872 | tf_op jit(solution)/shard_map/ppermute | solution.py:259
  14.6 14.0 %collective-permute-start.8 = (bf16[2,256,512]{2,1,0:T(8,128)(2,1)S(1)}, bf16[2,256,512]{2,1,0:T(8,128)(2,1)S(1)}, u32[]{:S(2)}, u32[]{:S(2)}) collective-permute-start(bf16[2,256,512]{2,1,0:T(8,128)(2,1)S(1)} %pad_maximum_fusion.1), channel_id=1, source_target_pairs={{0,4},{2,6},{4,0},{6,2},{8,12},{10,14},{12,8},{14,10},{16,20},{18,... | collective-permute-start | bytes 1572872 | tf_op jit(solution)/shard_map/ppermute | solution.py:248
  15.8 13.5 %collective-permute-start.10 = (bf16[256,512]{1,0:T(8,128)(2,1)S(1)}, bf16[256,512]{1,0:T(8,128)(2,1)S(1)}, u32[]{:S(2)}, u32[]{:S(2)}) collective-permute-start(bf16[256,512]{1,0:T(8,128)(2,1)S(1)} %get-tuple-element.19), channel_id=1, source_target_pairs={{0,10},{4,14},{8,18},{10,0},{12,22},{14,4},{16,26},{18,8},{20,30},... | collective-permute-start | bytes 786440 | tf_op jit(solution)/shard_map/ppermute | solution.py:259
  16.5 12.8 %collective-permute-start.9 = (bf16[256,512]{1,0:T(8,128)(2,1)S(1)}, bf16[256,512]{1,0:T(8,128)(2,1)S(1)}, u32[]{:S(2)}, u32[]{:S(2)}) collective-permute-start(bf16[256,512]{1,0:T(8,128)(2,1)S(1)} %get-tuple-element.20), channel_id=1, source_target_pairs={{2,10},{6,14},{8,0},{10,18},{12,4},{14,22},{16,8},{18,26},{20,12},... | collective-permute-start | bytes 786440 | tf_op jit(solution)/shard_map/ppermute | solution.py:259
  23.7 4.9 %collective-permute-start.4 = (bf16[128,512]{1,0:T(8,128)(2,1)S(1)}, bf16[128,512]{1,0:T(8,128)(2,1)S(1)}, u32[]{:S(2)}, u32[]{:S(2)}) collective-permute-start(bf16[128,512]{1,0:T(8,128)(2,1)S(1)} %get-tuple-element.22), channel_id=1, source_target_pairs={{0,2},{2,0},{4,6},{6,4},{8,10},{10,8},{12,14},{14,12},{16,18},{18,... | collective-permute-start | bytes 393224 | tf_op jit(solution)/shard_map/ppermute | solution.py:248
  23.8 4.8 %collective-permute-start.5 = (bf16[128,512]{1,0:T(8,128)(2,1)S(1)}, bf16[128,512]{1,0:T(8,128)(2,1)S(1)}, u32[]{:S(2)}, u32[]{:S(2)}) collective-permute-start(bf16[128,512]{1,0:T(8,128)(2,1)S(1)} %get-tuple-element.21), channel_id=1, source_target_pairs={{0,2},{2,0},{4,6},{6,4},{8,10},{10,8},{12,14},{14,12},{16,18},{18,... | collective-permute-start | bytes 393224 | tf_op jit(solution)/shard_map/ppermute | solution.py:248
  55.7 4.6 %collective-permute-start.11 = (f32[2,8,128]{2,1,0:T(8,128)S(1)}, f32[2,8,128]{2,1,0:T(8,128)S(1)}, u32[]{:S(2)}, u32[]{:S(2)}) collective-permute-start(f32[2,8,128]{2,1,0:T(8,128)S(1)} %reduce_sum.9), channel_id=1, source_target_pairs={{0,2},{2,0},{4,6},{6,4},{8,10},{10,8},{12,14},{14,12},{16,18},{18,... | collective-permute-start | bytes 24584 | tf_op jit(solution)/shard_map/ppermute | solution.py:248
